TPU v7x, 32 devices: a whole 2x2x4 slice. The times are simulated.
32 devices in a mesh: sub: 16 (over z, y, core), row: 2 (over x).
Axes of the slice: x: 2, y: 2, z: 4, core: 2. Of those that a mesh axis runs over, the one named last changes fastest.
Arguments:
- compliance: bfloat16 [16, 36, 18, 128, 128], P('sub', 'row'), may hold values from -0.0625 to 0.0625
- block_columns: int32 [16, 36, 18], P('sub', 'row'), may hold values from 0 to 35, as said below
- load_response: bfloat16 [16, 32, 4608], P('sub', None, 'row'), may hold values from -6 to 6
- starting_motion: bfloat16 [16, 32, 4608], P('sub', None, 'row'), may hold values from -6 to 6
- start_traction: bfloat16 [16, 32, 4608], P('sub', None, 'row'), may hold values from -6 to 6
- stiffness: float32 [16, 4608], P('sub', 'row'), may hold values from 1 to 10
- history: float32 [16, 4608], P('sub', 'row'), may hold values from 0 to 0.6
- face_partner: int32 [16, 36], P('sub', 'row'), may hold values from -1 to 8, as said below
- orientation: int32 [16, 36, 128], P('sub', 'row'), may hold values from 0 to 127, as said below
Outputs:
- displacement: bfloat16 [16, 32, 4608], P('sub', None, 'row')
- traction: bfloat16 [16, 32, 4608], P('sub', None, 'row')
Inputs may be any that keep to these rules, and one draw needn't show every extreme that they name: `block_columns`: each block row names 18 distinct face columns. `face_partner`: an entry is -1 for a free face, else the position, within the facing group of the same run of the neighbouring substructure, of the matched face. Matches are mutual. Faces facing s+1 on the last substructure and faces facing s-1 on the first are free. In some run of some substructure all 9 faces facing s+1 are matched. `orientation`: each face's row is a permutation of 0 to 127; matched faces carry mutually inverse permutations.
All inputs are finite; a program needn't handle non-finite values.
Results may differ from a plain program's by a relative error of at most 0.0045.
The roundings to bfloat16 on the way count: a program that leaves them out, or rounds other values in their place, can miss the bound.
Values may be sent and summed in bfloat16 or wider, within the bound.
No kernel may reach another device: no remote copies, remote signals or barrier semaphores. Data moves between devices by JAX's collectives and lax.ppermute only.
A program may use at most 64 MiB of HBM per device.

v0:
```python
import functools

import jax
import jax.numpy as jnp
from jax import lax
from jax.experimental import pallas as pl
from jax.experimental.pallas import tpu as pltpu
from jax.sharding import PartitionSpec as P

ITERS = 3
SUBLANES = 8
LEAST = 2.0**-100
EARLY = (6, 10)
VMEM_BYTES = 24 * 2**20

ONSET_JUMP = 0.15
FAILURE_JUMP = 1.5

VMEM = pl.BlockSpec(memory_space=pltpu.VMEM)
SMEM = pl.BlockSpec(memory_space=pltpu.SMEM)
ANY = pl.BlockSpec(memory_space=pl.ANY)
HBM = pl.BlockSpec(memory_space=pltpu.HBM)


def position(group):
    near = group * (lax.axis_index("sub") % 2)
    return near, group - near, lax.axis_index("row")


def lanes_of(face, extent):
    return pl.ds(pl.multiple_of(face * extent, extent), extent)


def sort_blocks(columns_ref, order_ref, sorted_ref, ready_ref):
    faces, _, stored = columns_ref.shape
    group = faces // 2
    near, far, mine = position(group)
    own = mine * faces
    partner = (1 - mine) * faces + near

    def sort_row(face, _):
        in_far = (face >= far) & (face < far + group)
        width = jnp.where(in_far, group, 0)
        front, back = jnp.int32(0), jnp.int32(stored - 1)
        for j in range(stored):
            column = columns_ref[face, 0, j]
            early = ((column >= own) & (column < own + faces)) | ((column >= partner) & (column < partner + width))
            place = jnp.where(early, front, back)
            order_ref[face, 0, place] = j
            sorted_ref[face, 0, place] = column
            front = jnp.where(early, front + 1, front)
            back = jnp.where(early, back, back - 1)
        ready_ref[0, face] = front
        return 0

    lax.fori_loop(0, faces, sort_row, 0)


def fetch(blocks_hbm, load_hbm, motion_hbm, stress_hbm, stiff_hbm, record_hbm, turn_hbm, columns_hbm, partner_hbm,
          blocks_ref, load_ref, motion_ref, stress_ref, stiff_ref, record_ref, turn_ref, partner_ref,
          order_ref, sorted_ref, ready_ref, columns_ref, sems):
    pairs = [
        (columns_hbm, columns_ref), (load_hbm, load_ref), (motion_hbm, motion_ref), (stress_hbm, stress_ref),
        (stiff_hbm, stiff_ref), (record_hbm, record_ref), (turn_hbm, turn_ref), (partner_hbm, partner_ref),
    ]
    pairs += [(blocks_hbm.at[face], blocks_ref.at[face]) for face in range(blocks_hbm.shape[0])]
    copies = [pltpu.make_async_copy(source, target, sems.at[n]) for n, (source, target) in enumerate(pairs)]
    for copy in copies:
        copy.start()
    copies[0].wait()
    sort_blocks(columns_ref, order_ref, sorted_ref, ready_ref)
    for copy in copies[1:]:
        copy.wait()


def block_products(parts):
    times, extent = parts[0][0][0].shape
    zero = jnp.zeros_like(parts[0][0][1])
    depth = max(len(part) for part in parts)
    parts = [part + [(part[0][0], zero)] * (depth - len(part)) for part in parts]
    values = jnp.concatenate([jnp.concatenate([v for v, _ in part], axis=1) for part in parts], axis=0)
    blocks = jnp.concatenate([jnp.concatenate([c for _, c in part], axis=1) for part in parts], axis=0)
    product = lax.dot_general(values, blocks, (((1,), (1,)), ((), ())), preferred_element_type=jnp.float32)
    return [
        product[p * times : (p + 1) * times, p * extent : (p + 1) * extent] for p in range(len(parts))
    ]


def group_products(first, group, entries, finish):
    for index in range(0, group - 1, 2):
        pair = block_products([entries(first + index + k) for k in range(2)])
        for k in range(2):
            finish(index + k, pair[k])
    if group % 2:
        whole = entries(first + group - 1)
        cut = (len(whole) + 3) // 4 * 2
        finish(group - 1, sum(block_products([whole[:cut], whole[cut:]])))


def early_products(side, order_ref, sorted_ref, ready_ref, compliance_ref, own0_ref, own1_ref, *refs):
    out_ref, half_ref = refs[-2:]
    group, times, _ = out_ref.shape
    faces = compliance_ref.shape[0]
    *starts, mine = position(group)
    none = half_ref.shape[0] - 1
    half_ref[none] = jnp.zeros_like(half_ref[none])
    for start, ref in zip(starts, (own0_ref, own1_ref)):
        half_ref[pl.ds(mine * faces + start, group)] = ref[...]
    for ref in refs[:side]:
        half_ref[pl.ds((1 - mine) * faces + starts[0], group)] = ref[...]

    def entries(face):
        ready = ready_ref[0, face]
        return [
            (half_ref[jnp.where(slot < ready, sorted_ref[face, 0, slot], none)], compliance_ref[face, order_ref[face, 0, slot]])
            for slot in range(EARLY[side])
        ]

    def finish(index, product):
        out_ref[index] = product

    group_products(starts[side], group, entries, finish)


def sorted_entry(half_ref, order_ref, sorted_ref, compliance_ref, face, slot):
    return half_ref[sorted_ref[face, 0, slot]], compliance_ref[face, order_ref[face, 0, slot]]


def first_section(side, order_ref, sorted_ref, compliance_ref, own_ref, other_ref, motion_ref, stress_ref, load_ref,
                  stiff_ref, record_ref, out_ref, half_ref):
    times = motion_ref.shape[0]
    faces, stored, extent, _ = compliance_ref.shape
    group = faces // 2
    *starts, mine = position(group)
    first = starts[side]
    for run, ref in ((mine, own_ref), (1 - mine, other_ref)):
        for face in range(faces):
            half_ref[run * faces + face] = ref[:, face * extent : (face + 1) * extent]
    entry = functools.partial(sorted_entry, half_ref, order_ref, sorted_ref, compliance_ref)

    def finish(index, product):
        lanes = lanes_of(first + index, extent)
        robin = stress_ref[:, lanes].astype(jnp.float32) + motion_ref[:, lanes].astype(jnp.float32)
        response = product + load_ref[:, lanes].astype(jnp.float32)
        out_ref[index] = robin - 2.0 * response
        out_ref[group, index : index + 1] = stiff_ref[:, lanes]
        out_ref[group, group + index : group + index + 1] = record_ref[:, lanes]

    for plane in range(group, out_ref.shape[0]):
        out_ref[plane] = jnp.zeros_like(out_ref[plane])
    group_products(first, group, lambda face: [entry(face, slot) for slot in range(stored)], finish)


def linear_section(side, order_ref, sorted_ref, ready_ref, compliance_ref, own0_ref, own1_ref, other0_ref, other1_ref,
                   robin_ref, load_ref, early_ref, out_ref, sent_ref, half_ref):
    group, times, extent = own0_ref.shape
    faces, stored = compliance_ref.shape[:2]
    *starts, mine = position(group)
    first, done = starts[side], EARLY[side]
    for run, parts in ((mine, (own0_ref, own1_ref)), (1 - mine, (other0_ref, other1_ref))):
        for start, ref in zip(starts, parts):
            half_ref[pl.ds(run * faces + start, group)] = ref[...]
    entry = functools.partial(sorted_entry, half_ref, order_ref, sorted_ref, compliance_ref)

    def finish(index, product):
        response = early_ref[index] + product + load_ref[:, lanes_of(first + index, extent)].astype(jnp.float32)
        out_ref[index] = robin_ref[index] - 2.0 * response

    group_products(first, group, lambda face: [entry(face, slot) for slot in range(done, stored)], finish)

    def missed(slot, index):
        out_ref[index] -= 2.0 * block_products([[entry(first + index, slot)]])[0]
        return index

    least = ready_ref[0, first]
    for index in range(1, group):
        least = jnp.minimum(least, ready_ref[0, first + index])

    @pl.when(least < done)
    def _():
        for index in range(group):
            lax.fori_loop(ready_ref[0, first + index], done, missed, index)

    encode(out_ref, sent_ref)


def encode(values_ref, sent_ref):
    group, times, extent = values_ref.shape
    lane = lax.broadcasted_iota(jnp.int32, (times, extent), 1)
    exponents = jnp.zeros((times, extent), jnp.float32)
    for index in range(group):
        values = values_ref[index]
        largest = jnp.max(jnp.abs(values), axis=1, keepdims=True)
        exponent = jnp.floor(jnp.log2(jnp.maximum(largest, LEAST))) - 14.0
        steps = jnp.clip(jnp.round(values * jnp.exp2(-exponent)), -32767.0, 32767.0)
        sent_ref[index] = steps.astype(jnp.int32).astype(jnp.int16)
        exponents = jnp.where(lane == index, exponent, exponents)
    sent_ref[group] = exponents.astype(jnp.int32).astype(jnp.int16)
    for plane in range(group + 1, sent_ref.shape[0]):
        sent_ref[plane] = jnp.zeros_like(sent_ref[plane])


def decoder(sent_ref, group):
    exponents = sent_ref[group].astype(jnp.int32).astype(jnp.float32)
    lane = lax.broadcasted_iota(jnp.int32, exponents.shape, 1)

    def face_of(index):
        exponent = jnp.sum(jnp.where(lane == index, exponents, 0.0), axis=1, keepdims=True)
        return sent_ref[index].astype(jnp.int32).astype(jnp.float32) * jnp.exp2(exponent)

    return face_of


def running_peak(sizes):
    row = lax.broadcasted_iota(jnp.int32, sizes.shape, 0)
    step = 1
    while step < sizes.shape[0]:
        earlier = pltpu.roll(sizes, step, 0)
        sizes = jnp.maximum(sizes, jnp.where(row >= step, earlier, 0.0))
        step *= 2
    return sizes


def turned(values, turn):
    return jnp.take_along_axis(values, jnp.broadcast_to(turn, values.shape), axis=1, mode="promise_in_bounds")


def local_face(ascent, mate_ascent, stiffness, record, live):
    difference = ascent - mate_ascent
    jump = difference / (1.0 + 2.0 * stiffness)
    peak = jnp.maximum(record, running_peak(jnp.abs(jump)))
    damage = jnp.clip((peak - ONSET_JUMP) / (FAILURE_JUMP - ONSET_JUMP), 0.0, 1.0)
    effective = stiffness * (1.0 - damage)
    traction = jnp.where(live, effective * difference / (1.0 + 2.0 * effective), 0.0)
    return traction, traction - ascent


def local_first(side, partner_ref, turn_ref, own_ref, mate_ref, stiff_ref, record_ref,
                robin_ref, half_ref, pair_stiff_ref, pair_record_ref):
    group, _, extent = robin_ref.shape
    first = position(group)[side]
    for index in range(group):
        face = first + index
        lanes, here = lanes_of(face, extent), lanes_of(index, extent)
        partner = partner_ref[0, face]
        mate = jnp.maximum(partner, 0)
        turn = turn_ref[:, lanes]

        def constant(row):
            return turned(jnp.broadcast_to(mate_ref[group, pl.ds(row, 1), :], (SUBLANES, extent)), turn)[:1]

        stiffness = 0.5 * (stiff_ref[:, lanes] + constant(mate))
        record = jnp.maximum(record_ref[:, lanes], constant(group + mate))
        pair_stiff_ref[:, here] = stiffness
        pair_record_ref[:, here] = record
        traction, motion = local_face(own_ref[index], turned(mate_ref[mate], turn), stiffness, record, partner >= 0)
        robin = traction + motion
        robin_ref[index] = robin
        half_ref[index] = robin.astype(jnp.bfloat16)


def local_faces(side, partner_ref, turn_ref, own_ref, mate_ref, stiff_ref, record_ref):
    group, _, extent = own_ref.shape
    first = position(group)[side]
    mate_face = decoder(mate_ref, group)
    for index in range(group):
        face = first + index
        here = lanes_of(index, extent)
        partner = partner_ref[0, face]
        mate_ascent = turned(mate_face(jnp.maximum(partner, 0)), turn_ref[:, lanes_of(face, extent)])
        yield index, *local_face(own_ref[index], mate_ascent, stiff_ref[:, here], record_ref[:, here], partner >= 0)


def local_group(side, *refs):
    *ins, robin_ref, half_ref = refs
    for index, traction, motion in local_faces(side, *ins):
        robin = traction + motion
        robin_ref[index] = robin
        half_ref[index] = robin.astype(jnp.bfloat16)


def local_last(side, *refs):
    ins, (motion_hbm, traction_hbm, motion_ref, traction_ref, sems) = refs[:6], refs[-5:]
    group, _, extent = ins[2].shape
    for index, traction, motion in local_faces(side, *ins):
        here = lanes_of(index, extent)
        motion_ref[:, here] = motion.astype(jnp.bfloat16)
        traction_ref[:, here] = traction.astype(jnp.bfloat16)
    lanes = pl.ds(pl.multiple_of(position(group)[side] * extent, extent), group * extent)
    copies = [
        pltpu.make_async_copy(motion_ref, motion_hbm.at[:, lanes], sems.at[0]),
        pltpu.make_async_copy(traction_ref, traction_hbm.at[:, lanes], sems.at[1]),
    ]
    for copy in copies:
        copy.start()
    for copy in copies:
        copy.wait()


def shards(
    compliance,
    block_columns,
    load_response,
    starting_motion,
    start_traction,
    stiffness,
    history,
    face_partner,
    orientation,
):
    _, faces, stored, extent, _ = compliance.shape
    times = starting_motion.shape[1]
    group = faces // 2
    subs = lax.axis_size("sub")
    rows = lax.axis_size("row")
    near_pairs = [(s, s ^ 1) for s in range(subs)]
    far_pairs = []
    for s in range(subs):
        mate = s - 1 if s % 2 == 0 else s + 1
        for r in range(rows):
            there = mate * rows + r if 0 <= mate < subs else s * rows + rows - 1 - r
            far_pairs.append((s * rows + r, there))
    swap = [(r, rows - 1 - r) for r in range(rows)]

    def f32(*shape):
        return jax.ShapeDtypeStruct(shape, jnp.float32)

    def bf16(*shape):
        return jax.ShapeDtypeStruct(shape, jnp.bfloat16)

    def s32(*shape):
        return jax.ShapeDtypeStruct(shape, jnp.int32)

    def call(kernel, in_specs, out_shape, scratch=(), moved=0, out_specs=(), aliases={}):
        outs = out_shape if isinstance(out_shape, tuple) else (out_shape,)
        out_specs = out_specs or (VMEM,) * len(outs)
        return pl.pallas_call(
            kernel,
            out_shape=out_shape,
            in_specs=in_specs,
            out_specs=out_specs if isinstance(out_shape, tuple) else out_specs[0],
            scratch_shapes=scratch,
            input_output_aliases=aliases,
            compiler_params=pltpu.CompilerParams(vmem_limit_bytes=VMEM_BYTES),
            cost_estimate=pl.CostEstimate(flops=moved, bytes_accessed=moved, transcendentals=0) if moved else None,
        )

    part = (group, times, extent)
    flat = (times, faces * extent)
    block_bytes = faces * stored * extent * extent * 2
    halves = pltpu.VMEM((rows * faces, times, extent), jnp.bfloat16)
    in_hbm = functools.partial(pltpu.with_memory_space_constraint, memory_space=pltpu.HBM)
    own = (start_traction[0].astype(jnp.float32) + starting_motion[0].astype(jnp.float32)).astype(jnp.bfloat16)
    other = lax.ppermute(own, "row", swap)
    blocks, load, motion, stress, stiff, record, turn, partner, *tables = call(
        fetch, [HBM] * 9,
        (pltpu.VMEM((faces, stored, extent, extent), jnp.bfloat16), bf16(*flat), bf16(*flat), bf16(*flat),
         f32(1, faces * extent), f32(1, faces * extent), s32(1, faces * extent), pltpu.SMEM((1, faces), jnp.int32),
         pltpu.SMEM((faces, 1, stored), jnp.int32), pltpu.SMEM((faces, 1, stored), jnp.int32), pltpu.SMEM((1, faces), jnp.int32)),
        [pltpu.SMEM((faces, 1, stored), jnp.int32), pltpu.SemaphoreType.DMA((8 + faces,))],
        block_bytes, (VMEM,) * 7 + (SMEM,) * 4,
    )(
        in_hbm(compliance[0]), in_hbm(load_response[0]), in_hbm(starting_motion[0]), in_hbm(start_traction[0]),
        in_hbm(stiffness), in_hbm(history), in_hbm(orientation.reshape(1, -1)),
        in_hbm(jnp.transpose(block_columns, (1, 0, 2))), in_hbm(face_partner),
    )
    in_smem = functools.partial(pltpu.with_memory_space_constraint, memory_space=pltpu.SMEM)
    partner, tables = in_smem(partner), [in_smem(table) for table in tables]

    robin, half = [None, None], [None, None]
    stiffs, records = [stiff, stiff], [record, record]
    for iteration in range(ITERS):
        begin, last = iteration == 0, iteration == ITERS - 1
        if not begin:
            other = [lax.ppermute(half[side], "row", swap) for side in range(2)]
        ascent, mates, early = [None, None], [None, None], []
        for side in range(0 if begin else 2):
            early.append(call(
                functools.partial(early_products, side), [SMEM] * 3 + [VMEM] * (3 + side) + [ANY] * side, f32(*part),
                [pltpu.VMEM((rows * faces + 1, times, extent), jnp.bfloat16)], block_bytes,
            )(*tables, blocks, *half, *other[:side], *early))
        for side, (axes, pairs) in enumerate((("sub", near_pairs), (("sub", "row"), far_pairs))):
            if begin:
                ascent[side] = sent = call(
                    functools.partial(first_section, side), [SMEM] * 2 + [VMEM] * 8,
                    f32(group + 1 + side, times, extent), [halves], 2 * block_bytes,
                )(*tables[:2], blocks, own, other, motion, stress, load, stiff, record)
            else:
                ascent[side], sent = call(
                    functools.partial(linear_section, side), [SMEM] * 3 + [VMEM] * 8,
                    (f32(*part), jax.ShapeDtypeStruct((group + 1 + side, times, extent), jnp.int16)),
                    [halves], 2 * block_bytes,
                )(*tables, blocks, *half, *other, robin[side], load, early[side])
            mates[side] = lax.ppermute(sent, axes, pairs)
        outs = ()
        for side in range(2):
            ins = (partner, turn, ascent[side], mates[side], stiffs[side], records[side])
            specs = [SMEM] + [VMEM] * 5
            if begin:
                robin[side], half[side], stiffs[side], records[side] = call(
                    functools.partial(local_first, side), specs,
                    (f32(*part), bf16(*part), f32(1, group * extent), f32(1, group * extent)),
                )(*ins)
            elif not last:
                robin[side], half[side] = call(functools.partial(local_group, side), specs, (f32(*part), bf16(*part)))(*ins)
            else:
                share = pltpu.VMEM((times, group * extent), jnp.bfloat16)
                outs = call(
                    functools.partial(local_last, side), specs + [HBM] * len(outs), (bf16(*flat),) * 2,
                    [share, share, pltpu.SemaphoreType.DMA((2,))], 0, (HBM,) * 2, {6 + n: n for n in range(len(outs))},
                )(*ins, *outs)
    return tuple(out[None] for out in outs)


def solution(mesh):
    in_specs = (
        P("sub", "row", None, None, None),
        P("sub", "row", None),
        P("sub", None, "row"),
        P("sub", None, "row"),
        P("sub", None, "row"),
        P("sub", "row"),
        P("sub", "row"),
        P("sub", "row"),
        P("sub", "row", None),
    )
    out_specs = (P("sub", None, "row"), P("sub", None, "row"))
    return jax.shard_map(shards, mesh=mesh, in_specs=in_specs, out_specs=out_specs, check_vma=False)
```

profile of v0, /device:TPU:0, one launch (start us, length us, event | category | flops | bytes accessed | tf_op | source)
XLA Modules:
  0.0 41.9 jit_solution(13498587093817439813)
XLA Ops:
  0.6 1.0 %add_convert_fusion.own_ref = bf16[32,2304]{1,0:T(8,128)(2,1)S(1)} fusion(bf16[1,32,2304]{2,1,0:T(8,128)(2,1)} %param.13, bf16[1,32,2304]{2,1,0:T(8,128)(2,1)} %param.12), kind=kLoop, calls=%fused_computation | loop fusion | flops 294912 | bytes 442368 | tf_op jit(solution)/shard_map/convert_element_type | solution.py:353
  1.7 3.0 %collective-permute-start = (bf16[32,2304]{1,0:T(8,128)(2,1)S(1)}, bf16[32,2304]{1,0:T(8,128)(2,1)S(1)}, u32[]{:S(2)}, u32[]{:S(2)}) collective-permute-start(bf16[32,2304]{1,0:T(8,128)(2,1)S(1)} %add_convert_fusion.own_ref), channel_id=1, source_target_pairs={{0,1},{1,0},{2,3},{3,2},{4,5},{5,4},{6,7},{7,6},{8,9},{9,8},{10,11... | collective-permute-start | bytes 442376 | tf_op jit(solution)/shard_map/ppermute | solution.py:354
  4.7 4.5 %shard_map.104 = (bf16[18,18,128,128]{3,2,1,0:T(8,128)(2,1)S(1)}, bf16[32,2304]{1,0:T(8,128)(2,1)S(1)}, bf16[32,2304]{1,0:T(8,128)(2,1)S(1)}, bf16[32,2304]{1,0:...) custom-call(bf16[18,18,128,128]{3,2,1,0:T(8,128)(2,1)} %bitcast.10, ...), custom_call_target="tpu_custom_call" | custom-call | flops 10616832 | bytes 10616832 | tf_op jit(solution)/shard_map/pallas_call | solution.py:355
  9.2 1.8 %shard_map.107.own_ref = f32[11,32,128]{2,1,0:T(8,128)S(1)} custom-call(s32[18,1,18]{2,1,0:T(1,128)S(4)} %get-tuple-element.39.order_ref, s32[18,1,18]{2,1,0:T(1,128)S(4)} %get-tuple-element.40.sorted_ref, bf16[18,18,128,128]{3,2,1,0:T(8,128)(2,1)S(1)} %get-tuple-element.42.compliance_ref, bf16[32,2304]{1,0:T(8,128)(2,1)S(1)} %add_convert_fusion.own_ref, ...), custom_call_target="tpu_custom_call" | custom-call | flops 21233664 | bytes 21233664 | tf_op jit(solution)/shard_map/pallas_call | solution.py:384
  11.0 1.1 %collective-permute-start.2 = (f32[11,32,128]{2,1,0:T(8,128)S(1)}, f32[11,32,128]{2,1,0:T(8,128)S(1)}, u32[]{:S(2)}, u32[]{:S(2)}) collective-permute-start(f32[11,32,128]{2,1,0:T(8,128)S(1)} %shard_map.107.own_ref), channel_id=1, source_target_pairs={{0,1},{1,0},{2,4},{3,5},{4,2},{5,3},{6,8},{7,9},{8,6},{9,7},{10,12... | collective-permute-start | bytes 540680 | tf_op jit(solution)/shard_map/ppermute | solution.py:394
  12.1 1.7 %shard_map.105.own_ref = f32[10,32,128]{2,1,0:T(8,128)S(1)} custom-call(s32[18,1,18]{2,1,0:T(1,128)S(4)} %get-tuple-element.39.order_ref, s32[18,1,18]{2,1,0:T(1,128)S(4)} %get-tuple-element.40.sorted_ref, bf16[18,18,128,128]{3,2,1,0:T(8,128)(2,1)S(1)} %get-tuple-element.42.compliance_ref, bf16[32,2304]{1,0:T(8,128)(2,1)S(1)} %add_convert_fusion.own_ref, ...), custom_call_target="tpu_custom_call" | custom-call | flops 21233664 | bytes 21233664 | tf_op jit(solution)/shard_map/pallas_call | solution.py:384
  13.8 0.6 %collective-permute-start.1 = (f32[10,32,128]{2,1,0:T(8,128)S(1)}, f32[10,32,128]{2,1,0:T(8,128)S(1)}, u32[]{:S(2)}, u32[]{:S(2)}) collective-permute-start(f32[10,32,128]{2,1,0:T(8,128)S(1)} %shard_map.105.own_ref), channel_id=1, source_target_pairs={{0,2},{2,0},{4,6},{6,4},{8,10},{10,8},{12,14},{14,12},{16,18},{18,... | collective-permute-start | bytes 491528 | tf_op jit(solution)/shard_map/ppermute | solution.py:394
  14.5 1.0 %collective-permute-done.1.mate_ref = f32[10,32,128]{2,1,0:T(8,128)S(1)} collective-permute-done((f32[10,32,128]{2,1,0:T(8,128)S(1)}, f32[10,32,128]{2,1,0:T(8,128)S(1)}, u32[]{:S(2)}, u32[]{:S(2)}) %collective-permute-start.1) | collective-permute-done | bytes 163872 | tf_op jit(solution)/shard_map/ppermute | solution.py:394
  15.8 1.1 %collective-permute-start.3 = (bf16[9,32,128]{2,1,0:T(8,128)(2,1)S(1)}, bf16[9,32,128]{2,1,0:T(8,128)(2,1)S(1)}, u32[]{:S(2)}, u32[]{:S(2)}) collective-permute-start(bf16[9,32,128]{2,1,0:T(8,128)(2,1)S(1)} %get-tuple-element.48.own0_ref), channel_id=1, source_target_pairs={{0,1},{1,0},{2,3},{3,2},{4,5},{5,4},{6,7},{7,6},{8,9},{9,8},{10,11... | collective-permute-start | bytes 221192 | tf_op jit(solution)/shard_map/ppermute | solution.py:375
  17.2 1.0 %collective-permute-start.4 = (bf16[9,32,128]{2,1,0:T(8,128)(2,1)S(1)}, bf16[9,32,128]{2,1,0:T(8,128)(2,1)S(1)}, u32[]{:S(2)}, u32[]{:S(2)}) collective-permute-start(bf16[9,32,128]{2,1,0:T(8,128)(2,1)S(1)} %get-tuple-element.49.own1_ref), channel_id=1, source_target_pairs={{0,1},{1,0},{2,3},{3,2},{4,5},{5,4},{6,7},{7,6},{8,9},{9,8},{10,11... | collective-permute-start | bytes 221192 | tf_op jit(solution)/shard_map/ppermute | solution.py:375
  18.2 0.7 %shard_map.109.early_ref.refs_1_ = f32[9,32,128]{2,1,0:T(8,128)S(1)} custom-call(s32[18,1,18]{2,1,0:T(1,128)S(4)} %get-tuple-element.39.order_ref, s32[18,1,18]{2,1,0:T(1,128)S(4)} %get-tuple-element.40.sorted_ref, s32[1,18]{1,0:T(1,128)S(4)} %get-tuple-element.41.ready_ref, bf16[18,18,128,128]{3,2,1,0:T(8,128)(2,1)S(1)} %get-tuple-element.42.compliance_ref, ...), custom_call_target="tpu_custom_call" | custom-call | flops 10616832 | bytes 10616832 | tf_op jit(solution)/shard_map/pallas_call | solution.py:378
  18.9 2.0 %collective-permute-done.3.other0_ref.refs_0_ = bf16[9,32,128]{2,1,0:T(8,128)(2,1)S(1)} collective-permute-done((bf16[9,32,128]{2,1,0:T(8,128)(2,1)S(1)}, bf16[9,32,128]{2,1,0:T(8,128)(2,1)S(1)}, u32[]{:S(2)}, u32[]{:S(2)}) %collective-permute-start.3) | collective-permute-done | bytes 73760 | tf_op jit(solution)/shard_map/ppermute | solution.py:375
  20.9 1.0 %shard_map.112.early_ref = f32[9,32,128]{2,1,0:T(8,128)S(1)} custom-call(s32[18,1,18]{2,1,0:T(1,128)S(4)} %get-tuple-element.39.order_ref, s32[18,1,18]{2,1,0:T(1,128)S(4)} %get-tuple-element.40.sorted_ref, s32[1,18]{1,0:T(1,128)S(4)} %get-tuple-element.41.ready_ref, bf16[18,18,128,128]{3,2,1,0:T(8,128)(2,1)S(1)} %get-tuple-element.42.compliance_ref, ...), custom_call_target="tpu_custom_call" | custom-call | flops 10616832 | bytes 10616832 | tf_op jit(solution)/shard_map/pallas_call | solution.py:378
  22.0 1.0 %shard_map.113 = (f32[9,32,128]{2,1,0:T(8,128)S(1)}, s16[11,32,128]{2,1,0:T(8,128)(2,1)S(1)}) custom-call(s32[18,1,18]{2,1,0:T(1,128)S(4)} %get-tuple-element.39.order_ref, s32[18,1,18]{2,1,0:T(1,128)S(4)} %get-tuple-element.40.sorted_ref, s32[1,18]{1,0:T(1,128)S(4)} %get-tuple-element.41.ready_ref, ...), custom_call_target="tpu_custom_call" | custom-call | flops 21233664 | bytes 21233664 | tf_op jit(solution)/shard_map/pallas_call | solution.py:389
  23.0 1.1 %collective-permute-start.6 = (s16[11,32,128]{2,1,0:T(8,128)(2,1)S(1)}, s16[11,32,128]{2,1,0:T(8,128)(2,1)S(1)}, u32[]{:S(2)}, u32[]{:S(2)}) collective-permute-start(s16[11,32,128]{2,1,0:T(8,128)(2,1)S(1)} %get-tuple-element.58), channel_id=1, source_target_pairs={{0,1},{1,0},{2,4},{3,5},{4,2},{5,3},{6,8},{7,9},{8,6},{9,7},{10,12... | collective-permute-start | bytes 270344 | tf_op jit(solution)/shard_map/ppermute | solution.py:394
  24.1 1.4 %shard_map.110 = (f32[9,32,128]{2,1,0:T(8,128)S(1)}, s16[10,32,128]{2,1,0:T(8,128)(2,1)S(1)}) custom-call(s32[18,1,18]{2,1,0:T(1,128)S(4)} %get-tuple-element.39.order_ref, s32[18,1,18]{2,1,0:T(1,128)S(4)} %get-tuple-element.40.sorted_ref, s32[1,18]{1,0:T(1,128)S(4)} %get-tuple-element.41.ready_ref, ...), custom_call_target="tpu_custom_call" | custom-call | flops 21233664 | bytes 21233664 | tf_op jit(solution)/shard_map/pallas_call | solution.py:389
  25.5 1.3 %collective-permute-start.5 = (s16[10,32,128]{2,1,0:T(8,128)(2,1)S(1)}, s16[10,32,128]{2,1,0:T(8,128)(2,1)S(1)}, u32[]{:S(2)}, u32[]{:S(2)}) collective-permute-start(s16[10,32,128]{2,1,0:T(8,128)(2,1)S(1)} %get-tuple-element.52), channel_id=1, source_target_pairs={{0,2},{2,0},{4,6},{6,4},{8,10},{10,8},{12,14},{14,12},{16,18},{18,... | collective-permute-start | bytes 245768 | tf_op jit(solution)/shard_map/ppermute | solution.py:394
  26.7 0.9 %collective-permute-done.5.refs_3_ = s16[10,32,128]{2,1,0:T(8,128)(2,1)S(1)} collective-permute-done((s16[10,32,128]{2,1,0:T(8,128)(2,1)S(1)}, s16[10,32,128]{2,1,0:T(8,128)(2,1)S(1)}, u32[]{:S(2)}, u32[]{:S(2)}) %collective-permute-start.5) | collective-permute-done | bytes 81952 | tf_op jit(solution)/shard_map/ppermute | solution.py:394
  27.6 0.6 %shard_map.111 = (f32[9,32,128]{2,1,0:T(8,128)S(1)}, bf16[9,32,128]{2,1,0:T(8,128)(2,1)S(1)}) custom-call(s32[1,18]{1,0:T(1,128)S(4)} %get-tuple-element.37.partner_ref.refs_0_, s32[1,2304]{1,0:T(1,128)S(1)} %get-tuple-element.38.turn_ref.refs_1_, f32[9,32,128]{2,1,0:T(8,128)S(1)} %get-tuple-element.51.refs_2_, ...), custom_call_target="tpu_custom_call" | custom-call | tf_op jit(solution)/shard_map/pallas_call | solution.py:405
  28.2 1.1 %collective-permute-start.7 = (bf16[9,32,128]{2,1,0:T(8,128)(2,1)S(1)}, bf16[9,32,128]{2,1,0:T(8,128)(2,1)S(1)}, u32[]{:S(2)}, u32[]{:S(2)}) collective-permute-start(bf16[9,32,128]{2,1,0:T(8,128)(2,1)S(1)} %get-tuple-element.55.own0_ref), channel_id=1, source_target_pairs={{0,1},{1,0},{2,3},{3,2},{4,5},{5,4},{6,7},{7,6},{8,9},{9,8},{10,11... | collective-permute-start | bytes 221192 | tf_op jit(solution)/shard_map/ppermute | solution.py:375
  29.4 0.6 %shard_map.114 = (f32[9,32,128]{2,1,0:T(8,128)S(1)}, bf16[9,32,128]{2,1,0:T(8,128)(2,1)S(1)}) custom-call(s32[1,18]{1,0:T(1,128)S(4)} %get-tuple-element.37.partner_ref.refs_0_, s32[1,2304]{1,0:T(1,128)S(1)} %get-tuple-element.38.turn_ref.refs_1_, f32[9,32,128]{2,1,0:T(8,128)S(1)} %get-tuple-element.57.refs_2_, ...), custom_call_target="tpu_custom_call" | custom-call | tf_op jit(solution)/shard_map/pallas_call | solution.py:405
  30.0 1.0 %collective-permute-start.8 = (bf16[9,32,128]{2,1,0:T(8,128)(2,1)S(1)}, bf16[9,32,128]{2,1,0:T(8,128)(2,1)S(1)}, u32[]{:S(2)}, u32[]{:S(2)}) collective-permute-start(bf16[9,32,128]{2,1,0:T(8,128)(2,1)S(1)} %get-tuple-element.61.own1_ref), channel_id=1, source_target_pairs={{0,1},{1,0},{2,3},{3,2},{4,5},{5,4},{6,7},{7,6},{8,9},{9,8},{10,11... | collective-permute-start | bytes 221192 | tf_op jit(solution)/shard_map/ppermute | solution.py:375
  31.0 0.7 %shard_map.115.refs_1_.early_ref = f32[9,32,128]{2,1,0:T(8,128)S(1)} custom-call(s32[18,1,18]{2,1,0:T(1,128)S(4)} %get-tuple-element.39.order_ref, s32[18,1,18]{2,1,0:T(1,128)S(4)} %get-tuple-element.40.sorted_ref, s32[1,18]{1,0:T(1,128)S(4)} %get-tuple-element.41.ready_ref, bf16[18,18,128,128]{3,2,1,0:T(8,128)(2,1)S(1)} %get-tuple-element.42.compliance_ref, ...), custom_call_target="tpu_custom_call" | custom-call | flops 10616832 | bytes 10616832 | tf_op jit(solution)/shard_map/pallas_call | solution.py:378
  31.7 1.3 %collective-permute-done.7.refs_0_.other0_ref = bf16[9,32,128]{2,1,0:T(8,128)(2,1)S(1)} collective-permute-done((bf16[9,32,128]{2,1,0:T(8,128)(2,1)S(1)}, bf16[9,32,128]{2,1,0:T(8,128)(2,1)S(1)}, u32[]{:S(2)}, u32[]{:S(2)}) %collective-permute-start.7) | collective-permute-done | bytes 73760 | tf_op jit(solution)/shard_map/ppermute | solution.py:375
  33.0 1.0 %shard_map.116.early_ref = f32[9,32,128]{2,1,0:T(8,128)S(1)} custom-call(s32[18,1,18]{2,1,0:T(1,128)S(4)} %get-tuple-element.39.order_ref, s32[18,1,18]{2,1,0:T(1,128)S(4)} %get-tuple-element.40.sorted_ref, s32[1,18]{1,0:T(1,128)S(4)} %get-tuple-element.41.ready_ref, bf16[18,18,128,128]{3,2,1,0:T(8,128)(2,1)S(1)} %get-tuple-element.42.compliance_ref, ...), custom_call_target="tpu_custom_call" | custom-call | flops 10616832 | bytes 10616832 | tf_op jit(solution)/shard_map/pallas_call | solution.py:378
  34.0 0.4 %collective-permute-done.8.other1_ref = bf16[9,32,128]{2,1,0:T(8,128)(2,1)S(1)} collective-permute-done((bf16[9,32,128]{2,1,0:T(8,128)(2,1)S(1)}, bf16[9,32,128]{2,1,0:T(8,128)(2,1)S(1)}, u32[]{:S(2)}, u32[]{:S(2)}) %collective-permute-start.8) | collective-permute-done | bytes 73760 | tf_op jit(solution)/shard_map/ppermute | solution.py:375
  34.4 1.0 %shard_map.117 = (f32[9,32,128]{2,1,0:T(8,128)S(1)}, s16[11,32,128]{2,1,0:T(8,128)(2,1)S(1)}) custom-call(s32[18,1,18]{2,1,0:T(1,128)S(4)} %get-tuple-element.39.order_ref, s32[18,1,18]{2,1,0:T(1,128)S(4)} %get-tuple-element.40.sorted_ref, s32[1,18]{1,0:T(1,128)S(4)} %get-tuple-element.41.ready_ref, ...), custom_call_target="tpu_custom_call" | custom-call | flops 21233664 | bytes 21233664 | tf_op jit(solution)/shard_map/pallas_call | solution.py:389
  35.4 1.1 %collective-permute-start.9 = (s16[11,32,128]{2,1,0:T(8,128)(2,1)S(1)}, s16[11,32,128]{2,1,0:T(8,128)(2,1)S(1)}, u32[]{:S(2)}, u32[]{:S(2)}) collective-permute-start(s16[11,32,128]{2,1,0:T(8,128)(2,1)S(1)} %get-tuple-element.64), channel_id=1, source_target_pairs={{0,1},{1,0},{2,4},{3,5},{4,2},{5,3},{6,8},{7,9},{8,6},{9,7},{10,12... | collective-permute-start | bytes 270344 | tf_op jit(solution)/shard_map/ppermute | solution.py:394
  36.5 1.4 %shard_map.118 = (f32[9,32,128]{2,1,0:T(8,128)S(1)}, s16[10,32,128]{2,1,0:T(8,128)(2,1)S(1)}) custom-call(s32[18,1,18]{2,1,0:T(1,128)S(4)} %get-tuple-element.39.order_ref, s32[18,1,18]{2,1,0:T(1,128)S(4)} %get-tuple-element.40.sorted_ref, s32[1,18]{1,0:T(1,128)S(4)} %get-tuple-element.41.ready_ref, ...), custom_call_target="tpu_custom_call" | custom-call | flops 21233664 | bytes 21233664 | tf_op jit(solution)/shard_map/pallas_call | solution.py:389
  38.3 1.0 %collective-permute-done.10.refs_3_ = s16[10,32,128]{2,1,0:T(8,128)(2,1)S(1)} collective-permute-done((s16[10,32,128]{2,1,0:T(8,128)(2,1)S(1)}, s16[10,32,128]{2,1,0:T(8,128)(2,1)S(1)}, u32[]{:S(2)}, u32[]{:S(2)}) %collective-permute-start.10) | collective-permute-done | bytes 81952 | tf_op jit(solution)/shard_map/ppermute | solution.py:394
  39.3 1.3 %shard_map.119 = (bf16[32,2304]{1,0:T(8,128)(2,1)}, bf16[32,2304]{1,0:T(8,128)(2,1)}) custom-call(s32[1,18]{1,0:T(1,128)S(4)} %get-tuple-element.37.partner_ref.refs_0_, s32[1,2304]{1,0:T(1,128)S(1)} %get-tuple-element.38.turn_ref.refs_1_, f32[9,32,128]{2,1,0:T(8,128)S(1)} %get-tuple-element.66.refs_2_, ...), custom_call_target="tpu_custom_call" | custom-call | tf_op jit(solution)/shard_map/pallas_call | solution.py:408
  40.6 1.3 %shard_map.120 = (bf16[32,2304]{1,0:T(8,128)(2,1)}, bf16[32,2304]{1,0:T(8,128)(2,1)}) custom-call(s32[1,18]{1,0:T(1,128)S(4)} %get-tuple-element.37.partner_ref.refs_0_, s32[1,2304]{1,0:T(1,128)S(1)} %get-tuple-element.38.turn_ref.refs_1_, f32[9,32,128]{2,1,0:T(8,128)S(1)} %get-tuple-element.63.refs_2_, ...), custom_call_target="tpu_custom_call", output_to_operand_aliasing={{0}: (6, {}), {1}: (7, {})} | custom-call | tf_op jit(solution)/shard_map/pallas_call | solution.py:408
  (8 shorter events, 1.0 us)
Async XLA Ops:
  1.7 7.5 %collective-permute-start = (bf16[32,2304]{1,0:T(8,128)(2,1)S(1)}, bf16[32,2304]{1,0:T(8,128)(2,1)S(1)}, u32[]{:S(2)}, u32[]{:S(2)}) collective-permute-start(bf16[32,2304]{1,0:T(8,128)(2,1)S(1)} %add_convert_fusion.own_ref), channel_id=1, source_target_pairs={{0,1},{1,0},{2,3},{3,2},{4,5},{5,4},{6,7},{7,6},{8,9},{9,8},{10,11... | collective-permute-start | bytes 442376 | tf_op jit(solution)/shard_map/ppermute | solution.py:354
  11.0 6.0 %collective-permute-start.2 = (f32[11,32,128]{2,1,0:T(8,128)S(1)}, f32[11,32,128]{2,1,0:T(8,128)S(1)}, u32[]{:S(2)}, u32[]{:S(2)}) collective-permute-start(f32[11,32,128]{2,1,0:T(8,128)S(1)} %shard_map.107.own_ref), channel_id=1, source_target_pairs={{0,1},{1,0},{2,4},{3,5},{4,2},{5,3},{6,8},{7,9},{8,6},{9,7},{10,12... | collective-permute-start | bytes 540680 | tf_op jit(solution)/shard_map/ppermute | solution.py:394
  13.8 1.7 %collective-permute-start.1 = (f32[10,32,128]{2,1,0:T(8,128)S(1)}, f32[10,32,128]{2,1,0:T(8,128)S(1)}, u32[]{:S(2)}, u32[]{:S(2)}) collective-permute-start(f32[10,32,128]{2,1,0:T(8,128)S(1)} %shard_map.105.own_ref), channel_id=1, source_target_pairs={{0,2},{2,0},{4,6},{6,4},{8,10},{10,8},{12,14},{14,12},{16,18},{18,... | collective-permute-start | bytes 491528 | tf_op jit(solution)/shard_map/ppermute | solution.py:394
  15.8 5.1 %collective-permute-start.3 = (bf16[9,32,128]{2,1,0:T(8,128)(2,1)S(1)}, bf16[9,32,128]{2,1,0:T(8,128)(2,1)S(1)}, u32[]{:S(2)}, u32[]{:S(2)}) collective-permute-start(bf16[9,32,128]{2,1,0:T(8,128)(2,1)S(1)} %get-tuple-element.48.own0_ref), channel_id=1, source_target_pairs={{0,1},{1,0},{2,3},{3,2},{4,5},{5,4},{6,7},{7,6},{8,9},{9,8},{10,11... | collective-permute-start | bytes 221192 | tf_op jit(solution)/shard_map/ppermute | solution.py:375
  17.2 4.8 %collective-permute-start.4 = (bf16[9,32,128]{2,1,0:T(8,128)(2,1)S(1)}, bf16[9,32,128]{2,1,0:T(8,128)(2,1)S(1)}, u32[]{:S(2)}, u32[]{:S(2)}) collective-permute-start(bf16[9,32,128]{2,1,0:T(8,128)(2,1)S(1)} %get-tuple-element.49.own1_ref), channel_id=1, source_target_pairs={{0,1},{1,0},{2,3},{3,2},{4,5},{5,4},{6,7},{7,6},{8,9},{9,8},{10,11... | collective-permute-start | bytes 221192 | tf_op jit(solution)/shard_map/ppermute | solution.py:375
  23.0 6.4 %collective-permute-start.6 = (s16[11,32,128]{2,1,0:T(8,128)(2,1)S(1)}, s16[11,32,128]{2,1,0:T(8,128)(2,1)S(1)}, u32[]{:S(2)}, u32[]{:S(2)}) collective-permute-start(s16[11,32,128]{2,1,0:T(8,128)(2,1)S(1)} %get-tuple-element.58), channel_id=1, source_target_pairs={{0,1},{1,0},{2,4},{3,5},{4,2},{5,3},{6,8},{7,9},{8,6},{9,7},{10,12... | collective-permute-start | bytes 270344 | tf_op jit(solution)/shard_map/ppermute | solution.py:394
  25.5 2.2 %collective-permute-start.5 = (s16[10,32,128]{2,1,0:T(8,128)(2,1)S(1)}, s16[10,32,128]{2,1,0:T(8,128)(2,1)S(1)}, u32[]{:S(2)}, u32[]{:S(2)}) collective-permute-start(s16[10,32,128]{2,1,0:T(8,128)(2,1)S(1)} %get-tuple-element.52), channel_id=1, source_target_pairs={{0,2},{2,0},{4,6},{6,4},{8,10},{10,8},{12,14},{14,12},{16,18},{18,... | collective-permute-start | bytes 245768 | tf_op jit(solution)/shard_map/ppermute | solution.py:394
  28.2 4.7 %collective-permute-start.7 = (bf16[9,32,128]{2,1,0:T(8,128)(2,1)S(1)}, bf16[9,32,128]{2,1,0:T(8,128)(2,1)S(1)}, u32[]{:S(2)}, u32[]{:S(2)}) collective-permute-start(bf16[9,32,128]{2,1,0:T(8,128)(2,1)S(1)} %get-tuple-element.55.own0_ref), channel_id=1, source_target_pairs={{0,1},{1,0},{2,3},{3,2},{4,5},{5,4},{6,7},{7,6},{8,9},{9,8},{10,11... | collective-permute-start | bytes 221192 | tf_op jit(solution)/shard_map/ppermute | solution.py:375
  30.0 4.4 %collective-permute-start.8 = (bf16[9,32,128]{2,1,0:T(8,128)(2,1)S(1)}, bf16[9,32,128]{2,1,0:T(8,128)(2,1)S(1)}, u32[]{:S(2)}, u32[]{:S(2)}) collective-permute-start(bf16[9,32,128]{2,1,0:T(8,128)(2,1)S(1)} %get-tuple-element.61.own1_ref), channel_id=1, source_target_pairs={{0,1},{1,0},{2,3},{3,2},{4,5},{5,4},{6,7},{7,6},{8,9},{9,8},{10,11... | collective-permute-start | bytes 221192 | tf_op jit(solution)/shard_map/ppermute | solution.py:375
  35.4 5.1 %collective-permute-start.9 = (s16[11,32,128]{2,1,0:T(8,128)(2,1)S(1)}, s16[11,32,128]{2,1,0:T(8,128)(2,1)S(1)}, u32[]{:S(2)}, u32[]{:S(2)}) collective-permute-start(s16[11,32,128]{2,1,0:T(8,128)(2,1)S(1)} %get-tuple-element.64), channel_id=1, source_target_pairs={{0,1},{1,0},{2,4},{3,5},{4,2},{5,3},{6,8},{7,9},{8,6},{9,7},{10,12... | collective-permute-start | bytes 270344 | tf_op jit(solution)/shard_map/ppermute | solution.py:394
  37.9 1.3 %collective-permute-start.10 = (s16[10,32,128]{2,1,0:T(8,128)(2,1)S(1)}, s16[10,32,128]{2,1,0:T(8,128)(2,1)S(1)}, u32[]{:S(2)}, u32[]{:S(2)}) collective-permute-start(s16[10,32,128]{2,1,0:T(8,128)(2,1)S(1)} %get-tuple-element.67), channel_id=1, source_target_pairs={{0,2},{2,0},{4,6},{6,4},{8,10},{10,8},{12,14},{14,12},{16,18},{18,... | collective-permute-start | bytes 245768 | tf_op jit(solution)/shard_map/ppermute | solution.py:394
where the time goes:
time: 42.1 us; the launch traced here: 41.9 us
  Pallas kernels  20.4 us (48%)
  starting transfers between devices  12.9 us (31%)
  waiting for transfers between devices  6.76 us (16%)
  other arithmetic  1.02 us (2%)
  between operations  0.77 us (2%)
    ppermute x6, starting transfers between devices, shards(): mates[side] = lax.ppermute(sent, axes, pairs)  5.61 us
    pallas_call x4, Pallas kernels, shards(): call(functools.partial(linear_section, side), [SMEM] * 3 + [VMEM] * 8, (f...  4.74 us
    pallas_call x1, Pallas kernels, shards(): call(fetch, [HBM] * 9, (pltpu.VMEM((faces, stored, extent, extent), jnp.b...  4.5 us
    ppermute x4, starting transfers between devices, shards(): other = [lax.ppermute(half[side], 'row', swap) for side in range(2)]  4.33 us
    ppermute x4, waiting for transfers between devices, shards(): other = [lax.ppermute(half[side], 'row', swap) for side in range(2)]  3.81 us
    pallas_call x2, Pallas kernels, shards(): call(functools.partial(first_section, side), [SMEM] * 2 + [VMEM] * 8, f32...  3.51 us
    pallas_call x4, Pallas kernels, shards(): call(functools.partial(early_products, side), [SMEM] * 3 + [VMEM] * (3 +...  3.31 us
    ppermute x1, starting transfers between devices, shards(): other = lax.ppermute(own, 'row', swap)  3 us
  transfers between devices with their start and end apart: 11, of which 7 were waited for; matrix products, arithmetic and copies ran while one was open for 0% of the time, Pallas kernels for 36%

commit v1 on v0

--- a/solution.py
+++ b/solution.py
@@ -186,27 +186,25 @@
 
 def encode(values_ref, sent_ref):
     group, times, extent = values_ref.shape
-    lane = lax.broadcasted_iota(jnp.int32, (times, extent), 1)
+    row = lax.broadcasted_iota(jnp.int32, (times, extent), 0)
     exponents = jnp.zeros((times, extent), jnp.float32)
     for index in range(group):
         values = values_ref[index]
-        largest = jnp.max(jnp.abs(values), axis=1, keepdims=True)
+        largest = jnp.max(jnp.max(jnp.abs(values), axis=0, keepdims=True), axis=1, keepdims=True)
         exponent = jnp.floor(jnp.log2(jnp.maximum(largest, LEAST))) - 14.0
         steps = jnp.clip(jnp.round(values * jnp.exp2(-exponent)), -32767.0, 32767.0)
         sent_ref[index] = steps.astype(jnp.int32).astype(jnp.int16)
-        exponents = jnp.where(lane == index, exponent, exponents)
+        exponents = jnp.where(row == index, exponent, exponents)
     sent_ref[group] = exponents.astype(jnp.int32).astype(jnp.int16)
     for plane in range(group + 1, sent_ref.shape[0]):
         sent_ref[plane] = jnp.zeros_like(sent_ref[plane])
 
 
-def decoder(sent_ref, group):
-    exponents = sent_ref[group].astype(jnp.int32).astype(jnp.float32)
-    lane = lax.broadcasted_iota(jnp.int32, exponents.shape, 1)
+def decoder(group, sent_ref, steps_ref):
+    steps_ref[...] = jnp.exp2(sent_ref[group].astype(jnp.int32).astype(jnp.float32))
 
     def face_of(index):
-        exponent = jnp.sum(jnp.where(lane == index, exponents, 0.0), axis=1, keepdims=True)
-        return sent_ref[index].astype(jnp.int32).astype(jnp.float32) * jnp.exp2(exponent)
+        return sent_ref[index].astype(jnp.int32).astype(jnp.float32) * steps_ref[pl.ds(index, 1), :]
 
     return face_of
 
@@ -259,10 +257,10 @@
         half_ref[index] = robin.astype(jnp.bfloat16)
 
 
-def local_faces(side, partner_ref, turn_ref, own_ref, mate_ref, stiff_ref, record_ref):
+def local_faces(side, partner_ref, turn_ref, own_ref, mate_ref, stiff_ref, record_ref, steps_ref):
     group, _, extent = own_ref.shape
     first = position(group)[side]
-    mate_face = decoder(mate_ref, group)
+    mate_face = decoder(group, mate_ref, steps_ref)
     for index in range(group):
         face = first + index
         here = lanes_of(index, extent)
@@ -272,17 +270,17 @@
 
 
 def local_group(side, *refs):
-    *ins, robin_ref, half_ref = refs
-    for index, traction, motion in local_faces(side, *ins):
+    *ins, robin_ref, half_ref, steps_ref = refs
+    for index, traction, motion in local_faces(side, *ins, steps_ref):
         robin = traction + motion
         robin_ref[index] = robin
         half_ref[index] = robin.astype(jnp.bfloat16)
 
 
 def local_last(side, *refs):
-    ins, (motion_hbm, traction_hbm, motion_ref, traction_ref, sems) = refs[:6], refs[-5:]
+    ins, (motion_hbm, traction_hbm, steps_ref, motion_ref, traction_ref, sems) = refs[:6], refs[-6:]
     group, _, extent = ins[2].shape
-    for index, traction, motion in local_faces(side, *ins):
+    for index, traction, motion in local_faces(side, *ins, steps_ref):
         here = lanes_of(index, extent)
         motion_ref[:, here] = motion.astype(jnp.bfloat16)
         traction_ref[:, here] = traction.astype(jnp.bfloat16)
@@ -348,6 +346,7 @@
     part = (group, times, extent)
     flat = (times, faces * extent)
     block_bytes = faces * stored * extent * extent * 2
+    steps = pltpu.VMEM((times, extent), jnp.float32)
     halves = pltpu.VMEM((rows * faces, times, extent), jnp.bfloat16)
     in_hbm = functools.partial(pltpu.with_memory_space_constraint, memory_space=pltpu.HBM)
     own = (start_traction[0].astype(jnp.float32) + starting_motion[0].astype(jnp.float32)).astype(jnp.bfloat16)
@@ -402,12 +401,14 @@
                     (f32(*part), bf16(*part), f32(1, group * extent), f32(1, group * extent)),
                 )(*ins)
             elif not last:
-                robin[side], half[side] = call(functools.partial(local_group, side), specs, (f32(*part), bf16(*part)))(*ins)
+                robin[side], half[side] = call(
+                    functools.partial(local_group, side), specs, (f32(*part), bf16(*part)), [steps],
+                )(*ins)
             else:
                 share = pltpu.VMEM((times, group * extent), jnp.bfloat16)
                 outs = call(
                     functools.partial(local_last, side), specs + [HBM] * len(outs), (bf16(*flat),) * 2,
-                    [share, share, pltpu.SemaphoreType.DMA((2,))], 0, (HBM,) * 2, {6 + n: n for n in range(len(outs))},
+                    [steps, share, share, pltpu.SemaphoreType.DMA((2,))], 0, (HBM,) * 2, {6 + n: n for n in range(len(outs))},
                 )(*ins, *outs)
     return tuple(out[None] for out in outs)
 

time: 42.1 us -> 41 us (0.974)
  Pallas kernels: 20.4 us -> 18.9 us
    pallas_call x2, Pallas kernels: 2.59 us -> 1.89 us  [shards(): call(functools.partial(local_last, side), specs + [HBM] * len(outs), (bf1...]
    pallas_call x2, Pallas kernels: 1.21 us -> 0.51 us  [shards(): call(functools.partial(local_group, side), specs, (f32(*part), bf16(*part...]
  transfers between devices with their start and end apart: 11 -> 11, of which waited for: 7 -> 7; matrix products, arithmetic and copies ran while one was open for 0% -> 0% of each run, Pallas kernels for 36% -> 35%
where the time goes in v1:
time: 41 us; the launch traced here: 40.7 us
  Pallas kernels  18.9 us (46%)
  starting transfers between devices  12.9 us (31%)
  waiting for transfers between devices  7.12 us (17%)
  other arithmetic  1.02 us (2%)
  between operations  0.78 us (2%)
    ppermute x6, starting transfers between devices, shards(): mates[side] = lax.ppermute(sent, axes, pairs)  5.61 us
    pallas_call x4, Pallas kernels, shards(): call(functools.partial(linear_section, side), [SMEM] * 3 + [VMEM] * 8, (f...  4.66 us
    pallas_call x1, Pallas kernels, shards(): call(fetch, [HBM] * 9, (pltpu.VMEM((faces, stored, extent, extent), jnp.b...  4.5 us
    ppermute x4, starting transfers between devices, shards(): other = [lax.ppermute(half[side], 'row', swap) for side in range(2)]  4.33 us
    ppermute x4, waiting for transfers between devices, shards(): other = [lax.ppermute(half[side], 'row', swap) for side in range(2)]  4.16 us
    pallas_call x2, Pallas kernels, shards(): call(functools.partial(first_section, side), [SMEM] * 2 + [VMEM] * 8, f32...  3.51 us
    pallas_call x4, Pallas kernels, shards(): call(functools.partial(early_products, side), [SMEM] * 3 + [VMEM] * (3 +...  3.31 us
    ppermute x1, starting transfers between devices, shards(): other = lax.ppermute(own, 'row', swap)  3 us
  transfers between devices with their start and end apart: 11, of which 7 were waited for; matrix products, arithmetic and copies ran while one was open for 0% of the time, Pallas kernels for 35%

profile of v1, /device:TPU:0, one launch (start us, length us, event | category | flops | bytes accessed | tf_op | source)
XLA Modules:
  0.0 40.7 jit_solution(15861723864200246506)
XLA Ops:
  0.6 1.0 %add_convert_fusion.own_ref = bf16[32,2304]{1,0:T(8,128)(2,1)S(1)} fusion(bf16[1,32,2304]{2,1,0:T(8,128)(2,1)} %param.13, bf16[1,32,2304]{2,1,0:T(8,128)(2,1)} %param.12), kind=kLoop, calls=%fused_computation | loop fusion | flops 294912 | bytes 442368 | tf_op jit(solution)/shard_map/convert_element_type | solution.py:352
  1.7 3.0 %collective-permute-start = (bf16[32,2304]{1,0:T(8,128)(2,1)S(1)}, bf16[32,2304]{1,0:T(8,128)(2,1)S(1)}, u32[]{:S(2)}, u32[]{:S(2)}) collective-permute-start(bf16[32,2304]{1,0:T(8,128)(2,1)S(1)} %add_convert_fusion.own_ref), channel_id=1, source_target_pairs={{0,1},{1,0},{2,3},{3,2},{4,5},{5,4},{6,7},{7,6},{8,9},{9,8},{10,11... | collective-permute-start | bytes 442376 | tf_op jit(solution)/shard_map/ppermute | solution.py:353
  4.7 4.5 %shard_map.104 = (bf16[18,18,128,128]{3,2,1,0:T(8,128)(2,1)S(1)}, bf16[32,2304]{1,0:T(8,128)(2,1)S(1)}, bf16[32,2304]{1,0:T(8,128)(2,1)S(1)}, bf16[32,2304]{1,0:...) custom-call(bf16[18,18,128,128]{3,2,1,0:T(8,128)(2,1)} %bitcast.10, ...), custom_call_target="tpu_custom_call" | custom-call | flops 10616832 | bytes 10616832 | tf_op jit(solution)/shard_map/pallas_call | solution.py:354
  9.2 1.8 %shard_map.107.own_ref = f32[11,32,128]{2,1,0:T(8,128)S(1)} custom-call(s32[18,1,18]{2,1,0:T(1,128)S(4)} %get-tuple-element.39.order_ref, s32[18,1,18]{2,1,0:T(1,128)S(4)} %get-tuple-element.40.sorted_ref, bf16[18,18,128,128]{3,2,1,0:T(8,128)(2,1)S(1)} %get-tuple-element.42.compliance_ref, bf16[32,2304]{1,0:T(8,128)(2,1)S(1)} %add_convert_fusion.own_ref, ...), custom_call_target="tpu_custom_call" | custom-call | flops 21233664 | bytes 21233664 | tf_op jit(solution)/shard_map/pallas_call | solution.py:383
  11.0 1.1 %collective-permute-start.2 = (f32[11,32,128]{2,1,0:T(8,128)S(1)}, f32[11,32,128]{2,1,0:T(8,128)S(1)}, u32[]{:S(2)}, u32[]{:S(2)}) collective-permute-start(f32[11,32,128]{2,1,0:T(8,128)S(1)} %shard_map.107.own_ref), channel_id=1, source_target_pairs={{0,1},{1,0},{2,4},{3,5},{4,2},{5,3},{6,8},{7,9},{8,6},{9,7},{10,12... | collective-permute-start | bytes 540680 | tf_op jit(solution)/shard_map/ppermute | solution.py:393
  12.1 1.7 %shard_map.105.own_ref = f32[10,32,128]{2,1,0:T(8,128)S(1)} custom-call(s32[18,1,18]{2,1,0:T(1,128)S(4)} %get-tuple-element.39.order_ref, s32[18,1,18]{2,1,0:T(1,128)S(4)} %get-tuple-element.40.sorted_ref, bf16[18,18,128,128]{3,2,1,0:T(8,128)(2,1)S(1)} %get-tuple-element.42.compliance_ref, bf16[32,2304]{1,0:T(8,128)(2,1)S(1)} %add_convert_fusion.own_ref, ...), custom_call_target="tpu_custom_call" | custom-call | flops 21233664 | bytes 21233664 | tf_op jit(solution)/shard_map/pallas_call | solution.py:383
  13.8 0.6 %collective-permute-start.1 = (f32[10,32,128]{2,1,0:T(8,128)S(1)}, f32[10,32,128]{2,1,0:T(8,128)S(1)}, u32[]{:S(2)}, u32[]{:S(2)}) collective-permute-start(f32[10,32,128]{2,1,0:T(8,128)S(1)} %shard_map.105.own_ref), channel_id=1, source_target_pairs={{0,2},{2,0},{4,6},{6,4},{8,10},{10,8},{12,14},{14,12},{16,18},{18,... | collective-permute-start | bytes 491528 | tf_op jit(solution)/shard_map/ppermute | solution.py:393
  14.5 1.0 %collective-permute-done.1.mate_ref = f32[10,32,128]{2,1,0:T(8,128)S(1)} collective-permute-done((f32[10,32,128]{2,1,0:T(8,128)S(1)}, f32[10,32,128]{2,1,0:T(8,128)S(1)}, u32[]{:S(2)}, u32[]{:S(2)}) %collective-permute-start.1) | collective-permute-done | bytes 163872 | tf_op jit(solution)/shard_map/ppermute | solution.py:393
  15.8 1.1 %collective-permute-start.3 = (bf16[9,32,128]{2,1,0:T(8,128)(2,1)S(1)}, bf16[9,32,128]{2,1,0:T(8,128)(2,1)S(1)}, u32[]{:S(2)}, u32[]{:S(2)}) collective-permute-start(bf16[9,32,128]{2,1,0:T(8,128)(2,1)S(1)} %get-tuple-element.48.own0_ref), channel_id=1, source_target_pairs={{0,1},{1,0},{2,3},{3,2},{4,5},{5,4},{6,7},{7,6},{8,9},{9,8},{10,11... | collective-permute-start | bytes 221192 | tf_op jit(solution)/shard_map/ppermute | solution.py:374
  16.9 0.3 shard_map.108
  17.2 1.0 %collective-permute-start.4 = (bf16[9,32,128]{2,1,0:T(8,128)(2,1)S(1)}, bf16[9,32,128]{2,1,0:T(8,128)(2,1)S(1)}, u32[]{:S(2)}, u32[]{:S(2)}) collective-permute-start(bf16[9,32,128]{2,1,0:T(8,128)(2,1)S(1)} %get-tuple-element.49.own1_ref), channel_id=1, source_target_pairs={{0,1},{1,0},{2,3},{3,2},{4,5},{5,4},{6,7},{7,6},{8,9},{9,8},{10,11... | collective-permute-start | bytes 221192 | tf_op jit(solution)/shard_map/ppermute | solution.py:374
  18.2 0.7 %shard_map.109.early_ref.refs_1_ = f32[9,32,128]{2,1,0:T(8,128)S(1)} custom-call(s32[18,1,18]{2,1,0:T(1,128)S(4)} %get-tuple-element.39.order_ref, s32[18,1,18]{2,1,0:T(1,128)S(4)} %get-tuple-element.40.sorted_ref, s32[1,18]{1,0:T(1,128)S(4)} %get-tuple-element.41.ready_ref, bf16[18,18,128,128]{3,2,1,0:T(8,128)(2,1)S(1)} %get-tuple-element.42.compliance_ref, ...), custom_call_target="tpu_custom_call" | custom-call | flops 10616832 | bytes 10616832 | tf_op jit(solution)/shard_map/pallas_call | solution.py:377
  18.9 2.0 %collective-permute-done.3.other0_ref.refs_0_ = bf16[9,32,128]{2,1,0:T(8,128)(2,1)S(1)} collective-permute-done((bf16[9,32,128]{2,1,0:T(8,128)(2,1)S(1)}, bf16[9,32,128]{2,1,0:T(8,128)(2,1)S(1)}, u32[]{:S(2)}, u32[]{:S(2)}) %collective-permute-start.3) | collective-permute-done | bytes 73760 | tf_op jit(solution)/shard_map/ppermute | solution.py:374
  20.8 1.0 %shard_map.112.early_ref = f32[9,32,128]{2,1,0:T(8,128)S(1)} custom-call(s32[18,1,18]{2,1,0:T(1,128)S(4)} %get-tuple-element.39.order_ref, s32[18,1,18]{2,1,0:T(1,128)S(4)} %get-tuple-element.40.sorted_ref, s32[1,18]{1,0:T(1,128)S(4)} %get-tuple-element.41.ready_ref, bf16[18,18,128,128]{3,2,1,0:T(8,128)(2,1)S(1)} %get-tuple-element.42.compliance_ref, ...), custom_call_target="tpu_custom_call" | custom-call | flops 10616832 | bytes 10616832 | tf_op jit(solution)/shard_map/pallas_call | solution.py:377
  21.9 1.0 %shard_map.113 = (f32[9,32,128]{2,1,0:T(8,128)S(1)}, s16[11,32,128]{2,1,0:T(8,128)(2,1)S(1)}) custom-call(s32[18,1,18]{2,1,0:T(1,128)S(4)} %get-tuple-element.39.order_ref, s32[18,1,18]{2,1,0:T(1,128)S(4)} %get-tuple-element.40.sorted_ref, s32[1,18]{1,0:T(1,128)S(4)} %get-tuple-element.41.ready_ref, ...), custom_call_target="tpu_custom_call" | custom-call | flops 21233664 | bytes 21233664 | tf_op jit(solution)/shard_map/pallas_call | solution.py:388
  22.9 1.1 %collective-permute-start.6 = (s16[11,32,128]{2,1,0:T(8,128)(2,1)S(1)}, s16[11,32,128]{2,1,0:T(8,128)(2,1)S(1)}, u32[]{:S(2)}, u32[]{:S(2)}) collective-permute-start(s16[11,32,128]{2,1,0:T(8,128)(2,1)S(1)} %get-tuple-element.58), channel_id=1, source_target_pairs={{0,1},{1,0},{2,4},{3,5},{4,2},{5,3},{6,8},{7,9},{8,6},{9,7},{10,12... | collective-permute-start | bytes 270344 | tf_op jit(solution)/shard_map/ppermute | solution.py:393
  24.1 1.3 %shard_map.110 = (f32[9,32,128]{2,1,0:T(8,128)S(1)}, s16[10,32,128]{2,1,0:T(8,128)(2,1)S(1)}) custom-call(s32[18,1,18]{2,1,0:T(1,128)S(4)} %get-tuple-element.39.order_ref, s32[18,1,18]{2,1,0:T(1,128)S(4)} %get-tuple-element.40.sorted_ref, s32[1,18]{1,0:T(1,128)S(4)} %get-tuple-element.41.ready_ref, ...), custom_call_target="tpu_custom_call" | custom-call | flops 21233664 | bytes 21233664 | tf_op jit(solution)/shard_map/pallas_call | solution.py:388
  25.4 1.3 %collective-permute-start.5 = (s16[10,32,128]{2,1,0:T(8,128)(2,1)S(1)}, s16[10,32,128]{2,1,0:T(8,128)(2,1)S(1)}, u32[]{:S(2)}, u32[]{:S(2)}) collective-permute-start(s16[10,32,128]{2,1,0:T(8,128)(2,1)S(1)} %get-tuple-element.52), channel_id=1, source_target_pairs={{0,2},{2,0},{4,6},{6,4},{8,10},{10,8},{12,14},{14,12},{16,18},{18,... | collective-permute-start | bytes 245768 | tf_op jit(solution)/shard_map/ppermute | solution.py:393
  26.7 0.9 %collective-permute-done.5.refs_3_ = s16[10,32,128]{2,1,0:T(8,128)(2,1)S(1)} collective-permute-done((s16[10,32,128]{2,1,0:T(8,128)(2,1)S(1)}, s16[10,32,128]{2,1,0:T(8,128)(2,1)S(1)}, u32[]{:S(2)}, u32[]{:S(2)}) %collective-permute-start.5) | collective-permute-done | bytes 81952 | tf_op jit(solution)/shard_map/ppermute | solution.py:393
  27.9 1.1 %collective-permute-start.7 = (bf16[9,32,128]{2,1,0:T(8,128)(2,1)S(1)}, bf16[9,32,128]{2,1,0:T(8,128)(2,1)S(1)}, u32[]{:S(2)}, u32[]{:S(2)}) collective-permute-start(bf16[9,32,128]{2,1,0:T(8,128)(2,1)S(1)} %get-tuple-element.55.own0_ref), channel_id=1, source_target_pairs={{0,1},{1,0},{2,3},{3,2},{4,5},{5,4},{6,7},{7,6},{8,9},{9,8},{10,11... | collective-permute-start | bytes 221192 | tf_op jit(solution)/shard_map/ppermute | solution.py:374
  29.0 0.3 shard_map.114
  29.2 1.0 %collective-permute-start.8 = (bf16[9,32,128]{2,1,0:T(8,128)(2,1)S(1)}, bf16[9,32,128]{2,1,0:T(8,128)(2,1)S(1)}, u32[]{:S(2)}, u32[]{:S(2)}) collective-permute-start(bf16[9,32,128]{2,1,0:T(8,128)(2,1)S(1)} %get-tuple-element.61.own1_ref), channel_id=1, source_target_pairs={{0,1},{1,0},{2,3},{3,2},{4,5},{5,4},{6,7},{7,6},{8,9},{9,8},{10,11... | collective-permute-start | bytes 221192 | tf_op jit(solution)/shard_map/ppermute | solution.py:374
  30.3 0.7 %shard_map.115.refs_1_.early_ref = f32[9,32,128]{2,1,0:T(8,128)S(1)} custom-call(s32[18,1,18]{2,1,0:T(1,128)S(4)} %get-tuple-element.39.order_ref, s32[18,1,18]{2,1,0:T(1,128)S(4)} %get-tuple-element.40.sorted_ref, s32[1,18]{1,0:T(1,128)S(4)} %get-tuple-element.41.ready_ref, bf16[18,18,128,128]{3,2,1,0:T(8,128)(2,1)S(1)} %get-tuple-element.42.compliance_ref, ...), custom_call_target="tpu_custom_call" | custom-call | flops 10616832 | bytes 10616832 | tf_op jit(solution)/shard_map/pallas_call | solution.py:377
  30.9 2.0 %collective-permute-done.7.refs_0_.other0_ref = bf16[9,32,128]{2,1,0:T(8,128)(2,1)S(1)} collective-permute-done((bf16[9,32,128]{2,1,0:T(8,128)(2,1)S(1)}, bf16[9,32,128]{2,1,0:T(8,128)(2,1)S(1)}, u32[]{:S(2)}, u32[]{:S(2)}) %collective-permute-start.7) | collective-permute-done | bytes 73760 | tf_op jit(solution)/shard_map/ppermute | solution.py:374
  32.9 1.0 %shard_map.116.early_ref = f32[9,32,128]{2,1,0:T(8,128)S(1)} custom-call(s32[18,1,18]{2,1,0:T(1,128)S(4)} %get-tuple-element.39.order_ref, s32[18,1,18]{2,1,0:T(1,128)S(4)} %get-tuple-element.40.sorted_ref, s32[1,18]{1,0:T(1,128)S(4)} %get-tuple-element.41.ready_ref, bf16[18,18,128,128]{3,2,1,0:T(8,128)(2,1)S(1)} %get-tuple-element.42.compliance_ref, ...), custom_call_target="tpu_custom_call" | custom-call | flops 10616832 | bytes 10616832 | tf_op jit(solution)/shard_map/pallas_call | solution.py:377
  34.0 1.0 %shard_map.117 = (f32[9,32,128]{2,1,0:T(8,128)S(1)}, s16[11,32,128]{2,1,0:T(8,128)(2,1)S(1)}) custom-call(s32[18,1,18]{2,1,0:T(1,128)S(4)} %get-tuple-element.39.order_ref, s32[18,1,18]{2,1,0:T(1,128)S(4)} %get-tuple-element.40.sorted_ref, s32[1,18]{1,0:T(1,128)S(4)} %get-tuple-element.41.ready_ref, ...), custom_call_target="tpu_custom_call" | custom-call | flops 21233664 | bytes 21233664 | tf_op jit(solution)/shard_map/pallas_call | solution.py:388
  35.0 1.1 %collective-permute-start.9 = (s16[11,32,128]{2,1,0:T(8,128)(2,1)S(1)}, s16[11,32,128]{2,1,0:T(8,128)(2,1)S(1)}, u32[]{:S(2)}, u32[]{:S(2)}) collective-permute-start(s16[11,32,128]{2,1,0:T(8,128)(2,1)S(1)} %get-tuple-element.64), channel_id=1, source_target_pairs={{0,1},{1,0},{2,4},{3,5},{4,2},{5,3},{6,8},{7,9},{8,6},{9,7},{10,12... | collective-permute-start | bytes 270344 | tf_op jit(solution)/shard_map/ppermute | solution.py:393
  36.1 1.3 %shard_map.118 = (f32[9,32,128]{2,1,0:T(8,128)S(1)}, s16[10,32,128]{2,1,0:T(8,128)(2,1)S(1)}) custom-call(s32[18,1,18]{2,1,0:T(1,128)S(4)} %get-tuple-element.39.order_ref, s32[18,1,18]{2,1,0:T(1,128)S(4)} %get-tuple-element.40.sorted_ref, s32[1,18]{1,0:T(1,128)S(4)} %get-tuple-element.41.ready_ref, ...), custom_call_target="tpu_custom_call" | custom-call | flops 21233664 | bytes 21233664 | tf_op jit(solution)/shard_map/pallas_call | solution.py:388
  37.5 0.3 collective-permute-start.10
  37.8 1.0 %collective-permute-done.10.refs_3_ = s16[10,32,128]{2,1,0:T(8,128)(2,1)S(1)} collective-permute-done((s16[10,32,128]{2,1,0:T(8,128)(2,1)S(1)}, s16[10,32,128]{2,1,0:T(8,128)(2,1)S(1)}, u32[]{:S(2)}, u32[]{:S(2)}) %collective-permute-start.10) | collective-permute-done | bytes 81952 | tf_op jit(solution)/shard_map/ppermute | solution.py:393
  38.8 0.9 %shard_map.119 = (bf16[32,2304]{1,0:T(8,128)(2,1)}, bf16[32,2304]{1,0:T(8,128)(2,1)}) custom-call(s32[1,18]{1,0:T(1,128)S(4)} %get-tuple-element.37.partner_ref.refs_0_, s32[1,2304]{1,0:T(1,128)S(1)} %get-tuple-element.38.turn_ref.refs_1_, f32[9,32,128]{2,1,0:T(8,128)S(1)} %get-tuple-element.66.refs_2_, ...), custom_call_target="tpu_custom_call" | custom-call | tf_op jit(solution)/shard_map/pallas_call | solution.py:409
  39.8 0.9 %shard_map.120 = (bf16[32,2304]{1,0:T(8,128)(2,1)}, bf16[32,2304]{1,0:T(8,128)(2,1)}) custom-call(s32[1,18]{1,0:T(1,128)S(4)} %get-tuple-element.37.partner_ref.refs_0_, s32[1,2304]{1,0:T(1,128)S(1)} %get-tuple-element.38.turn_ref.refs_1_, f32[9,32,128]{2,1,0:T(8,128)S(1)} %get-tuple-element.63.refs_2_, ...), custom_call_target="tpu_custom_call", output_to_operand_aliasing={{0}: (6, {}), {1}: (7, {})} | custom-call | tf_op jit(solution)/shard_map/pallas_call | solution.py:409
  (8 shorter events, 0.7 us)
Async XLA Ops:
  1.7 7.5 %collective-permute-start = (bf16[32,2304]{1,0:T(8,128)(2,1)S(1)}, bf16[32,2304]{1,0:T(8,128)(2,1)S(1)}, u32[]{:S(2)}, u32[]{:S(2)}) collective-permute-start(bf16[32,2304]{1,0:T(8,128)(2,1)S(1)} %add_convert_fusion.own_ref), channel_id=1, source_target_pairs={{0,1},{1,0},{2,3},{3,2},{4,5},{5,4},{6,7},{7,6},{8,9},{9,8},{10,11... | collective-permute-start | bytes 442376 | tf_op jit(solution)/shard_map/ppermute | solution.py:353
  11.0 5.9 %collective-permute-start.2 = (f32[11,32,128]{2,1,0:T(8,128)S(1)}, f32[11,32,128]{2,1,0:T(8,128)S(1)}, u32[]{:S(2)}, u32[]{:S(2)}) collective-permute-start(f32[11,32,128]{2,1,0:T(8,128)S(1)} %shard_map.107.own_ref), channel_id=1, source_target_pairs={{0,1},{1,0},{2,4},{3,5},{4,2},{5,3},{6,8},{7,9},{8,6},{9,7},{10,12... | collective-permute-start | bytes 540680 | tf_op jit(solution)/shard_map/ppermute | solution.py:393
  13.8 1.7 %collective-permute-start.1 = (f32[10,32,128]{2,1,0:T(8,128)S(1)}, f32[10,32,128]{2,1,0:T(8,128)S(1)}, u32[]{:S(2)}, u32[]{:S(2)}) collective-permute-start(f32[10,32,128]{2,1,0:T(8,128)S(1)} %shard_map.105.own_ref), channel_id=1, source_target_pairs={{0,2},{2,0},{4,6},{6,4},{8,10},{10,8},{12,14},{14,12},{16,18},{18,... | collective-permute-start | bytes 491528 | tf_op jit(solution)/shard_map/ppermute | solution.py:393
  15.8 5.1 %collective-permute-start.3 = (bf16[9,32,128]{2,1,0:T(8,128)(2,1)S(1)}, bf16[9,32,128]{2,1,0:T(8,128)(2,1)S(1)}, u32[]{:S(2)}, u32[]{:S(2)}) collective-permute-start(bf16[9,32,128]{2,1,0:T(8,128)(2,1)S(1)} %get-tuple-element.48.own0_ref), channel_id=1, source_target_pairs={{0,1},{1,0},{2,3},{3,2},{4,5},{5,4},{6,7},{7,6},{8,9},{9,8},{10,11... | collective-permute-start | bytes 221192 | tf_op jit(solution)/shard_map/ppermute | solution.py:374
  17.2 4.8 %collective-permute-start.4 = (bf16[9,32,128]{2,1,0:T(8,128)(2,1)S(1)}, bf16[9,32,128]{2,1,0:T(8,128)(2,1)S(1)}, u32[]{:S(2)}, u32[]{:S(2)}) collective-permute-start(bf16[9,32,128]{2,1,0:T(8,128)(2,1)S(1)} %get-tuple-element.49.own1_ref), channel_id=1, source_target_pairs={{0,1},{1,0},{2,3},{3,2},{4,5},{5,4},{6,7},{7,6},{8,9},{9,8},{10,11... | collective-permute-start | bytes 221192 | tf_op jit(solution)/shard_map/ppermute | solution.py:374
  22.9 6.0 %collective-permute-start.6 = (s16[11,32,128]{2,1,0:T(8,128)(2,1)S(1)}, s16[11,32,128]{2,1,0:T(8,128)(2,1)S(1)}, u32[]{:S(2)}, u32[]{:S(2)}) collective-permute-start(s16[11,32,128]{2,1,0:T(8,128)(2,1)S(1)} %get-tuple-element.58), channel_id=1, source_target_pairs={{0,1},{1,0},{2,4},{3,5},{4,2},{5,3},{6,8},{7,9},{8,6},{9,7},{10,12... | collective-permute-start | bytes 270344 | tf_op jit(solution)/shard_map/ppermute | solution.py:393
  25.4 2.2 %collective-permute-start.5 = (s16[10,32,128]{2,1,0:T(8,128)(2,1)S(1)}, s16[10,32,128]{2,1,0:T(8,128)(2,1)S(1)}, u32[]{:S(2)}, u32[]{:S(2)}) collective-permute-start(s16[10,32,128]{2,1,0:T(8,128)(2,1)S(1)} %get-tuple-element.52), channel_id=1, source_target_pairs={{0,2},{2,0},{4,6},{6,4},{8,10},{10,8},{12,14},{14,12},{16,18},{18,... | collective-permute-start | bytes 245768 | tf_op jit(solution)/shard_map/ppermute | solution.py:393
  27.9 5.1 %collective-permute-start.7 = (bf16[9,32,128]{2,1,0:T(8,128)(2,1)S(1)}, bf16[9,32,128]{2,1,0:T(8,128)(2,1)S(1)}, u32[]{:S(2)}, u32[]{:S(2)}) collective-permute-start(bf16[9,32,128]{2,1,0:T(8,128)(2,1)S(1)} %get-tuple-element.55.own0_ref), channel_id=1, source_target_pairs={{0,1},{1,0},{2,3},{3,2},{4,5},{5,4},{6,7},{7,6},{8,9},{9,8},{10,11... | collective-permute-start | bytes 221192 | tf_op jit(solution)/shard_map/ppermute | solution.py:374
  29.2 4.8 %collective-permute-start.8 = (bf16[9,32,128]{2,1,0:T(8,128)(2,1)S(1)}, bf16[9,32,128]{2,1,0:T(8,128)(2,1)S(1)}, u32[]{:S(2)}, u32[]{:S(2)}) collective-permute-start(bf16[9,32,128]{2,1,0:T(8,128)(2,1)S(1)} %get-tuple-element.61.own1_ref), channel_id=1, source_target_pairs={{0,1},{1,0},{2,3},{3,2},{4,5},{5,4},{6,7},{7,6},{8,9},{9,8},{10,11... | collective-permute-start | bytes 221192 | tf_op jit(solution)/shard_map/ppermute | solution.py:374
  35.0 4.8 %collective-permute-start.9 = (s16[11,32,128]{2,1,0:T(8,128)(2,1)S(1)}, s16[11,32,128]{2,1,0:T(8,128)(2,1)S(1)}, u32[]{:S(2)}, u32[]{:S(2)}) collective-permute-start(s16[11,32,128]{2,1,0:T(8,128)(2,1)S(1)} %get-tuple-element.64), channel_id=1, source_target_pairs={{0,1},{1,0},{2,4},{3,5},{4,2},{5,3},{6,8},{7,9},{8,6},{9,7},{10,12... | collective-permute-start | bytes 270344 | tf_op jit(solution)/shard_map/ppermute | solution.py:393
  37.5 1.3 %collective-permute-start.10 = (s16[10,32,128]{2,1,0:T(8,128)(2,1)S(1)}, s16[10,32,128]{2,1,0:T(8,128)(2,1)S(1)}, u32[]{:S(2)}, u32[]{:S(2)}) collective-permute-start(s16[10,32,128]{2,1,0:T(8,128)(2,1)S(1)} %get-tuple-element.67), channel_id=1, source_target_pairs={{0,2},{2,0},{4,6},{6,4},{8,10},{10,8},{12,14},{14,12},{16,18},{18,... | collective-permute-start | bytes 245768 | tf_op jit(solution)/shard_map/ppermute | solution.py:393

commit v2 on v1

--- a/solution.py
+++ b/solution.py
@@ -11,6 +11,7 @@
 SUBLANES = 8
 LEAST = 2.0**-100
 EARLY = (6, 10)
+FIRST = 6
 VMEM_BYTES = 24 * 2**20
 
 ONSET_JUMP = 0.15
@@ -31,7 +32,7 @@
     return pl.ds(pl.multiple_of(face * extent, extent), extent)
 
 
-def sort_blocks(columns_ref, order_ref, sorted_ref, ready_ref):
+def sort_blocks(columns_ref, order_ref, sorted_ref, own_ref, ready_ref):
     faces, _, stored = columns_ref.shape
     group = faces // 2
     near, far, mine = position(group)
@@ -41,36 +42,23 @@
     def sort_row(face, _):
         in_far = (face >= far) & (face < far + group)
         width = jnp.where(in_far, group, 0)
-        front, back = jnp.int32(0), jnp.int32(stored - 1)
+        columns = [columns_ref[face, 0, j] for j in range(stored)]
+        owned = [(column >= own) & (column < own + faces) for column in columns]
+        count = sum(jnp.where(here, 1, 0) for here in owned)
+        front, middle, back = jnp.int32(0), count, jnp.int32(stored - 1)
         for j in range(stored):
-            column = columns_ref[face, 0, j]
-            early = ((column >= own) & (column < own + faces)) | ((column >= partner) & (column < partner + width))
-            place = jnp.where(early, front, back)
+            soon = (columns[j] >= partner) & (columns[j] < partner + width)
+            place = jnp.where(owned[j], front, jnp.where(soon, middle, back))
             order_ref[face, 0, place] = j
-            sorted_ref[face, 0, place] = column
-            front = jnp.where(early, front + 1, front)
-            back = jnp.where(early, back, back - 1)
-        ready_ref[0, face] = front
+            sorted_ref[face, 0, place] = columns[j]
+            front = jnp.where(owned[j], front + 1, front)
+            middle = jnp.where(soon, middle + 1, middle)
+            back = jnp.where(owned[j] | soon, back, back - 1)
+        own_ref[0, face] = count
+        ready_ref[0, face] = middle
         return 0
 
     lax.fori_loop(0, faces, sort_row, 0)
-
-
-def fetch(blocks_hbm, load_hbm, motion_hbm, stress_hbm, stiff_hbm, record_hbm, turn_hbm, columns_hbm, partner_hbm,
-          blocks_ref, load_ref, motion_ref, stress_ref, stiff_ref, record_ref, turn_ref, partner_ref,
-          order_ref, sorted_ref, ready_ref, columns_ref, sems):
-    pairs = [
-        (columns_hbm, columns_ref), (load_hbm, load_ref), (motion_hbm, motion_ref), (stress_hbm, stress_ref),
-        (stiff_hbm, stiff_ref), (record_hbm, record_ref), (turn_hbm, turn_ref), (partner_hbm, partner_ref),
-    ]
-    pairs += [(blocks_hbm.at[face], blocks_ref.at[face]) for face in range(blocks_hbm.shape[0])]
-    copies = [pltpu.make_async_copy(source, target, sems.at[n]) for n, (source, target) in enumerate(pairs)]
-    for copy in copies:
-        copy.start()
-    copies[0].wait()
-    sort_blocks(columns_ref, order_ref, sorted_ref, ready_ref)
-    for copy in copies[1:]:
-        copy.wait()
 
 
 def block_products(parts):
@@ -97,9 +85,58 @@
         finish(group - 1, sum(block_products([whole[:cut], whole[cut:]])))
 
 
+def early_entries(half_ref, order_ref, sorted_ref, ready_ref, compliance_ref, count, face):
+    ready, none = ready_ref[0, face], half_ref.shape[0] - 1
+    return [
+        (half_ref[jnp.where(slot < ready, sorted_ref[face, 0, slot], none)], compliance_ref[face, order_ref[face, 0, slot]])
+        for slot in range(count)
+    ]
+
+
+def fetch(blocks_hbm, load_hbm, motion_hbm, stress_hbm, stiff_hbm, record_hbm, turn_hbm, columns_hbm, partner_hbm, half_in_ref,
+          blocks_ref, load_ref, motion_ref, stress_ref, stiff_ref, record_ref, turn_ref, partner_ref,
+          order_ref, sorted_ref, own_ref, ready_ref, early0_ref, early1_ref, columns_ref, half_ref, sems):
+    group, _, extent = early0_ref.shape
+    faces = 2 * group
+    *starts, mine = position(group)
+    columns_copy = pltpu.make_async_copy(columns_hbm, columns_ref, sems.at[0])
+    columns_copy.start()
+    rows = [[], []]
+    for side in (1, 0):
+        for index in range(group):
+            face = starts[side] + index
+            row = pltpu.make_async_copy(blocks_hbm.at[face], blocks_ref.at[face], sems.at[1 + side * group + index])
+            row.start()
+            rows[side].append(row)
+    pairs = (
+        (load_hbm, load_ref), (motion_hbm, motion_ref), (stress_hbm, stress_ref), (stiff_hbm, stiff_ref),
+        (record_hbm, record_ref), (turn_hbm, turn_ref), (partner_hbm, partner_ref),
+    )
+    small = [pltpu.make_async_copy(source, target, sems.at[1 + faces + n]) for n, (source, target) in enumerate(pairs)]
+    for copy in small:
+        copy.start()
+    for face in range(faces):
+        half_ref[mine * faces + face] = half_in_ref[:, face * extent : (face + 1) * extent]
+    none = half_ref.shape[0] - 1
+    half_ref[none] = jnp.zeros_like(half_ref[none])
+    columns_copy.wait()
+    sort_blocks(columns_ref, order_ref, sorted_ref, own_ref, ready_ref)
+    entries = functools.partial(early_entries, half_ref, order_ref, sorted_ref, own_ref, blocks_ref, FIRST)
+    for side, out_ref in ((1, early1_ref), (0, early0_ref)):
+        for index in range(0, group, 2):
+            count = min(2, group - index)
+            for row in rows[side][index : index + count]:
+                row.wait()
+            products = block_products([entries(starts[side] + index + k) for k in range(count)])
+            for k in range(count):
+                out_ref[index + k] = products[k]
+    for copy in small:
+        copy.wait()
+
+
 def early_products(side, order_ref, sorted_ref, ready_ref, compliance_ref, own0_ref, own1_ref, *refs):
     out_ref, half_ref = refs[-2:]
-    group, times, _ = out_ref.shape
+    group = out_ref.shape[0]
     faces = compliance_ref.shape[0]
     *starts, mine = position(group)
     none = half_ref.shape[0] - 1
@@ -108,13 +145,7 @@
         half_ref[pl.ds(mine * faces + start, group)] = ref[...]
     for ref in refs[:side]:
         half_ref[pl.ds((1 - mine) * faces + starts[0], group)] = ref[...]
-
-    def entries(face):
-        ready = ready_ref[0, face]
-        return [
-            (half_ref[jnp.where(slot < ready, sorted_ref[face, 0, slot], none)], compliance_ref[face, order_ref[face, 0, slot]])
-            for slot in range(EARLY[side])
-        ]
+    entries = functools.partial(early_entries, half_ref, order_ref, sorted_ref, ready_ref, compliance_ref, EARLY[side])
 
     def finish(index, product):
         out_ref[index] = product
@@ -122,65 +153,66 @@
     group_products(starts[side], group, entries, finish)
 
 
-def sorted_entry(half_ref, order_ref, sorted_ref, compliance_ref, face, slot):
-    return half_ref[sorted_ref[face, 0, slot]], compliance_ref[face, order_ref[face, 0, slot]]
-
-
-def first_section(side, order_ref, sorted_ref, compliance_ref, own_ref, other_ref, motion_ref, stress_ref, load_ref,
-                  stiff_ref, record_ref, out_ref, half_ref):
-    times = motion_ref.shape[0]
-    faces, stored, extent, _ = compliance_ref.shape
+def late_products(first, done, order_ref, sorted_ref, ready_ref, compliance_ref, half_ref, finish, out_ref):
+    group, stored = compliance_ref.shape[0] // 2, compliance_ref.shape[1]
+
+    def entry(face, slot):
+        return half_ref[sorted_ref[face, 0, slot]], compliance_ref[face, order_ref[face, 0, slot]]
+
+    group_products(first, group, lambda face: [entry(face, slot) for slot in range(done, stored)], finish)
+
+    def missed(slot, index):
+        out_ref[index] -= 2.0 * block_products([[entry(first + index, slot)]])[0]
+        return index
+
+    least = ready_ref[0, first]
+    for index in range(1, group):
+        least = jnp.minimum(least, ready_ref[0, first + index])
+
+    @pl.when(least < done)
+    def _():
+        for index in range(group):
+            lax.fori_loop(ready_ref[0, first + index], done, missed, index)
+
+
+def first_section(side, order_ref, sorted_ref, own_count_ref, compliance_ref, own_ref, other_ref, motion_ref, stress_ref,
+                  load_ref, early_ref, stiff_ref, record_ref, out_ref, half_ref):
+    faces, _, extent, _ = compliance_ref.shape
     group = faces // 2
     *starts, mine = position(group)
     first = starts[side]
     for run, ref in ((mine, own_ref), (1 - mine, other_ref)):
         for face in range(faces):
             half_ref[run * faces + face] = ref[:, face * extent : (face + 1) * extent]
-    entry = functools.partial(sorted_entry, half_ref, order_ref, sorted_ref, compliance_ref)
 
     def finish(index, product):
         lanes = lanes_of(first + index, extent)
         robin = stress_ref[:, lanes].astype(jnp.float32) + motion_ref[:, lanes].astype(jnp.float32)
-        response = product + load_ref[:, lanes].astype(jnp.float32)
+        response = early_ref[index] + product + load_ref[:, lanes].astype(jnp.float32)
         out_ref[index] = robin - 2.0 * response
         out_ref[group, index : index + 1] = stiff_ref[:, lanes]
         out_ref[group, group + index : group + index + 1] = record_ref[:, lanes]
 
     for plane in range(group, out_ref.shape[0]):
         out_ref[plane] = jnp.zeros_like(out_ref[plane])
-    group_products(first, group, lambda face: [entry(face, slot) for slot in range(stored)], finish)
+    late_products(first, FIRST, order_ref, sorted_ref, own_count_ref, compliance_ref, half_ref, finish, out_ref)
 
 
 def linear_section(side, order_ref, sorted_ref, ready_ref, compliance_ref, own0_ref, own1_ref, other0_ref, other1_ref,
                    robin_ref, load_ref, early_ref, out_ref, sent_ref, half_ref):
-    group, times, extent = own0_ref.shape
-    faces, stored = compliance_ref.shape[:2]
+    group, _, extent = own0_ref.shape
+    faces = compliance_ref.shape[0]
     *starts, mine = position(group)
-    first, done = starts[side], EARLY[side]
+    first = starts[side]
     for run, parts in ((mine, (own0_ref, own1_ref)), (1 - mine, (other0_ref, other1_ref))):
         for start, ref in zip(starts, parts):
             half_ref[pl.ds(run * faces + start, group)] = ref[...]
-    entry = functools.partial(sorted_entry, half_ref, order_ref, sorted_ref, compliance_ref)
 
     def finish(index, product):
         response = early_ref[index] + product + load_ref[:, lanes_of(first + index, extent)].astype(jnp.float32)
         out_ref[index] = robin_ref[index] - 2.0 * response
 
-    group_products(first, group, lambda face: [entry(face, slot) for slot in range(done, stored)], finish)
-
-    def missed(slot, index):
-        out_ref[index] -= 2.0 * block_products([[entry(first + index, slot)]])[0]
-        return index
-
-    least = ready_ref[0, first]
-    for index in range(1, group):
-        least = jnp.minimum(least, ready_ref[0, first + index])
-
-    @pl.when(least < done)
-    def _():
-        for index in range(group):
-            lax.fori_loop(ready_ref[0, first + index], done, missed, index)
-
+    late_products(first, EARLY[side], order_ref, sorted_ref, ready_ref, compliance_ref, half_ref, finish, out_ref)
     encode(out_ref, sent_ref)
 
 
@@ -278,21 +310,33 @@
 
 
 def local_last(side, *refs):
-    ins, (motion_hbm, traction_hbm, steps_ref, motion_ref, traction_ref, sems) = refs[:6], refs[-6:]
+    ins, near = refs[:6], refs[6:8]
+    if side:
+        *outs, steps_ref, motion_ref, traction_ref, sems = refs[8:]
+    else:
+        motion_ref, traction_ref, steps_ref = refs[6:]
     group, _, extent = ins[2].shape
+    starts = position(group)[:2]
+
+    def copies(part, sources):
+        lanes = pl.ds(pl.multiple_of(starts[part] * extent, extent), group * extent)
+        return [
+            pltpu.make_async_copy(source, out.at[:, lanes], sems.at[2 * part + n])
+            for n, (source, out) in enumerate(zip(sources, outs))
+        ]
+
+    if side:
+        for copy in copies(0, near):
+            copy.start()
     for index, traction, motion in local_faces(side, *ins, steps_ref):
         here = lanes_of(index, extent)
         motion_ref[:, here] = motion.astype(jnp.bfloat16)
         traction_ref[:, here] = traction.astype(jnp.bfloat16)
-    lanes = pl.ds(pl.multiple_of(position(group)[side] * extent, extent), group * extent)
-    copies = [
-        pltpu.make_async_copy(motion_ref, motion_hbm.at[:, lanes], sems.at[0]),
-        pltpu.make_async_copy(traction_ref, traction_hbm.at[:, lanes], sems.at[1]),
-    ]
-    for copy in copies:
-        copy.start()
-    for copy in copies:
-        copy.wait()
+    if side:
+        for copy in copies(1, (motion_ref, traction_ref)):
+            copy.start()
+        for copy in copies(0, near) + copies(1, (motion_ref, traction_ref)):
+            copy.wait()
 
 
 def shards(
@@ -329,7 +373,7 @@
     def s32(*shape):
         return jax.ShapeDtypeStruct(shape, jnp.int32)
 
-    def call(kernel, in_specs, out_shape, scratch=(), moved=0, out_specs=(), aliases={}):
+    def call(kernel, in_specs, out_shape, scratch=(), moved=0, out_specs=()):
         outs = out_shape if isinstance(out_shape, tuple) else (out_shape,)
         out_specs = out_specs or (VMEM,) * len(outs)
         return pl.pallas_call(
@@ -338,7 +382,6 @@
             in_specs=in_specs,
             out_specs=out_specs if isinstance(out_shape, tuple) else out_specs[0],
             scratch_shapes=scratch,
-            input_output_aliases=aliases,
             compiler_params=pltpu.CompilerParams(vmem_limit_bytes=VMEM_BYTES),
             cost_estimate=pl.CostEstimate(flops=moved, bytes_accessed=moved, transcendentals=0) if moved else None,
         )
@@ -351,20 +394,20 @@
     in_hbm = functools.partial(pltpu.with_memory_space_constraint, memory_space=pltpu.HBM)
     own = (start_traction[0].astype(jnp.float32) + starting_motion[0].astype(jnp.float32)).astype(jnp.bfloat16)
     other = lax.ppermute(own, "row", swap)
-    blocks, load, motion, stress, stiff, record, turn, partner, *tables = call(
-        fetch, [HBM] * 9,
+    table, counts = pltpu.SMEM((faces, 1, stored), jnp.int32), pltpu.SMEM((1, faces), jnp.int32)
+    blocks, load, motion, stress, stiff, record, turn, *tables, first0, first1 = call(
+        fetch, [HBM] * 9 + [VMEM],
         (pltpu.VMEM((faces, stored, extent, extent), jnp.bfloat16), bf16(*flat), bf16(*flat), bf16(*flat),
-         f32(1, faces * extent), f32(1, faces * extent), s32(1, faces * extent), pltpu.SMEM((1, faces), jnp.int32),
-         pltpu.SMEM((faces, 1, stored), jnp.int32), pltpu.SMEM((faces, 1, stored), jnp.int32), pltpu.SMEM((1, faces), jnp.int32)),
-        [pltpu.SMEM((faces, 1, stored), jnp.int32), pltpu.SemaphoreType.DMA((8 + faces,))],
-        block_bytes, (VMEM,) * 7 + (SMEM,) * 4,
+         f32(1, faces * extent), f32(1, faces * extent), s32(1, faces * extent),
+         counts, table, table, counts, counts, f32(*part), f32(*part)),
+        [table, pltpu.VMEM((rows * faces + 1, times, extent), jnp.bfloat16), pltpu.SemaphoreType.DMA((8 + faces,))],
+        block_bytes, (VMEM,) * 7 + (SMEM,) * 5 + (VMEM,) * 2,
     )(
         in_hbm(compliance[0]), in_hbm(load_response[0]), in_hbm(starting_motion[0]), in_hbm(start_traction[0]),
         in_hbm(stiffness), in_hbm(history), in_hbm(orientation.reshape(1, -1)),
-        in_hbm(jnp.transpose(block_columns, (1, 0, 2))), in_hbm(face_partner),
+        in_hbm(jnp.transpose(block_columns, (1, 0, 2))), in_hbm(face_partner), own,
     )
-    in_smem = functools.partial(pltpu.with_memory_space_constraint, memory_space=pltpu.SMEM)
-    partner, tables = in_smem(partner), [in_smem(table) for table in tables]
+    partner, order, columns, owned, ready = (pltpu.with_memory_space_constraint(value, pltpu.SMEM) for value in tables)
 
     robin, half = [None, None], [None, None]
     stiffs, records = [stiff, stiff], [record, record]
@@ -377,19 +420,19 @@
             early.append(call(
                 functools.partial(early_products, side), [SMEM] * 3 + [VMEM] * (3 + side) + [ANY] * side, f32(*part),
                 [pltpu.VMEM((rows * faces + 1, times, extent), jnp.bfloat16)], block_bytes,
-            )(*tables, blocks, *half, *other[:side], *early))
+            )(order, columns, ready, blocks, *half, *other[:side], *early))
         for side, (axes, pairs) in enumerate((("sub", near_pairs), (("sub", "row"), far_pairs))):
             if begin:
                 ascent[side] = sent = call(
-                    functools.partial(first_section, side), [SMEM] * 2 + [VMEM] * 8,
+                    functools.partial(first_section, side), [SMEM] * 3 + [VMEM] * 9,
                     f32(group + 1 + side, times, extent), [halves], 2 * block_bytes,
-                )(*tables[:2], blocks, own, other, motion, stress, load, stiff, record)
+                )(order, columns, owned, blocks, own, other, motion, stress, load, (first0, first1)[side], stiff, record)
             else:
                 ascent[side], sent = call(
                     functools.partial(linear_section, side), [SMEM] * 3 + [VMEM] * 8,
                     (f32(*part), jax.ShapeDtypeStruct((group + 1 + side, times, extent), jnp.int16)),
                     [halves], 2 * block_bytes,
-                )(*tables, blocks, *half, *other, robin[side], load, early[side])
+                )(order, columns, ready, blocks, *half, *other, robin[side], load, early[side])
             mates[side] = lax.ppermute(sent, axes, pairs)
         outs = ()
         for side in range(2):
@@ -405,11 +448,15 @@
                     functools.partial(local_group, side), specs, (f32(*part), bf16(*part)), [steps],
                 )(*ins)
             else:
-                share = pltpu.VMEM((times, group * extent), jnp.bfloat16)
-                outs = call(
-                    functools.partial(local_last, side), specs + [HBM] * len(outs), (bf16(*flat),) * 2,
-                    [steps, share, share, pltpu.SemaphoreType.DMA((2,))], 0, (HBM,) * 2, {6 + n: n for n in range(len(outs))},
-                )(*ins, *outs)
+                share = (times, group * extent)
+                if side:
+                    outs = call(
+                        functools.partial(local_last, side), specs + [VMEM] * 2, (bf16(*flat),) * 2,
+                        [steps, pltpu.VMEM(share, jnp.bfloat16), pltpu.VMEM(share, jnp.bfloat16), pltpu.SemaphoreType.DMA((4,))],
+                        0, (HBM,) * 2,
+                    )(*ins, *outs)
+                else:
+                    outs = call(functools.partial(local_last, side), specs, (bf16(*share),) * 2, [steps])(*ins)
     return tuple(out[None] for out in outs)
 
 

time: 41 us -> 43.6 us (1.063)
  Pallas kernels: 18.9 us -> 20.5 us
  waiting for transfers between devices: 7.12 us -> 8.12 us
    pallas_call x5, Pallas kernels: 9.9 us -> 11.5 us  [the longest x1 7.77 us: shards(): call(fetch, [HBM] * 9 + [VMEM], (pltpu.VMEM((faces, stored, extent, exten...]
    ppermute x6, waiting for transfers between devices: 2.96 us -> 3.88 us  [shards(): mates[side] = lax.ppermute(sent, axes, pairs)]
  transfers between devices with their start and end apart: 11 -> 11, of which waited for: 7 -> 8; matrix products, arithmetic and copies ran while one was open for 0% -> 0% of each run, Pallas kernels for 35% -> 38%
where the time goes in v2:
time: 43.6 us; the launch traced here: 43.3 us
  Pallas kernels  20.5 us (47%)
  starting transfers between devices  12.9 us (30%)
  waiting for transfers between devices  8.12 us (19%)
  other arithmetic  1.02 us (2%)
  between operations  0.77 us (2%)
    pallas_call x1, Pallas kernels, shards(): call(fetch, [HBM] * 9 + [VMEM], (pltpu.VMEM((faces, stored, extent, exten...  7.77 us
    ppermute x6, starting transfers between devices, shards(): mates[side] = lax.ppermute(sent, axes, pairs)  6.03 us
    pallas_call x4, Pallas kernels, shards(): call(functools.partial(linear_section, side), [SMEM] * 3 + [VMEM] * 8, (f...  4.69 us
    ppermute x4, waiting for transfers between devices, shards(): other = [lax.ppermute(half[side], 'row', swap) for side in range(2)]  4.23 us
    ppermute x4, starting transfers between devices, shards(): other = [lax.ppermute(half[side], 'row', swap) for side in range(2)]  3.91 us
    ppermute x6, waiting for transfers between devices, shards(): mates[side] = lax.ppermute(sent, axes, pairs)  3.88 us
    pallas_call x4, Pallas kernels, shards(): call(functools.partial(early_products, side), [SMEM] * 3 + [VMEM] * (3 +...  3.31 us
    ppermute x1, starting transfers between devices, shards(): other = lax.ppermute(own, 'row', swap)  3 us
  transfers between devices with their start and end apart: 11, of which 8 were waited for; matrix products, arithmetic and copies ran while one was open for 0% of the time, Pallas kernels for 38%

profile of v2, /device:TPU:0, one launch (start us, length us, event | category | flops | bytes accessed | tf_op | source)
XLA Modules:
  0.0 43.3 jit_solution(9321808366396386114)
XLA Ops:
  0.6 1.0 %add_convert_fusion.half_in_ref.own_ref = bf16[32,2304]{1,0:T(8,128)(2,1)S(1)} fusion(bf16[1,32,2304]{2,1,0:T(8,128)(2,1)} %param.13, bf16[1,32,2304]{2,1,0:T(8,128)(2,1)} %param.12), kind=kLoop, calls=%fused_computation | loop fusion | flops 294912 | bytes 442368 | tf_op jit(solution)/shard_map/convert_element_type | solution.py:395
  1.7 3.0 %collective-permute-start = (bf16[32,2304]{1,0:T(8,128)(2,1)S(1)}, bf16[32,2304]{1,0:T(8,128)(2,1)S(1)}, u32[]{:S(2)}, u32[]{:S(2)}) collective-permute-start(bf16[32,2304]{1,0:T(8,128)(2,1)S(1)} %add_convert_fusion.half_in_ref.own_ref), channel_id=1, source_target_pairs={{0,1},{1,0},{2,3},{3,2},{4,5},{5,4},{6,7},{7,6},{8,9},{9,8},{10,11... | collective-permute-start | bytes 442376 | tf_op jit(solution)/shard_map/ppermute | solution.py:396
  4.7 7.8 %shard_map.104 = (bf16[18,18,128,128]{3,2,1,0:T(8,128)(2,1)S(1)}, bf16[32,2304]{1,0:T(8,128)(2,1)S(1)}, bf16[32,2304]{1,0:T(8,128)(2,1)S(1)}, bf16[32,2304]{1,0:...) custom-call(bf16[18,18,128,128]{3,2,1,0:T(8,128)(2,1)} %bitcast.10, ...), custom_call_target="tpu_custom_call" | custom-call | flops 10616832 | bytes 10616832 | tf_op jit(solution)/shard_map/pallas_call | solution.py:398
  12.4 1.3 %shard_map.107.own_ref = f32[11,32,128]{2,1,0:T(8,128)S(1)} custom-call(s32[18,1,18]{2,1,0:T(1,128)S(4)} %get-tuple-element.42.order_ref, s32[18,1,18]{2,1,0:T(1,128)S(4)} %get-tuple-element.43.sorted_ref, s32[1,18]{1,0:T(1,128)S(4)} %get-tuple-element.46.own_count_ref, bf16[18,18,128,128]{3,2,1,0:T(8,128)(2,1)S(1)} %get-tuple-element.45.compliance_ref, ...), custom_call_target="tpu_custom_call" | custom-call | flops 21233664 | bytes 21233664 | tf_op jit(solution)/shard_map/pallas_call | solution.py:426
  13.8 1.2 %shard_map.105.own_ref = f32[10,32,128]{2,1,0:T(8,128)S(1)} custom-call(s32[18,1,18]{2,1,0:T(1,128)S(4)} %get-tuple-element.42.order_ref, s32[18,1,18]{2,1,0:T(1,128)S(4)} %get-tuple-element.43.sorted_ref, s32[1,18]{1,0:T(1,128)S(4)} %get-tuple-element.46.own_count_ref, bf16[18,18,128,128]{3,2,1,0:T(8,128)(2,1)S(1)} %get-tuple-element.45.compliance_ref, ...), custom_call_target="tpu_custom_call" | custom-call | flops 21233664 | bytes 21233664 | tf_op jit(solution)/shard_map/pallas_call | solution.py:426
  15.1 1.7 %collective-permute-start.1 = (f32[10,32,128]{2,1,0:T(8,128)S(1)}, f32[10,32,128]{2,1,0:T(8,128)S(1)}, u32[]{:S(2)}, u32[]{:S(2)}) collective-permute-start(f32[10,32,128]{2,1,0:T(8,128)S(1)} %shard_map.105.own_ref), channel_id=1, source_target_pairs={{0,2},{2,0},{4,6},{6,4},{8,10},{10,8},{12,14},{14,12},{16,18},{18,... | collective-permute-start | bytes 491528 | tf_op jit(solution)/shard_map/ppermute | solution.py:436
  16.7 1.0 %collective-permute-done.1.mate_ref = f32[10,32,128]{2,1,0:T(8,128)S(1)} collective-permute-done((f32[10,32,128]{2,1,0:T(8,128)S(1)}, f32[10,32,128]{2,1,0:T(8,128)S(1)}, u32[]{:S(2)}, u32[]{:S(2)}) %collective-permute-start.1) | collective-permute-done | bytes 163872 | tf_op jit(solution)/shard_map/ppermute | solution.py:436
  18.0 0.8 %collective-permute-start.3 = (bf16[9,32,128]{2,1,0:T(8,128)(2,1)S(1)}, bf16[9,32,128]{2,1,0:T(8,128)(2,1)S(1)}, u32[]{:S(2)}, u32[]{:S(2)}) collective-permute-start(bf16[9,32,128]{2,1,0:T(8,128)(2,1)S(1)} %get-tuple-element.53.own0_ref), channel_id=1, source_target_pairs={{0,1},{1,0},{2,3},{3,2},{4,5},{5,4},{6,7},{7,6},{8,9},{9,8},{10,11... | collective-permute-start | bytes 221192 | tf_op jit(solution)/shard_map/ppermute | solution.py:417
  18.8 0.4 collective-permute-done.2.mate_ref
  19.3 0.3 shard_map.108
  19.5 0.9 %collective-permute-start.4 = (bf16[9,32,128]{2,1,0:T(8,128)(2,1)S(1)}, bf16[9,32,128]{2,1,0:T(8,128)(2,1)S(1)}, u32[]{:S(2)}, u32[]{:S(2)}) collective-permute-start(bf16[9,32,128]{2,1,0:T(8,128)(2,1)S(1)} %get-tuple-element.55.own1_ref), channel_id=1, source_target_pairs={{0,1},{1,0},{2,3},{3,2},{4,5},{5,4},{6,7},{7,6},{8,9},{9,8},{10,11... | collective-permute-start | bytes 221192 | tf_op jit(solution)/shard_map/ppermute | solution.py:417
  20.5 0.7 %shard_map.109.early_ref.refs_1_ = f32[9,32,128]{2,1,0:T(8,128)S(1)} custom-call(s32[18,1,18]{2,1,0:T(1,128)S(4)} %get-tuple-element.42.order_ref, s32[18,1,18]{2,1,0:T(1,128)S(4)} %get-tuple-element.43.sorted_ref, s32[1,18]{1,0:T(1,128)S(4)} %get-tuple-element.44.ready_ref, bf16[18,18,128,128]{3,2,1,0:T(8,128)(2,1)S(1)} %get-tuple-element.45.compliance_ref, ...), custom_call_target="tpu_custom_call" | custom-call | flops 10616832 | bytes 10616832 | tf_op jit(solution)/shard_map/pallas_call | solution.py:420
  21.1 1.5 %collective-permute-done.3.other0_ref.refs_0_ = bf16[9,32,128]{2,1,0:T(8,128)(2,1)S(1)} collective-permute-done((bf16[9,32,128]{2,1,0:T(8,128)(2,1)S(1)}, bf16[9,32,128]{2,1,0:T(8,128)(2,1)S(1)}, u32[]{:S(2)}, u32[]{:S(2)}) %collective-permute-start.3) | collective-permute-done | bytes 73760 | tf_op jit(solution)/shard_map/ppermute | solution.py:417
  22.6 1.0 %shard_map.112.early_ref = f32[9,32,128]{2,1,0:T(8,128)S(1)} custom-call(s32[18,1,18]{2,1,0:T(1,128)S(4)} %get-tuple-element.42.order_ref, s32[18,1,18]{2,1,0:T(1,128)S(4)} %get-tuple-element.43.sorted_ref, s32[1,18]{1,0:T(1,128)S(4)} %get-tuple-element.44.ready_ref, bf16[18,18,128,128]{3,2,1,0:T(8,128)(2,1)S(1)} %get-tuple-element.45.compliance_ref, ...), custom_call_target="tpu_custom_call" | custom-call | flops 10616832 | bytes 10616832 | tf_op jit(solution)/shard_map/pallas_call | solution.py:420
  23.6 0.7 %collective-permute-done.4.other1_ref = bf16[9,32,128]{2,1,0:T(8,128)(2,1)S(1)} collective-permute-done((bf16[9,32,128]{2,1,0:T(8,128)(2,1)S(1)}, bf16[9,32,128]{2,1,0:T(8,128)(2,1)S(1)}, u32[]{:S(2)}, u32[]{:S(2)}) %collective-permute-start.4) | collective-permute-done | bytes 73760 | tf_op jit(solution)/shard_map/ppermute | solution.py:417
  24.3 1.0 %shard_map.113 = (f32[9,32,128]{2,1,0:T(8,128)S(1)}, s16[11,32,128]{2,1,0:T(8,128)(2,1)S(1)}) custom-call(s32[18,1,18]{2,1,0:T(1,128)S(4)} %get-tuple-element.42.order_ref, s32[18,1,18]{2,1,0:T(1,128)S(4)} %get-tuple-element.43.sorted_ref, s32[1,18]{1,0:T(1,128)S(4)} %get-tuple-element.44.ready_ref, ...), custom_call_target="tpu_custom_call" | custom-call | flops 21233664 | bytes 21233664 | tf_op jit(solution)/shard_map/pallas_call | solution.py:431
  25.3 0.6 %collective-permute-start.6 = (s16[11,32,128]{2,1,0:T(8,128)(2,1)S(1)}, s16[11,32,128]{2,1,0:T(8,128)(2,1)S(1)}, u32[]{:S(2)}, u32[]{:S(2)}) collective-permute-start(s16[11,32,128]{2,1,0:T(8,128)(2,1)S(1)} %get-tuple-element.64), channel_id=1, source_target_pairs={{0,1},{1,0},{2,4},{3,5},{4,2},{5,3},{6,8},{7,9},{8,6},{9,7},{10,12... | collective-permute-start | bytes 270344 | tf_op jit(solution)/shard_map/ppermute | solution.py:436
  25.9 1.3 %shard_map.110 = (f32[9,32,128]{2,1,0:T(8,128)S(1)}, s16[10,32,128]{2,1,0:T(8,128)(2,1)S(1)}) custom-call(s32[18,1,18]{2,1,0:T(1,128)S(4)} %get-tuple-element.42.order_ref, s32[18,1,18]{2,1,0:T(1,128)S(4)} %get-tuple-element.43.sorted_ref, s32[1,18]{1,0:T(1,128)S(4)} %get-tuple-element.44.ready_ref, ...), custom_call_target="tpu_custom_call" | custom-call | flops 21233664 | bytes 21233664 | tf_op jit(solution)/shard_map/pallas_call | solution.py:431
  27.3 2.1 %collective-permute-start.5 = (s16[10,32,128]{2,1,0:T(8,128)(2,1)S(1)}, s16[10,32,128]{2,1,0:T(8,128)(2,1)S(1)}, u32[]{:S(2)}, u32[]{:S(2)}) collective-permute-start(s16[10,32,128]{2,1,0:T(8,128)(2,1)S(1)} %get-tuple-element.58), channel_id=1, source_target_pairs={{0,2},{2,0},{4,6},{6,4},{8,10},{10,8},{12,14},{14,12},{16,18},{18,... | collective-permute-start | bytes 245768 | tf_op jit(solution)/shard_map/ppermute | solution.py:436
  29.4 0.9 %collective-permute-done.5.refs_3_ = s16[10,32,128]{2,1,0:T(8,128)(2,1)S(1)} collective-permute-done((s16[10,32,128]{2,1,0:T(8,128)(2,1)S(1)}, s16[10,32,128]{2,1,0:T(8,128)(2,1)S(1)}, u32[]{:S(2)}, u32[]{:S(2)}) %collective-permute-start.5) | collective-permute-done | bytes 81952 | tf_op jit(solution)/shard_map/ppermute | solution.py:436
  30.6 0.8 %collective-permute-start.7 = (bf16[9,32,128]{2,1,0:T(8,128)(2,1)S(1)}, bf16[9,32,128]{2,1,0:T(8,128)(2,1)S(1)}, u32[]{:S(2)}, u32[]{:S(2)}) collective-permute-start(bf16[9,32,128]{2,1,0:T(8,128)(2,1)S(1)} %get-tuple-element.61.own0_ref), channel_id=1, source_target_pairs={{0,1},{1,0},{2,3},{3,2},{4,5},{5,4},{6,7},{7,6},{8,9},{9,8},{10,11... | collective-permute-start | bytes 221192 | tf_op jit(solution)/shard_map/ppermute | solution.py:417
  31.6 1.4 %collective-permute-start.8 = (bf16[9,32,128]{2,1,0:T(8,128)(2,1)S(1)}, bf16[9,32,128]{2,1,0:T(8,128)(2,1)S(1)}, u32[]{:S(2)}, u32[]{:S(2)}) collective-permute-start(bf16[9,32,128]{2,1,0:T(8,128)(2,1)S(1)} %get-tuple-element.67.own1_ref), channel_id=1, source_target_pairs={{0,1},{1,0},{2,3},{3,2},{4,5},{5,4},{6,7},{7,6},{8,9},{9,8},{10,11... | collective-permute-start | bytes 221192 | tf_op jit(solution)/shard_map/ppermute | solution.py:417
  33.0 0.7 %shard_map.115.refs_1_.early_ref = f32[9,32,128]{2,1,0:T(8,128)S(1)} custom-call(s32[18,1,18]{2,1,0:T(1,128)S(4)} %get-tuple-element.42.order_ref, s32[18,1,18]{2,1,0:T(1,128)S(4)} %get-tuple-element.43.sorted_ref, s32[1,18]{1,0:T(1,128)S(4)} %get-tuple-element.44.ready_ref, bf16[18,18,128,128]{3,2,1,0:T(8,128)(2,1)S(1)} %get-tuple-element.45.compliance_ref, ...), custom_call_target="tpu_custom_call" | custom-call | flops 10616832 | bytes 10616832 | tf_op jit(solution)/shard_map/pallas_call | solution.py:420
  33.7 2.1 %collective-permute-done.7.refs_0_.other0_ref = bf16[9,32,128]{2,1,0:T(8,128)(2,1)S(1)} collective-permute-done((bf16[9,32,128]{2,1,0:T(8,128)(2,1)S(1)}, bf16[9,32,128]{2,1,0:T(8,128)(2,1)S(1)}, u32[]{:S(2)}, u32[]{:S(2)}) %collective-permute-start.7) | collective-permute-done | bytes 73760 | tf_op jit(solution)/shard_map/ppermute | solution.py:417
  35.8 1.0 %shard_map.116.early_ref = f32[9,32,128]{2,1,0:T(8,128)S(1)} custom-call(s32[18,1,18]{2,1,0:T(1,128)S(4)} %get-tuple-element.42.order_ref, s32[18,1,18]{2,1,0:T(1,128)S(4)} %get-tuple-element.43.sorted_ref, s32[1,18]{1,0:T(1,128)S(4)} %get-tuple-element.44.ready_ref, bf16[18,18,128,128]{3,2,1,0:T(8,128)(2,1)S(1)} %get-tuple-element.45.compliance_ref, ...), custom_call_target="tpu_custom_call" | custom-call | flops 10616832 | bytes 10616832 | tf_op jit(solution)/shard_map/pallas_call | solution.py:420
  36.8 1.0 %shard_map.117 = (f32[9,32,128]{2,1,0:T(8,128)S(1)}, s16[11,32,128]{2,1,0:T(8,128)(2,1)S(1)}) custom-call(s32[18,1,18]{2,1,0:T(1,128)S(4)} %get-tuple-element.42.order_ref, s32[18,1,18]{2,1,0:T(1,128)S(4)} %get-tuple-element.43.sorted_ref, s32[1,18]{1,0:T(1,128)S(4)} %get-tuple-element.44.ready_ref, ...), custom_call_target="tpu_custom_call" | custom-call | flops 21233664 | bytes 21233664 | tf_op jit(solution)/shard_map/pallas_call | solution.py:431
  37.8 0.7 %collective-permute-start.9 = (s16[11,32,128]{2,1,0:T(8,128)(2,1)S(1)}, s16[11,32,128]{2,1,0:T(8,128)(2,1)S(1)}, u32[]{:S(2)}, u32[]{:S(2)}) collective-permute-start(s16[11,32,128]{2,1,0:T(8,128)(2,1)S(1)} %get-tuple-element.70), channel_id=1, source_target_pairs={{0,1},{1,0},{2,4},{3,5},{4,2},{5,3},{6,8},{7,9},{8,6},{9,7},{10,12... | collective-permute-start | bytes 270344 | tf_op jit(solution)/shard_map/ppermute | solution.py:436
  38.5 1.3 %shard_map.118 = (f32[9,32,128]{2,1,0:T(8,128)S(1)}, s16[10,32,128]{2,1,0:T(8,128)(2,1)S(1)}) custom-call(s32[18,1,18]{2,1,0:T(1,128)S(4)} %get-tuple-element.42.order_ref, s32[18,1,18]{2,1,0:T(1,128)S(4)} %get-tuple-element.43.sorted_ref, s32[1,18]{1,0:T(1,128)S(4)} %get-tuple-element.44.ready_ref, ...), custom_call_target="tpu_custom_call" | custom-call | flops 21233664 | bytes 21233664 | tf_op jit(solution)/shard_map/pallas_call | solution.py:431
  39.9 0.7 %collective-permute-start.10 = (s16[10,32,128]{2,1,0:T(8,128)(2,1)S(1)}, s16[10,32,128]{2,1,0:T(8,128)(2,1)S(1)}, u32[]{:S(2)}, u32[]{:S(2)}) collective-permute-start(s16[10,32,128]{2,1,0:T(8,128)(2,1)S(1)} %get-tuple-element.73), channel_id=1, source_target_pairs={{0,2},{2,0},{4,6},{6,4},{8,10},{10,8},{12,14},{14,12},{16,18},{18,... | collective-permute-start | bytes 245768 | tf_op jit(solution)/shard_map/ppermute | solution.py:436
  40.6 0.9 %collective-permute-done.10.refs_3_ = s16[10,32,128]{2,1,0:T(8,128)(2,1)S(1)} collective-permute-done((s16[10,32,128]{2,1,0:T(8,128)(2,1)S(1)}, s16[10,32,128]{2,1,0:T(8,128)(2,1)S(1)}, u32[]{:S(2)}, u32[]{:S(2)}) %collective-permute-start.10) | collective-permute-done | bytes 81952 | tf_op jit(solution)/shard_map/ppermute | solution.py:436
  41.8 0.6 %collective-permute-done.9.refs_3_ = s16[11,32,128]{2,1,0:T(8,128)(2,1)S(1)} collective-permute-done((s16[11,32,128]{2,1,0:T(8,128)(2,1)S(1)}, s16[11,32,128]{2,1,0:T(8,128)(2,1)S(1)}, u32[]{:S(2)}, u32[]{:S(2)}) %collective-permute-start.9) | collective-permute-done | bytes 90144 | tf_op jit(solution)/shard_map/ppermute | solution.py:436
  42.4 1.0 %shard_map.120 = (bf16[32,2304]{1,0:T(8,128)(2,1)}, bf16[32,2304]{1,0:T(8,128)(2,1)}) custom-call(s32[1,18]{1,0:T(1,128)S(4)} %get-tuple-element.40.partner_ref.refs_0_, s32[1,2304]{1,0:T(1,128)S(1)} %get-tuple-element.41.turn_ref.refs_1_, f32[9,32,128]{2,1,0:T(8,128)S(1)} %get-tuple-element.69.refs_2_, ...), custom_call_target="tpu_custom_call" | custom-call | tf_op jit(solution)/shard_map/pallas_call | solution.py:453
  (8 shorter events, 1.1 us)
Async XLA Ops:
  1.7 10.8 %collective-permute-start = (bf16[32,2304]{1,0:T(8,128)(2,1)S(1)}, bf16[32,2304]{1,0:T(8,128)(2,1)S(1)}, u32[]{:S(2)}, u32[]{:S(2)}) collective-permute-start(bf16[32,2304]{1,0:T(8,128)(2,1)S(1)} %add_convert_fusion.half_in_ref.own_ref), channel_id=1, source_target_pairs={{0,1},{1,0},{2,3},{3,2},{4,5},{5,4},{6,7},{7,6},{8,9},{9,8},{10,11... | collective-permute-start | bytes 442376 | tf_op jit(solution)/shard_map/ppermute | solution.py:396
  13.7 5.6 %collective-permute-start.2 = (f32[11,32,128]{2,1,0:T(8,128)S(1)}, f32[11,32,128]{2,1,0:T(8,128)S(1)}, u32[]{:S(2)}, u32[]{:S(2)}) collective-permute-start(f32[11,32,128]{2,1,0:T(8,128)S(1)} %shard_map.107.own_ref), channel_id=1, source_target_pairs={{0,1},{1,0},{2,4},{3,5},{4,2},{5,3},{6,8},{7,9},{8,6},{9,7},{10,12... | collective-permute-start | bytes 540680 | tf_op jit(solution)/shard_map/ppermute | solution.py:436
  15.1 2.7 %collective-permute-start.1 = (f32[10,32,128]{2,1,0:T(8,128)S(1)}, f32[10,32,128]{2,1,0:T(8,128)S(1)}, u32[]{:S(2)}, u32[]{:S(2)}) collective-permute-start(f32[10,32,128]{2,1,0:T(8,128)S(1)} %shard_map.105.own_ref), channel_id=1, source_target_pairs={{0,2},{2,0},{4,6},{6,4},{8,10},{10,8},{12,14},{14,12},{16,18},{18,... | collective-permute-start | bytes 491528 | tf_op jit(solution)/shard_map/ppermute | solution.py:436
  18.0 4.6 %collective-permute-start.3 = (bf16[9,32,128]{2,1,0:T(8,128)(2,1)S(1)}, bf16[9,32,128]{2,1,0:T(8,128)(2,1)S(1)}, u32[]{:S(2)}, u32[]{:S(2)}) collective-permute-start(bf16[9,32,128]{2,1,0:T(8,128)(2,1)S(1)} %get-tuple-element.53.own0_ref), channel_id=1, source_target_pairs={{0,1},{1,0},{2,3},{3,2},{4,5},{5,4},{6,7},{7,6},{8,9},{9,8},{10,11... | collective-permute-start | bytes 221192 | tf_op jit(solution)/shard_map/ppermute | solution.py:417
  19.5 4.7 %collective-permute-start.4 = (bf16[9,32,128]{2,1,0:T(8,128)(2,1)S(1)}, bf16[9,32,128]{2,1,0:T(8,128)(2,1)S(1)}, u32[]{:S(2)}, u32[]{:S(2)}) collective-permute-start(bf16[9,32,128]{2,1,0:T(8,128)(2,1)S(1)} %get-tuple-element.55.own1_ref), channel_id=1, source_target_pairs={{0,1},{1,0},{2,3},{3,2},{4,5},{5,4},{6,7},{7,6},{8,9},{9,8},{10,11... | collective-permute-start | bytes 221192 | tf_op jit(solution)/shard_map/ppermute | solution.py:417
  25.3 6.1 %collective-permute-start.6 = (s16[11,32,128]{2,1,0:T(8,128)(2,1)S(1)}, s16[11,32,128]{2,1,0:T(8,128)(2,1)S(1)}, u32[]{:S(2)}, u32[]{:S(2)}) collective-permute-start(s16[11,32,128]{2,1,0:T(8,128)(2,1)S(1)} %get-tuple-element.64), channel_id=1, source_target_pairs={{0,1},{1,0},{2,4},{3,5},{4,2},{5,3},{6,8},{7,9},{8,6},{9,7},{10,12... | collective-permute-start | bytes 270344 | tf_op jit(solution)/shard_map/ppermute | solution.py:436
  27.3 3.1 %collective-permute-start.5 = (s16[10,32,128]{2,1,0:T(8,128)(2,1)S(1)}, s16[10,32,128]{2,1,0:T(8,128)(2,1)S(1)}, u32[]{:S(2)}, u32[]{:S(2)}) collective-permute-start(s16[10,32,128]{2,1,0:T(8,128)(2,1)S(1)} %get-tuple-element.58), channel_id=1, source_target_pairs={{0,2},{2,0},{4,6},{6,4},{8,10},{10,8},{12,14},{14,12},{16,18},{18,... | collective-permute-start | bytes 245768 | tf_op jit(solution)/shard_map/ppermute | solution.py:436
  30.6 5.2 %collective-permute-start.7 = (bf16[9,32,128]{2,1,0:T(8,128)(2,1)S(1)}, bf16[9,32,128]{2,1,0:T(8,128)(2,1)S(1)}, u32[]{:S(2)}, u32[]{:S(2)}) collective-permute-start(bf16[9,32,128]{2,1,0:T(8,128)(2,1)S(1)} %get-tuple-element.61.own0_ref), channel_id=1, source_target_pairs={{0,1},{1,0},{2,3},{3,2},{4,5},{5,4},{6,7},{7,6},{8,9},{9,8},{10,11... | collective-permute-start | bytes 221192 | tf_op jit(solution)/shard_map/ppermute | solution.py:417
  31.6 5.1 %collective-permute-start.8 = (bf16[9,32,128]{2,1,0:T(8,128)(2,1)S(1)}, bf16[9,32,128]{2,1,0:T(8,128)(2,1)S(1)}, u32[]{:S(2)}, u32[]{:S(2)}) collective-permute-start(bf16[9,32,128]{2,1,0:T(8,128)(2,1)S(1)} %get-tuple-element.67.own1_ref), channel_id=1, source_target_pairs={{0,1},{1,0},{2,3},{3,2},{4,5},{5,4},{6,7},{7,6},{8,9},{9,8},{10,11... | collective-permute-start | bytes 221192 | tf_op jit(solution)/shard_map/ppermute | solution.py:417
  37.8 4.6 %collective-permute-start.9 = (s16[11,32,128]{2,1,0:T(8,128)(2,1)S(1)}, s16[11,32,128]{2,1,0:T(8,128)(2,1)S(1)}, u32[]{:S(2)}, u32[]{:S(2)}) collective-permute-start(s16[11,32,128]{2,1,0:T(8,128)(2,1)S(1)} %get-tuple-element.70), channel_id=1, source_target_pairs={{0,1},{1,0},{2,4},{3,5},{4,2},{5,3},{6,8},{7,9},{8,6},{9,7},{10,12... | collective-permute-start | bytes 270344 | tf_op jit(solution)/shard_map/ppermute | solution.py:436
  39.9 1.6 %collective-permute-start.10 = (s16[10,32,128]{2,1,0:T(8,128)(2,1)S(1)}, s16[10,32,128]{2,1,0:T(8,128)(2,1)S(1)}, u32[]{:S(2)}, u32[]{:S(2)}) collective-permute-start(s16[10,32,128]{2,1,0:T(8,128)(2,1)S(1)} %get-tuple-element.73), channel_id=1, source_target_pairs={{0,2},{2,0},{4,6},{6,4},{8,10},{10,8},{12,14},{14,12},{16,18},{18,... | collective-permute-start | bytes 245768 | tf_op jit(solution)/shard_map/ppermute | solution.py:436

commit v3 on v2

--- a/solution.py
+++ b/solution.py
@@ -36,29 +36,30 @@
     faces, _, stored = columns_ref.shape
     group = faces // 2
     near, far, mine = position(group)
-    own = mine * faces
-    partner = (1 - mine) * faces + near
-
-    def sort_row(face, _):
-        in_far = (face >= far) & (face < far + group)
-        width = jnp.where(in_far, group, 0)
-        columns = [columns_ref[face, 0, j] for j in range(stored)]
-        owned = [(column >= own) & (column < own + faces) for column in columns]
-        count = sum(jnp.where(here, 1, 0) for here in owned)
-        front, middle, back = jnp.int32(0), count, jnp.int32(stored - 1)
-        for j in range(stored):
-            soon = (columns[j] >= partner) & (columns[j] < partner + width)
-            place = jnp.where(owned[j], front, jnp.where(soon, middle, back))
-            order_ref[face, 0, place] = j
-            sorted_ref[face, 0, place] = columns[j]
-            front = jnp.where(owned[j], front + 1, front)
-            middle = jnp.where(soon, middle + 1, middle)
-            back = jnp.where(owned[j] | soon, back, back - 1)
-        own_ref[0, face] = count
-        ready_ref[0, face] = middle
-        return 0
-
-    lax.fori_loop(0, faces, sort_row, 0)
+    columns = jnp.concatenate([columns_ref[face] for face in range(faces)], axis=0).astype(jnp.float32)
+    row = lax.broadcasted_iota(jnp.int32, columns.shape, 0)
+    lane = lax.broadcasted_iota(jnp.int32, columns.shape, 1).astype(jnp.float32)
+    own = (mine * faces).astype(jnp.float32)
+    partner = ((1 - mine) * faces + near).astype(jnp.float32)
+    width = jnp.where((row >= far) & (row < far + group), group, 0).astype(jnp.float32)
+    count = jnp.sum(jnp.where((columns >= own) & (columns < own + faces), 1.0, 0.0), axis=1, keepdims=True)
+    front = jnp.zeros_like(columns)
+    middle = count + front
+    back = front + (stored - 1.0)
+    order, placed = front, front
+    for j in range(stored):
+        column = jnp.broadcast_to(columns[:, j : j + 1], columns.shape)
+        owned = (column >= own) & (column < own + faces)
+        soon = (column >= partner) & (column < partner + width)
+        there = lane == jnp.where(owned, front, jnp.where(soon, middle, back))
+        order = jnp.where(there, float(j), order)
+        placed = jnp.where(there, column, placed)
+        front = front + jnp.where(owned, 1.0, 0.0)
+        middle = middle + jnp.where(soon, 1.0, 0.0)
+        back = back - jnp.where(owned | soon, 0.0, 1.0)
+    for ref, values in ((order_ref, order), (sorted_ref, placed), (own_ref, front[:, :1]), (ready_ref, middle[:, :1])):
+        for face in range(faces):
+            ref[face] = values[face : face + 1].astype(jnp.int32)
 
 
 def block_products(parts):
@@ -86,7 +87,7 @@
 
 
 def early_entries(half_ref, order_ref, sorted_ref, ready_ref, compliance_ref, count, face):
-    ready, none = ready_ref[0, face], half_ref.shape[0] - 1
+    ready, none = ready_ref[face, 0, 0], half_ref.shape[0] - 1
     return [
         (half_ref[jnp.where(slot < ready, sorted_ref[face, 0, slot], none)], compliance_ref[face, order_ref[face, 0, slot]])
         for slot in range(count)
@@ -95,7 +96,8 @@
 
 def fetch(blocks_hbm, load_hbm, motion_hbm, stress_hbm, stiff_hbm, record_hbm, turn_hbm, columns_hbm, partner_hbm, half_in_ref,
           blocks_ref, load_ref, motion_ref, stress_ref, stiff_ref, record_ref, turn_ref, partner_ref,
-          order_ref, sorted_ref, own_ref, ready_ref, early0_ref, early1_ref, columns_ref, half_ref, sems):
+          order_ref, sorted_ref, own_ref, ready_ref, early0_ref, early1_ref,
+          columns_ref, order_vmem, sorted_vmem, own_vmem, ready_vmem, half_ref, sems):
     group, _, extent = early0_ref.shape
     faces = 2 * group
     *starts, mine = position(group)
@@ -120,7 +122,15 @@
     none = half_ref.shape[0] - 1
     half_ref[none] = jnp.zeros_like(half_ref[none])
     columns_copy.wait()
-    sort_blocks(columns_ref, order_ref, sorted_ref, own_ref, ready_ref)
+    tables = ((order_vmem, order_ref), (sorted_vmem, sorted_ref), (own_vmem, own_ref), (ready_vmem, ready_ref))
+    sort_blocks(columns_ref, *(source for source, _ in tables))
+    tables = [
+        pltpu.make_async_copy(source, target, sems.at[1 + faces + len(pairs) + n]) for n, (source, target) in enumerate(tables)
+    ]
+    for copy in tables:
+        copy.start()
+    for copy in tables:
+        copy.wait()
     entries = functools.partial(early_entries, half_ref, order_ref, sorted_ref, own_ref, blocks_ref, FIRST)
     for side, out_ref in ((1, early1_ref), (0, early0_ref)):
         for index in range(0, group, 2):
@@ -165,14 +175,14 @@
         out_ref[index] -= 2.0 * block_products([[entry(first + index, slot)]])[0]
         return index
 
-    least = ready_ref[0, first]
+    least = ready_ref[first, 0, 0]
     for index in range(1, group):
-        least = jnp.minimum(least, ready_ref[0, first + index])
+        least = jnp.minimum(least, ready_ref[first + index, 0, 0])
 
     @pl.when(least < done)
     def _():
         for index in range(group):
-            lax.fori_loop(ready_ref[0, first + index], done, missed, index)
+            lax.fori_loop(ready_ref[first + index, 0, 0], done, missed, index)
 
 
 def first_section(side, order_ref, sorted_ref, own_count_ref, compliance_ref, own_ref, other_ref, motion_ref, stress_ref,
@@ -394,13 +404,14 @@
     in_hbm = functools.partial(pltpu.with_memory_space_constraint, memory_space=pltpu.HBM)
     own = (start_traction[0].astype(jnp.float32) + starting_motion[0].astype(jnp.float32)).astype(jnp.bfloat16)
     other = lax.ppermute(own, "row", swap)
-    table, counts = pltpu.SMEM((faces, 1, stored), jnp.int32), pltpu.SMEM((1, faces), jnp.int32)
+    table, counts = pltpu.SMEM((faces, 1, stored), jnp.int32), pltpu.SMEM((faces, 1, 1), jnp.int32)
+    tables = [pltpu.VMEM((faces, 1, width), jnp.int32) for width in (stored, stored, stored, 1, 1)]
     blocks, load, motion, stress, stiff, record, turn, *tables, first0, first1 = call(
         fetch, [HBM] * 9 + [VMEM],
         (pltpu.VMEM((faces, stored, extent, extent), jnp.bfloat16), bf16(*flat), bf16(*flat), bf16(*flat),
          f32(1, faces * extent), f32(1, faces * extent), s32(1, faces * extent),
-         counts, table, table, counts, counts, f32(*part), f32(*part)),
-        [table, pltpu.VMEM((rows * faces + 1, times, extent), jnp.bfloat16), pltpu.SemaphoreType.DMA((8 + faces,))],
+         pltpu.SMEM((1, faces), jnp.int32), table, table, counts, counts, f32(*part), f32(*part)),
+        tables + [pltpu.VMEM((rows * faces + 1, times, extent), jnp.bfloat16), pltpu.SemaphoreType.DMA((12 + faces,))],
         block_bytes, (VMEM,) * 7 + (SMEM,) * 5 + (VMEM,) * 2,
     )(
         in_hbm(compliance[0]), in_hbm(load_response[0]), in_hbm(starting_motion[0]), in_hbm(start_traction[0]),

time: 43.6 us -> 41.3 us (0.947)
  Pallas kernels: 20.5 us -> 18.2 us
    pallas_call x1, Pallas kernels: 7.77 us -> 5.49 us  [shards(): call(fetch, [HBM] * 9 + [VMEM], (pltpu.VMEM((faces, stored, extent, exten...]
  transfers between devices with their start and end apart: 11 -> 11, of which waited for: 8 -> 8; matrix products, arithmetic and copies ran while one was open for 0% -> 0% of each run, Pallas kernels for 38% -> 34%
where the time goes in v3:
time: 41.3 us; the launch traced here: 41.1 us
  Pallas kernels  18.2 us (44%)
  starting transfers between devices  13 us (31%)
  waiting for transfers between devices  8.02 us (19%)
  other arithmetic  1.02 us (2%)
  between operations  0.77 us (2%)
    ppermute x6, starting transfers between devices, shards(): mates[side] = lax.ppermute(sent, axes, pairs)  6.15 us
    pallas_call x1, Pallas kernels, shards(): call(fetch, [HBM] * 9 + [VMEM], (pltpu.VMEM((faces, stored, extent, exten...  5.49 us
    pallas_call x4, Pallas kernels, shards(): call(functools.partial(linear_section, side), [SMEM] * 3 + [VMEM] * 8, (f...  4.72 us
    ppermute x4, waiting for transfers between devices, shards(): other = [lax.ppermute(half[side], 'row', swap) for side in range(2)]  4.25 us
    ppermute x4, starting transfers between devices, shards(): other = [lax.ppermute(half[side], 'row', swap) for side in range(2)]  3.89 us
    ppermute x6, waiting for transfers between devices, shards(): mates[side] = lax.ppermute(sent, axes, pairs)  3.77 us
    pallas_call x4, Pallas kernels, shards(): call(functools.partial(early_products, side), [SMEM] * 3 + [VMEM] * (3 +...  3.31 us
    ppermute x1, starting transfers between devices, shards(): other = lax.ppermute(own, 'row', swap)  3 us
  transfers between devices with their start and end apart: 11, of which 8 were waited for; matrix products, arithmetic and copies ran while one was open for 0% of the time, Pallas kernels for 34%

profile of v3, /device:TPU:0, one launch (start us, length us, event | category | flops | bytes accessed | tf_op | source)
XLA Modules:
  0.0 41.1 jit_solution(18310356151782112617)
XLA Ops:
  0.6 1.0 %add_convert_fusion.half_in_ref.own_ref = bf16[32,2304]{1,0:T(8,128)(2,1)S(1)} fusion(bf16[1,32,2304]{2,1,0:T(8,128)(2,1)} %param.13, bf16[1,32,2304]{2,1,0:T(8,128)(2,1)} %param.12), kind=kLoop, calls=%fused_computation | loop fusion | flops 294912 | bytes 442368 | tf_op jit(solution)/shard_map/convert_element_type | solution.py:405
  1.7 3.0 %collective-permute-start = (bf16[32,2304]{1,0:T(8,128)(2,1)S(1)}, bf16[32,2304]{1,0:T(8,128)(2,1)S(1)}, u32[]{:S(2)}, u32[]{:S(2)}) collective-permute-start(bf16[32,2304]{1,0:T(8,128)(2,1)S(1)} %add_convert_fusion.half_in_ref.own_ref), channel_id=1, source_target_pairs={{0,1},{1,0},{2,3},{3,2},{4,5},{5,4},{6,7},{7,6},{8,9},{9,8},{10,11... | collective-permute-start | bytes 442376 | tf_op jit(solution)/shard_map/ppermute | solution.py:406
  4.7 5.5 %shard_map.104 = (bf16[18,18,128,128]{3,2,1,0:T(8,128)(2,1)S(1)}, bf16[32,2304]{1,0:T(8,128)(2,1)S(1)}, bf16[32,2304]{1,0:T(8,128)(2,1)S(1)}, bf16[32,2304]{1,0:...) custom-call(bf16[18,18,128,128]{3,2,1,0:T(8,128)(2,1)} %bitcast.10, ...), custom_call_target="tpu_custom_call" | custom-call | flops 10616832 | bytes 10616832 | tf_op jit(solution)/shard_map/pallas_call | solution.py:409
  10.2 1.3 %shard_map.107.own_ref = f32[11,32,128]{2,1,0:T(8,128)S(1)} custom-call(s32[18,1,18]{2,1,0:T(1,128)S(4)} %get-tuple-element.42.order_ref, s32[18,1,18]{2,1,0:T(1,128)S(4)} %get-tuple-element.43.sorted_ref, s32[18,1,1]{2,1,0:T(1,128)S(4)} %get-tuple-element.46.own_count_ref, bf16[18,18,128,128]{3,2,1,0:T(8,128)(2,1)S(1)} %get-tuple-element.45.compliance_ref, ...), custom_call_target="tpu_custom_call" | custom-call | flops 21233664 | bytes 21233664 | tf_op jit(solution)/shard_map/pallas_call | solution.py:437
  11.6 1.2 %shard_map.105.own_ref = f32[10,32,128]{2,1,0:T(8,128)S(1)} custom-call(s32[18,1,18]{2,1,0:T(1,128)S(4)} %get-tuple-element.42.order_ref, s32[18,1,18]{2,1,0:T(1,128)S(4)} %get-tuple-element.43.sorted_ref, s32[18,1,1]{2,1,0:T(1,128)S(4)} %get-tuple-element.46.own_count_ref, bf16[18,18,128,128]{3,2,1,0:T(8,128)(2,1)S(1)} %get-tuple-element.45.compliance_ref, ...), custom_call_target="tpu_custom_call" | custom-call | flops 21233664 | bytes 21233664 | tf_op jit(solution)/shard_map/pallas_call | solution.py:437
  12.8 1.6 %collective-permute-start.1 = (f32[10,32,128]{2,1,0:T(8,128)S(1)}, f32[10,32,128]{2,1,0:T(8,128)S(1)}, u32[]{:S(2)}, u32[]{:S(2)}) collective-permute-start(f32[10,32,128]{2,1,0:T(8,128)S(1)} %shard_map.105.own_ref), channel_id=1, source_target_pairs={{0,2},{2,0},{4,6},{6,4},{8,10},{10,8},{12,14},{14,12},{16,18},{18,... | collective-permute-start | bytes 491528 | tf_op jit(solution)/shard_map/ppermute | solution.py:447
  14.4 1.0 %collective-permute-done.1.mate_ref = f32[10,32,128]{2,1,0:T(8,128)S(1)} collective-permute-done((f32[10,32,128]{2,1,0:T(8,128)S(1)}, f32[10,32,128]{2,1,0:T(8,128)S(1)}, u32[]{:S(2)}, u32[]{:S(2)}) %collective-permute-start.1) | collective-permute-done | bytes 163872 | tf_op jit(solution)/shard_map/ppermute | solution.py:447
  15.7 0.8 %collective-permute-start.3 = (bf16[9,32,128]{2,1,0:T(8,128)(2,1)S(1)}, bf16[9,32,128]{2,1,0:T(8,128)(2,1)S(1)}, u32[]{:S(2)}, u32[]{:S(2)}) collective-permute-start(bf16[9,32,128]{2,1,0:T(8,128)(2,1)S(1)} %get-tuple-element.53.own0_ref), channel_id=1, source_target_pairs={{0,1},{1,0},{2,3},{3,2},{4,5},{5,4},{6,7},{7,6},{8,9},{9,8},{10,11... | collective-permute-start | bytes 221192 | tf_op jit(solution)/shard_map/ppermute | solution.py:428
  16.5 0.4 %collective-permute-done.2.mate_ref = f32[11,32,128]{2,1,0:T(8,128)S(1)} collective-permute-done((f32[11,32,128]{2,1,0:T(8,128)S(1)}, f32[11,32,128]{2,1,0:T(8,128)S(1)}, u32[]{:S(2)}, u32[]{:S(2)}) %collective-permute-start.2) | collective-permute-done | bytes 180256 | tf_op jit(solution)/shard_map/ppermute | solution.py:447
  17.0 0.3 shard_map.108
  17.3 0.9 %collective-permute-start.4 = (bf16[9,32,128]{2,1,0:T(8,128)(2,1)S(1)}, bf16[9,32,128]{2,1,0:T(8,128)(2,1)S(1)}, u32[]{:S(2)}, u32[]{:S(2)}) collective-permute-start(bf16[9,32,128]{2,1,0:T(8,128)(2,1)S(1)} %get-tuple-element.55.own1_ref), channel_id=1, source_target_pairs={{0,1},{1,0},{2,3},{3,2},{4,5},{5,4},{6,7},{7,6},{8,9},{9,8},{10,11... | collective-permute-start | bytes 221192 | tf_op jit(solution)/shard_map/ppermute | solution.py:428
  18.2 0.7 %shard_map.109.early_ref.refs_1_ = f32[9,32,128]{2,1,0:T(8,128)S(1)} custom-call(s32[18,1,18]{2,1,0:T(1,128)S(4)} %get-tuple-element.42.order_ref, s32[18,1,18]{2,1,0:T(1,128)S(4)} %get-tuple-element.43.sorted_ref, s32[18,1,1]{2,1,0:T(1,128)S(4)} %get-tuple-element.44.ready_ref, bf16[18,18,128,128]{3,2,1,0:T(8,128)(2,1)S(1)} %get-tuple-element.45.compliance_ref, ...), custom_call_target="tpu_custom_call" | custom-call | flops 10616832 | bytes 10616832 | tf_op jit(solution)/shard_map/pallas_call | solution.py:431
  18.8 1.5 %collective-permute-done.3.other0_ref.refs_0_ = bf16[9,32,128]{2,1,0:T(8,128)(2,1)S(1)} collective-permute-done((bf16[9,32,128]{2,1,0:T(8,128)(2,1)S(1)}, bf16[9,32,128]{2,1,0:T(8,128)(2,1)S(1)}, u32[]{:S(2)}, u32[]{:S(2)}) %collective-permute-start.3) | collective-permute-done | bytes 73760 | tf_op jit(solution)/shard_map/ppermute | solution.py:428
  20.3 1.0 %shard_map.112.early_ref = f32[9,32,128]{2,1,0:T(8,128)S(1)} custom-call(s32[18,1,18]{2,1,0:T(1,128)S(4)} %get-tuple-element.42.order_ref, s32[18,1,18]{2,1,0:T(1,128)S(4)} %get-tuple-element.43.sorted_ref, s32[18,1,1]{2,1,0:T(1,128)S(4)} %get-tuple-element.44.ready_ref, bf16[18,18,128,128]{3,2,1,0:T(8,128)(2,1)S(1)} %get-tuple-element.45.compliance_ref, ...), custom_call_target="tpu_custom_call" | custom-call | flops 10616832 | bytes 10616832 | tf_op jit(solution)/shard_map/pallas_call | solution.py:431
  21.3 0.7 %collective-permute-done.4.other1_ref = bf16[9,32,128]{2,1,0:T(8,128)(2,1)S(1)} collective-permute-done((bf16[9,32,128]{2,1,0:T(8,128)(2,1)S(1)}, bf16[9,32,128]{2,1,0:T(8,128)(2,1)S(1)}, u32[]{:S(2)}, u32[]{:S(2)}) %collective-permute-start.4) | collective-permute-done | bytes 73760 | tf_op jit(solution)/shard_map/ppermute | solution.py:428
  22.0 1.0 %shard_map.113 = (f32[9,32,128]{2,1,0:T(8,128)S(1)}, s16[11,32,128]{2,1,0:T(8,128)(2,1)S(1)}) custom-call(s32[18,1,18]{2,1,0:T(1,128)S(4)} %get-tuple-element.42.order_ref, s32[18,1,18]{2,1,0:T(1,128)S(4)} %get-tuple-element.43.sorted_ref, s32[18,1,1]{2,1,0:T(1,128)S(4)} %get-tuple-element.44.ready_ref, ...), custom_call_target="tpu_custom_call" | custom-call | flops 21233664 | bytes 21233664 | tf_op jit(solution)/shard_map/pallas_call | solution.py:442
  23.0 0.6 %collective-permute-start.6 = (s16[11,32,128]{2,1,0:T(8,128)(2,1)S(1)}, s16[11,32,128]{2,1,0:T(8,128)(2,1)S(1)}, u32[]{:S(2)}, u32[]{:S(2)}) collective-permute-start(s16[11,32,128]{2,1,0:T(8,128)(2,1)S(1)} %get-tuple-element.64), channel_id=1, source_target_pairs={{0,1},{1,0},{2,4},{3,5},{4,2},{5,3},{6,8},{7,9},{8,6},{9,7},{10,12... | collective-permute-start | bytes 270344 | tf_op jit(solution)/shard_map/ppermute | solution.py:447
  23.6 1.4 %shard_map.110 = (f32[9,32,128]{2,1,0:T(8,128)S(1)}, s16[10,32,128]{2,1,0:T(8,128)(2,1)S(1)}) custom-call(s32[18,1,18]{2,1,0:T(1,128)S(4)} %get-tuple-element.42.order_ref, s32[18,1,18]{2,1,0:T(1,128)S(4)} %get-tuple-element.43.sorted_ref, s32[18,1,1]{2,1,0:T(1,128)S(4)} %get-tuple-element.44.ready_ref, ...), custom_call_target="tpu_custom_call" | custom-call | flops 21233664 | bytes 21233664 | tf_op jit(solution)/shard_map/pallas_call | solution.py:442
  25.0 2.2 %collective-permute-start.5 = (s16[10,32,128]{2,1,0:T(8,128)(2,1)S(1)}, s16[10,32,128]{2,1,0:T(8,128)(2,1)S(1)}, u32[]{:S(2)}, u32[]{:S(2)}) collective-permute-start(s16[10,32,128]{2,1,0:T(8,128)(2,1)S(1)} %get-tuple-element.58), channel_id=1, source_target_pairs={{0,2},{2,0},{4,6},{6,4},{8,10},{10,8},{12,14},{14,12},{16,18},{18,... | collective-permute-start | bytes 245768 | tf_op jit(solution)/shard_map/ppermute | solution.py:447
  27.2 0.9 %collective-permute-done.5.refs_3_ = s16[10,32,128]{2,1,0:T(8,128)(2,1)S(1)} collective-permute-done((s16[10,32,128]{2,1,0:T(8,128)(2,1)S(1)}, s16[10,32,128]{2,1,0:T(8,128)(2,1)S(1)}, u32[]{:S(2)}, u32[]{:S(2)}) %collective-permute-start.5) | collective-permute-done | bytes 81952 | tf_op jit(solution)/shard_map/ppermute | solution.py:447
  28.3 0.8 %collective-permute-start.7 = (bf16[9,32,128]{2,1,0:T(8,128)(2,1)S(1)}, bf16[9,32,128]{2,1,0:T(8,128)(2,1)S(1)}, u32[]{:S(2)}, u32[]{:S(2)}) collective-permute-start(bf16[9,32,128]{2,1,0:T(8,128)(2,1)S(1)} %get-tuple-element.61.own0_ref), channel_id=1, source_target_pairs={{0,1},{1,0},{2,3},{3,2},{4,5},{5,4},{6,7},{7,6},{8,9},{9,8},{10,11... | collective-permute-start | bytes 221192 | tf_op jit(solution)/shard_map/ppermute | solution.py:428
  29.4 1.4 %collective-permute-start.8 = (bf16[9,32,128]{2,1,0:T(8,128)(2,1)S(1)}, bf16[9,32,128]{2,1,0:T(8,128)(2,1)S(1)}, u32[]{:S(2)}, u32[]{:S(2)}) collective-permute-start(bf16[9,32,128]{2,1,0:T(8,128)(2,1)S(1)} %get-tuple-element.67.own1_ref), channel_id=1, source_target_pairs={{0,1},{1,0},{2,3},{3,2},{4,5},{5,4},{6,7},{7,6},{8,9},{9,8},{10,11... | collective-permute-start | bytes 221192 | tf_op jit(solution)/shard_map/ppermute | solution.py:428
  30.8 0.7 %shard_map.115.refs_1_.early_ref = f32[9,32,128]{2,1,0:T(8,128)S(1)} custom-call(s32[18,1,18]{2,1,0:T(1,128)S(4)} %get-tuple-element.42.order_ref, s32[18,1,18]{2,1,0:T(1,128)S(4)} %get-tuple-element.43.sorted_ref, s32[18,1,1]{2,1,0:T(1,128)S(4)} %get-tuple-element.44.ready_ref, bf16[18,18,128,128]{3,2,1,0:T(8,128)(2,1)S(1)} %get-tuple-element.45.compliance_ref, ...), custom_call_target="tpu_custom_call" | custom-call | flops 10616832 | bytes 10616832 | tf_op jit(solution)/shard_map/pallas_call | solution.py:431
  31.4 2.1 %collective-permute-done.7.refs_0_.other0_ref = bf16[9,32,128]{2,1,0:T(8,128)(2,1)S(1)} collective-permute-done((bf16[9,32,128]{2,1,0:T(8,128)(2,1)S(1)}, bf16[9,32,128]{2,1,0:T(8,128)(2,1)S(1)}, u32[]{:S(2)}, u32[]{:S(2)}) %collective-permute-start.7) | collective-permute-done | bytes 73760 | tf_op jit(solution)/shard_map/ppermute | solution.py:428
  33.5 1.0 %shard_map.116.early_ref = f32[9,32,128]{2,1,0:T(8,128)S(1)} custom-call(s32[18,1,18]{2,1,0:T(1,128)S(4)} %get-tuple-element.42.order_ref, s32[18,1,18]{2,1,0:T(1,128)S(4)} %get-tuple-element.43.sorted_ref, s32[18,1,1]{2,1,0:T(1,128)S(4)} %get-tuple-element.44.ready_ref, bf16[18,18,128,128]{3,2,1,0:T(8,128)(2,1)S(1)} %get-tuple-element.45.compliance_ref, ...), custom_call_target="tpu_custom_call" | custom-call | flops 10616832 | bytes 10616832 | tf_op jit(solution)/shard_map/pallas_call | solution.py:431
  34.5 1.0 %shard_map.117 = (f32[9,32,128]{2,1,0:T(8,128)S(1)}, s16[11,32,128]{2,1,0:T(8,128)(2,1)S(1)}) custom-call(s32[18,1,18]{2,1,0:T(1,128)S(4)} %get-tuple-element.42.order_ref, s32[18,1,18]{2,1,0:T(1,128)S(4)} %get-tuple-element.43.sorted_ref, s32[18,1,1]{2,1,0:T(1,128)S(4)} %get-tuple-element.44.ready_ref, ...), custom_call_target="tpu_custom_call" | custom-call | flops 21233664 | bytes 21233664 | tf_op jit(solution)/shard_map/pallas_call | solution.py:442
  35.5 0.8 %collective-permute-start.9 = (s16[11,32,128]{2,1,0:T(8,128)(2,1)S(1)}, s16[11,32,128]{2,1,0:T(8,128)(2,1)S(1)}, u32[]{:S(2)}, u32[]{:S(2)}) collective-permute-start(s16[11,32,128]{2,1,0:T(8,128)(2,1)S(1)} %get-tuple-element.70), channel_id=1, source_target_pairs={{0,1},{1,0},{2,4},{3,5},{4,2},{5,3},{6,8},{7,9},{8,6},{9,7},{10,12... | collective-permute-start | bytes 270344 | tf_op jit(solution)/shard_map/ppermute | solution.py:447
  36.3 1.4 %shard_map.118 = (f32[9,32,128]{2,1,0:T(8,128)S(1)}, s16[10,32,128]{2,1,0:T(8,128)(2,1)S(1)}) custom-call(s32[18,1,18]{2,1,0:T(1,128)S(4)} %get-tuple-element.42.order_ref, s32[18,1,18]{2,1,0:T(1,128)S(4)} %get-tuple-element.43.sorted_ref, s32[18,1,1]{2,1,0:T(1,128)S(4)} %get-tuple-element.44.ready_ref, ...), custom_call_target="tpu_custom_call" | custom-call | flops 21233664 | bytes 21233664 | tf_op jit(solution)/shard_map/pallas_call | solution.py:442
  37.7 0.8 %collective-permute-start.10 = (s16[10,32,128]{2,1,0:T(8,128)(2,1)S(1)}, s16[10,32,128]{2,1,0:T(8,128)(2,1)S(1)}, u32[]{:S(2)}, u32[]{:S(2)}) collective-permute-start(s16[10,32,128]{2,1,0:T(8,128)(2,1)S(1)} %get-tuple-element.73), channel_id=1, source_target_pairs={{0,2},{2,0},{4,6},{6,4},{8,10},{10,8},{12,14},{14,12},{16,18},{18,... | collective-permute-start | bytes 245768 | tf_op jit(solution)/shard_map/ppermute | solution.py:447
  38.5 0.9 %collective-permute-done.10.refs_3_ = s16[10,32,128]{2,1,0:T(8,128)(2,1)S(1)} collective-permute-done((s16[10,32,128]{2,1,0:T(8,128)(2,1)S(1)}, s16[10,32,128]{2,1,0:T(8,128)(2,1)S(1)}, u32[]{:S(2)}, u32[]{:S(2)}) %collective-permute-start.10) | collective-permute-done | bytes 81952 | tf_op jit(solution)/shard_map/ppermute | solution.py:447
  39.7 0.4 %collective-permute-done.9.refs_3_ = s16[11,32,128]{2,1,0:T(8,128)(2,1)S(1)} collective-permute-done((s16[11,32,128]{2,1,0:T(8,128)(2,1)S(1)}, s16[11,32,128]{2,1,0:T(8,128)(2,1)S(1)}, u32[]{:S(2)}, u32[]{:S(2)}) %collective-permute-start.9) | collective-permute-done | bytes 90144 | tf_op jit(solution)/shard_map/ppermute | solution.py:447
  40.1 1.0 %shard_map.120 = (bf16[32,2304]{1,0:T(8,128)(2,1)}, bf16[32,2304]{1,0:T(8,128)(2,1)}) custom-call(s32[1,18]{1,0:T(1,128)S(4)} %get-tuple-element.40.partner_ref.refs_0_, s32[1,2304]{1,0:T(1,128)S(1)} %get-tuple-element.41.turn_ref.refs_1_, f32[9,32,128]{2,1,0:T(8,128)S(1)} %get-tuple-element.69.refs_2_, ...), custom_call_target="tpu_custom_call" | custom-call | tf_op jit(solution)/shard_map/pallas_call | solution.py:464
  (8 shorter events, 1.2 us)
Async XLA Ops:
  1.7 8.5 %collective-permute-start = (bf16[32,2304]{1,0:T(8,128)(2,1)S(1)}, bf16[32,2304]{1,0:T(8,128)(2,1)S(1)}, u32[]{:S(2)}, u32[]{:S(2)}) collective-permute-start(bf16[32,2304]{1,0:T(8,128)(2,1)S(1)} %add_convert_fusion.half_in_ref.own_ref), channel_id=1, source_target_pairs={{0,1},{1,0},{2,3},{3,2},{4,5},{5,4},{6,7},{7,6},{8,9},{9,8},{10,11... | collective-permute-start | bytes 442376 | tf_op jit(solution)/shard_map/ppermute | solution.py:406
  11.4 5.6 %collective-permute-start.2 = (f32[11,32,128]{2,1,0:T(8,128)S(1)}, f32[11,32,128]{2,1,0:T(8,128)S(1)}, u32[]{:S(2)}, u32[]{:S(2)}) collective-permute-start(f32[11,32,128]{2,1,0:T(8,128)S(1)} %shard_map.107.own_ref), channel_id=1, source_target_pairs={{0,1},{1,0},{2,4},{3,5},{4,2},{5,3},{6,8},{7,9},{8,6},{9,7},{10,12... | collective-permute-start | bytes 540680 | tf_op jit(solution)/shard_map/ppermute | solution.py:447
  12.8 2.7 %collective-permute-start.1 = (f32[10,32,128]{2,1,0:T(8,128)S(1)}, f32[10,32,128]{2,1,0:T(8,128)S(1)}, u32[]{:S(2)}, u32[]{:S(2)}) collective-permute-start(f32[10,32,128]{2,1,0:T(8,128)S(1)} %shard_map.105.own_ref), channel_id=1, source_target_pairs={{0,2},{2,0},{4,6},{6,4},{8,10},{10,8},{12,14},{14,12},{16,18},{18,... | collective-permute-start | bytes 491528 | tf_op jit(solution)/shard_map/ppermute | solution.py:447
  15.7 4.6 %collective-permute-start.3 = (bf16[9,32,128]{2,1,0:T(8,128)(2,1)S(1)}, bf16[9,32,128]{2,1,0:T(8,128)(2,1)S(1)}, u32[]{:S(2)}, u32[]{:S(2)}) collective-permute-start(bf16[9,32,128]{2,1,0:T(8,128)(2,1)S(1)} %get-tuple-element.53.own0_ref), channel_id=1, source_target_pairs={{0,1},{1,0},{2,3},{3,2},{4,5},{5,4},{6,7},{7,6},{8,9},{9,8},{10,11... | collective-permute-start | bytes 221192 | tf_op jit(solution)/shard_map/ppermute | solution.py:428
  17.3 4.8 %collective-permute-start.4 = (bf16[9,32,128]{2,1,0:T(8,128)(2,1)S(1)}, bf16[9,32,128]{2,1,0:T(8,128)(2,1)S(1)}, u32[]{:S(2)}, u32[]{:S(2)}) collective-permute-start(bf16[9,32,128]{2,1,0:T(8,128)(2,1)S(1)} %get-tuple-element.55.own1_ref), channel_id=1, source_target_pairs={{0,1},{1,0},{2,3},{3,2},{4,5},{5,4},{6,7},{7,6},{8,9},{9,8},{10,11... | collective-permute-start | bytes 221192 | tf_op jit(solution)/shard_map/ppermute | solution.py:428
  23.0 6.1 %collective-permute-start.6 = (s16[11,32,128]{2,1,0:T(8,128)(2,1)S(1)}, s16[11,32,128]{2,1,0:T(8,128)(2,1)S(1)}, u32[]{:S(2)}, u32[]{:S(2)}) collective-permute-start(s16[11,32,128]{2,1,0:T(8,128)(2,1)S(1)} %get-tuple-element.64), channel_id=1, source_target_pairs={{0,1},{1,0},{2,4},{3,5},{4,2},{5,3},{6,8},{7,9},{8,6},{9,7},{10,12... | collective-permute-start | bytes 270344 | tf_op jit(solution)/shard_map/ppermute | solution.py:447
  25.0 3.1 %collective-permute-start.5 = (s16[10,32,128]{2,1,0:T(8,128)(2,1)S(1)}, s16[10,32,128]{2,1,0:T(8,128)(2,1)S(1)}, u32[]{:S(2)}, u32[]{:S(2)}) collective-permute-start(s16[10,32,128]{2,1,0:T(8,128)(2,1)S(1)} %get-tuple-element.58), channel_id=1, source_target_pairs={{0,2},{2,0},{4,6},{6,4},{8,10},{10,8},{12,14},{14,12},{16,18},{18,... | collective-permute-start | bytes 245768 | tf_op jit(solution)/shard_map/ppermute | solution.py:447
  28.3 5.2 %collective-permute-start.7 = (bf16[9,32,128]{2,1,0:T(8,128)(2,1)S(1)}, bf16[9,32,128]{2,1,0:T(8,128)(2,1)S(1)}, u32[]{:S(2)}, u32[]{:S(2)}) collective-permute-start(bf16[9,32,128]{2,1,0:T(8,128)(2,1)S(1)} %get-tuple-element.61.own0_ref), channel_id=1, source_target_pairs={{0,1},{1,0},{2,3},{3,2},{4,5},{5,4},{6,7},{7,6},{8,9},{9,8},{10,11... | collective-permute-start | bytes 221192 | tf_op jit(solution)/shard_map/ppermute | solution.py:428
  29.4 5.1 %collective-permute-start.8 = (bf16[9,32,128]{2,1,0:T(8,128)(2,1)S(1)}, bf16[9,32,128]{2,1,0:T(8,128)(2,1)S(1)}, u32[]{:S(2)}, u32[]{:S(2)}) collective-permute-start(bf16[9,32,128]{2,1,0:T(8,128)(2,1)S(1)} %get-tuple-element.67.own1_ref), channel_id=1, source_target_pairs={{0,1},{1,0},{2,3},{3,2},{4,5},{5,4},{6,7},{7,6},{8,9},{9,8},{10,11... | collective-permute-start | bytes 221192 | tf_op jit(solution)/shard_map/ppermute | solution.py:428
  35.5 4.6 %collective-permute-start.9 = (s16[11,32,128]{2,1,0:T(8,128)(2,1)S(1)}, s16[11,32,128]{2,1,0:T(8,128)(2,1)S(1)}, u32[]{:S(2)}, u32[]{:S(2)}) collective-permute-start(s16[11,32,128]{2,1,0:T(8,128)(2,1)S(1)} %get-tuple-element.70), channel_id=1, source_target_pairs={{0,1},{1,0},{2,4},{3,5},{4,2},{5,3},{6,8},{7,9},{8,6},{9,7},{10,12... | collective-permute-start | bytes 270344 | tf_op jit(solution)/shard_map/ppermute | solution.py:447
  37.7 1.8 %collective-permute-start.10 = (s16[10,32,128]{2,1,0:T(8,128)(2,1)S(1)}, s16[10,32,128]{2,1,0:T(8,128)(2,1)S(1)}, u32[]{:S(2)}, u32[]{:S(2)}) collective-permute-start(s16[10,32,128]{2,1,0:T(8,128)(2,1)S(1)} %get-tuple-element.73), channel_id=1, source_target_pairs={{0,2},{2,0},{4,6},{6,4},{8,10},{10,8},{12,14},{14,12},{16,18},{18,... | collective-permute-start | bytes 245768 | tf_op jit(solution)/shard_map/ppermute | solution.py:447

commit v4 on v3

--- a/solution.py
+++ b/solution.py
@@ -11,7 +11,6 @@
 SUBLANES = 8
 LEAST = 2.0**-100
 EARLY = (6, 10)
-FIRST = 6
 VMEM_BYTES = 24 * 2**20
 
 ONSET_JUMP = 0.15
@@ -32,7 +31,7 @@
     return pl.ds(pl.multiple_of(face * extent, extent), extent)
 
 
-def sort_blocks(columns_ref, order_ref, sorted_ref, own_ref, ready_ref):
+def sort_blocks(columns_ref, order_ref, sorted_ref, ready_ref):
     faces, _, stored = columns_ref.shape
     group = faces // 2
     near, far, mine = position(group)
@@ -42,24 +41,40 @@
     own = (mine * faces).astype(jnp.float32)
     partner = ((1 - mine) * faces + near).astype(jnp.float32)
     width = jnp.where((row >= far) & (row < far + group), group, 0).astype(jnp.float32)
-    count = jnp.sum(jnp.where((columns >= own) & (columns < own + faces), 1.0, 0.0), axis=1, keepdims=True)
     front = jnp.zeros_like(columns)
-    middle = count + front
     back = front + (stored - 1.0)
     order, placed = front, front
     for j in range(stored):
         column = jnp.broadcast_to(columns[:, j : j + 1], columns.shape)
-        owned = (column >= own) & (column < own + faces)
-        soon = (column >= partner) & (column < partner + width)
-        there = lane == jnp.where(owned, front, jnp.where(soon, middle, back))
+        early = ((column >= own) & (column < own + faces)) | ((column >= partner) & (column < partner + width))
+        there = lane == jnp.where(early, front, back)
         order = jnp.where(there, float(j), order)
         placed = jnp.where(there, column, placed)
-        front = front + jnp.where(owned, 1.0, 0.0)
-        middle = middle + jnp.where(soon, 1.0, 0.0)
-        back = back - jnp.where(owned | soon, 0.0, 1.0)
-    for ref, values in ((order_ref, order), (sorted_ref, placed), (own_ref, front[:, :1]), (ready_ref, middle[:, :1])):
+        front = front + jnp.where(early, 1.0, 0.0)
+        back = back - jnp.where(early, 0.0, 1.0)
+    for ref, values in ((order_ref, order), (sorted_ref, placed), (ready_ref, front[:, :1])):
         for face in range(faces):
             ref[face] = values[face : face + 1].astype(jnp.int32)
+
+
+def fetch(blocks_hbm, load_hbm, motion_hbm, stress_hbm, stiff_hbm, record_hbm, turn_hbm, columns_hbm, partner_hbm,
+          blocks_ref, load_ref, motion_ref, stress_ref, stiff_ref, record_ref, turn_ref, partner_ref,
+          order_ref, sorted_ref, ready_ref, columns_ref, order_vmem, sorted_vmem, ready_vmem, sems):
+    pairs = [
+        (columns_hbm, columns_ref), (load_hbm, load_ref), (motion_hbm, motion_ref), (stress_hbm, stress_ref),
+        (stiff_hbm, stiff_ref), (record_hbm, record_ref), (turn_hbm, turn_ref), (partner_hbm, partner_ref),
+    ]
+    pairs += [(blocks_hbm.at[face], blocks_ref.at[face]) for face in range(blocks_hbm.shape[0])]
+    pairs += [(order_vmem, order_ref), (sorted_vmem, sorted_ref), (ready_vmem, ready_ref)]
+    copies = [pltpu.make_async_copy(source, target, sems.at[n]) for n, (source, target) in enumerate(pairs)]
+    for copy in copies[:-3]:
+        copy.start()
+    copies[0].wait()
+    sort_blocks(columns_ref, order_vmem, sorted_vmem, ready_vmem)
+    for copy in copies[-3:]:
+        copy.start()
+    for copy in copies[1:]:
+        copy.wait()
 
 
 def block_products(parts):
@@ -86,64 +101,6 @@
         finish(group - 1, sum(block_products([whole[:cut], whole[cut:]])))
 
 
-def early_entries(half_ref, order_ref, sorted_ref, ready_ref, compliance_ref, count, face):
-    ready, none = ready_ref[face, 0, 0], half_ref.shape[0] - 1
-    return [
-        (half_ref[jnp.where(slot < ready, sorted_ref[face, 0, slot], none)], compliance_ref[face, order_ref[face, 0, slot]])
-        for slot in range(count)
-    ]
-
-
-def fetch(blocks_hbm, load_hbm, motion_hbm, stress_hbm, stiff_hbm, record_hbm, turn_hbm, columns_hbm, partner_hbm, half_in_ref,
-          blocks_ref, load_ref, motion_ref, stress_ref, stiff_ref, record_ref, turn_ref, partner_ref,
-          order_ref, sorted_ref, own_ref, ready_ref, early0_ref, early1_ref,
-          columns_ref, order_vmem, sorted_vmem, own_vmem, ready_vmem, half_ref, sems):
-    group, _, extent = early0_ref.shape
-    faces = 2 * group
-    *starts, mine = position(group)
-    columns_copy = pltpu.make_async_copy(columns_hbm, columns_ref, sems.at[0])
-    columns_copy.start()
-    rows = [[], []]
-    for side in (1, 0):
-        for index in range(group):
-            face = starts[side] + index
-            row = pltpu.make_async_copy(blocks_hbm.at[face], blocks_ref.at[face], sems.at[1 + side * group + index])
-            row.start()
-            rows[side].append(row)
-    pairs = (
-        (load_hbm, load_ref), (motion_hbm, motion_ref), (stress_hbm, stress_ref), (stiff_hbm, stiff_ref),
-        (record_hbm, record_ref), (turn_hbm, turn_ref), (partner_hbm, partner_ref),
-    )
-    small = [pltpu.make_async_copy(source, target, sems.at[1 + faces + n]) for n, (source, target) in enumerate(pairs)]
-    for copy in small:
-        copy.start()
-    for face in range(faces):
-        half_ref[mine * faces + face] = half_in_ref[:, face * extent : (face + 1) * extent]
-    none = half_ref.shape[0] - 1
-    half_ref[none] = jnp.zeros_like(half_ref[none])
-    columns_copy.wait()
-    tables = ((order_vmem, order_ref), (sorted_vmem, sorted_ref), (own_vmem, own_ref), (ready_vmem, ready_ref))
-    sort_blocks(columns_ref, *(source for source, _ in tables))
-    tables = [
-        pltpu.make_async_copy(source, target, sems.at[1 + faces + len(pairs) + n]) for n, (source, target) in enumerate(tables)
-    ]
-    for copy in tables:
-        copy.start()
-    for copy in tables:
-        copy.wait()
-    entries = functools.partial(early_entries, half_ref, order_ref, sorted_ref, own_ref, blocks_ref, FIRST)
-    for side, out_ref in ((1, early1_ref), (0, early0_ref)):
-        for index in range(0, group, 2):
-            count = min(2, group - index)
-            for row in rows[side][index : index + count]:
-                row.wait()
-            products = block_products([entries(starts[side] + index + k) for k in range(count)])
-            for k in range(count):
-                out_ref[index + k] = products[k]
-    for copy in small:
-        copy.wait()
-
-
 def early_products(side, order_ref, sorted_ref, ready_ref, compliance_ref, own0_ref, own1_ref, *refs):
     out_ref, half_ref = refs[-2:]
     group = out_ref.shape[0]
@@ -155,7 +112,13 @@
         half_ref[pl.ds(mine * faces + start, group)] = ref[...]
     for ref in refs[:side]:
         half_ref[pl.ds((1 - mine) * faces + starts[0], group)] = ref[...]
-    entries = functools.partial(early_entries, half_ref, order_ref, sorted_ref, ready_ref, compliance_ref, EARLY[side])
+
+    def entries(face):
+        ready = ready_ref[face, 0, 0]
+        return [
+            (half_ref[jnp.where(slot < ready, sorted_ref[face, 0, slot], none)], compliance_ref[face, order_ref[face, 0, slot]])
+            for slot in range(EARLY[side])
+        ]
 
     def finish(index, product):
         out_ref[index] = product
@@ -170,6 +133,9 @@
         return half_ref[sorted_ref[face, 0, slot]], compliance_ref[face, order_ref[face, 0, slot]]
 
     group_products(first, group, lambda face: [entry(face, slot) for slot in range(done, stored)], finish)
+
+    if not done:
+        return
 
     def missed(slot, index):
         out_ref[index] -= 2.0 * block_products([[entry(first + index, slot)]])[0]
@@ -185,8 +151,8 @@
             lax.fori_loop(ready_ref[first + index, 0, 0], done, missed, index)
 
 
-def first_section(side, order_ref, sorted_ref, own_count_ref, compliance_ref, own_ref, other_ref, motion_ref, stress_ref,
-                  load_ref, early_ref, stiff_ref, record_ref, out_ref, half_ref):
+def first_section(side, order_ref, sorted_ref, ready_ref, compliance_ref, own_ref, other_ref, motion_ref, stress_ref,
+                  load_ref, stiff_ref, record_ref, out_ref, half_ref):
     faces, _, extent, _ = compliance_ref.shape
     group = faces // 2
     *starts, mine = position(group)
@@ -198,14 +164,14 @@
     def finish(index, product):
         lanes = lanes_of(first + index, extent)
         robin = stress_ref[:, lanes].astype(jnp.float32) + motion_ref[:, lanes].astype(jnp.float32)
-        response = early_ref[index] + product + load_ref[:, lanes].astype(jnp.float32)
+        response = product + load_ref[:, lanes].astype(jnp.float32)
         out_ref[index] = robin - 2.0 * response
         out_ref[group, index : index + 1] = stiff_ref[:, lanes]
         out_ref[group, group + index : group + index + 1] = record_ref[:, lanes]
 
     for plane in range(group, out_ref.shape[0]):
         out_ref[plane] = jnp.zeros_like(out_ref[plane])
-    late_products(first, FIRST, order_ref, sorted_ref, own_count_ref, compliance_ref, half_ref, finish, out_ref)
+    late_products(first, 0, order_ref, sorted_ref, ready_ref, compliance_ref, half_ref, finish, out_ref)
 
 
 def linear_section(side, order_ref, sorted_ref, ready_ref, compliance_ref, own0_ref, own1_ref, other0_ref, other1_ref,
@@ -404,21 +370,20 @@
     in_hbm = functools.partial(pltpu.with_memory_space_constraint, memory_space=pltpu.HBM)
     own = (start_traction[0].astype(jnp.float32) + starting_motion[0].astype(jnp.float32)).astype(jnp.bfloat16)
     other = lax.ppermute(own, "row", swap)
-    table, counts = pltpu.SMEM((faces, 1, stored), jnp.int32), pltpu.SMEM((faces, 1, 1), jnp.int32)
-    tables = [pltpu.VMEM((faces, 1, width), jnp.int32) for width in (stored, stored, stored, 1, 1)]
-    blocks, load, motion, stress, stiff, record, turn, *tables, first0, first1 = call(
-        fetch, [HBM] * 9 + [VMEM],
+    in_smem = [pltpu.SMEM((faces, 1, width), jnp.int32) for width in (stored, stored, 1)]
+    in_vmem = [pltpu.VMEM((faces, 1, width), jnp.int32) for width in (stored, stored, stored, 1)]
+    blocks, load, motion, stress, stiff, record, turn, *tables = call(
+        fetch, [HBM] * 9,
         (pltpu.VMEM((faces, stored, extent, extent), jnp.bfloat16), bf16(*flat), bf16(*flat), bf16(*flat),
-         f32(1, faces * extent), f32(1, faces * extent), s32(1, faces * extent),
-         pltpu.SMEM((1, faces), jnp.int32), table, table, counts, counts, f32(*part), f32(*part)),
-        tables + [pltpu.VMEM((rows * faces + 1, times, extent), jnp.bfloat16), pltpu.SemaphoreType.DMA((12 + faces,))],
-        block_bytes, (VMEM,) * 7 + (SMEM,) * 5 + (VMEM,) * 2,
+         f32(1, faces * extent), f32(1, faces * extent), s32(1, faces * extent), pltpu.SMEM((1, faces), jnp.int32), *in_smem),
+        in_vmem + [pltpu.SemaphoreType.DMA((11 + faces,))],
+        block_bytes, (VMEM,) * 7 + (SMEM,) * 4,
     )(
         in_hbm(compliance[0]), in_hbm(load_response[0]), in_hbm(starting_motion[0]), in_hbm(start_traction[0]),
         in_hbm(stiffness), in_hbm(history), in_hbm(orientation.reshape(1, -1)),
-        in_hbm(jnp.transpose(block_columns, (1, 0, 2))), in_hbm(face_partner), own,
+        in_hbm(jnp.transpose(block_columns, (1, 0, 2))), in_hbm(face_partner),
     )
-    partner, order, columns, owned, ready = (pltpu.with_memory_space_constraint(value, pltpu.SMEM) for value in tables)
+    partner, order, columns, ready = (pltpu.with_memory_space_constraint(value, pltpu.SMEM) for value in tables)
 
     robin, half = [None, None], [None, None]
     stiffs, records = [stiff, stiff], [record, record]
@@ -435,9 +400,9 @@
         for side, (axes, pairs) in enumerate((("sub", near_pairs), (("sub", "row"), far_pairs))):
             if begin:
                 ascent[side] = sent = call(
-                    functools.partial(first_section, side), [SMEM] * 3 + [VMEM] * 9,
+                    functools.partial(first_section, side), [SMEM] * 3 + [VMEM] * 8,
                     f32(group + 1 + side, times, extent), [halves], 2 * block_bytes,
-                )(order, columns, owned, blocks, own, other, motion, stress, load, (first0, first1)[side], stiff, record)
+                )(order, columns, ready, blocks, own, other, motion, stress, load, stiff, record)
             else:
                 ascent[side], sent = call(
                     functools.partial(linear_section, side), [SMEM] * 3 + [VMEM] * 8,

time: 41.3 us -> 41 us (level)
  Pallas kernels: 18.2 us -> 18.8 us
  starting transfers between devices: 13 us -> 12.5 us
    ppermute x6, starting transfers between devices: 6.15 us -> 5.14 us  [shards(): mates[side] = lax.ppermute(sent, axes, pairs)]
    pallas_call x4, Pallas kernels: 4.72 us -> 5.17 us  [shards(): call(functools.partial(linear_section, side), [SMEM] * 3 + [VMEM] * 8, (f...]
    ppermute x4, starting transfers between devices: 3.89 us -> 4.33 us  [shards(): other = [lax.ppermute(half[side], 'row', swap) for side in range(2)]]
  transfers between devices with their start and end apart: 11 -> 11, of which waited for: 8 -> 8; matrix products, arithmetic and copies ran while one was open for 0% -> 0% of each run, Pallas kernels for 34% -> 33%
where the time goes in v4:
time: 41 us; the launch traced here: 40.9 us
  Pallas kernels  18.8 us (46%)
  starting transfers between devices  12.5 us (30%)
  waiting for transfers between devices  7.84 us (19%)
  other arithmetic  1.02 us (2%)
  between operations  0.77 us (2%)
    pallas_call x4, Pallas kernels, shards(): call(functools.partial(linear_section, side), [SMEM] * 3 + [VMEM] * 8, (f...  5.17 us
    ppermute x6, starting transfers between devices, shards(): mates[side] = lax.ppermute(sent, axes, pairs)  5.14 us
    pallas_call x1, Pallas kernels, shards(): call(fetch, [HBM] * 9, (pltpu.VMEM((faces, stored, extent, extent), jnp.b...  4.57 us
    ppermute x4, starting transfers between devices, shards(): other = [lax.ppermute(half[side], 'row', swap) for side in range(2)]  4.33 us
    ppermute x4, waiting for transfers between devices, shards(): other = [lax.ppermute(half[side], 'row', swap) for side in range(2)]  4.16 us
    ppermute x6, waiting for transfers between devices, shards(): mates[side] = lax.ppermute(sent, axes, pairs)  3.67 us
    pallas_call x2, Pallas kernels, shards(): call(functools.partial(first_section, side), [SMEM] * 3 + [VMEM] * 8, f32...  3.51 us
    pallas_call x4, Pallas kernels, shards(): call(functools.partial(early_products, side), [SMEM] * 3 + [VMEM] * (3 +...  3.31 us
  transfers between devices with their start and end apart: 11, of which 8 were waited for; matrix products, arithmetic and copies ran while one was open for 0% of the time, Pallas kernels for 33%

profile of v4, /device:TPU:0, one launch (start us, length us, event | category | flops | bytes accessed | tf_op | source)
XLA Modules:
  0.0 40.9 jit_solution(1747044915676018358)
XLA Ops:
  0.6 1.0 %add_convert_fusion.own_ref = bf16[32,2304]{1,0:T(8,128)(2,1)S(1)} fusion(bf16[1,32,2304]{2,1,0:T(8,128)(2,1)} %param.13, bf16[1,32,2304]{2,1,0:T(8,128)(2,1)} %param.12), kind=kLoop, calls=%fused_computation | loop fusion | flops 294912 | bytes 442368 | tf_op jit(solution)/shard_map/convert_element_type | solution.py:371
  1.7 3.0 %collective-permute-start = (bf16[32,2304]{1,0:T(8,128)(2,1)S(1)}, bf16[32,2304]{1,0:T(8,128)(2,1)S(1)}, u32[]{:S(2)}, u32[]{:S(2)}) collective-permute-start(bf16[32,2304]{1,0:T(8,128)(2,1)S(1)} %add_convert_fusion.own_ref), channel_id=1, source_target_pairs={{0,1},{1,0},{2,3},{3,2},{4,5},{5,4},{6,7},{7,6},{8,9},{9,8},{10,11... | collective-permute-start | bytes 442376 | tf_op jit(solution)/shard_map/ppermute | solution.py:372
  4.7 4.6 %shard_map.104 = (bf16[18,18,128,128]{3,2,1,0:T(8,128)(2,1)S(1)}, bf16[32,2304]{1,0:T(8,128)(2,1)S(1)}, bf16[32,2304]{1,0:T(8,128)(2,1)S(1)}, bf16[32,2304]{1,0:...) custom-call(bf16[18,18,128,128]{3,2,1,0:T(8,128)(2,1)} %bitcast.10, ...), custom_call_target="tpu_custom_call" | custom-call | flops 10616832 | bytes 10616832 | tf_op jit(solution)/shard_map/pallas_call | solution.py:375
  9.2 1.8 %shard_map.107.own_ref = f32[11,32,128]{2,1,0:T(8,128)S(1)} custom-call(s32[18,1,18]{2,1,0:T(1,128)S(4)} %get-tuple-element.39.order_ref, s32[18,1,18]{2,1,0:T(1,128)S(4)} %get-tuple-element.40.sorted_ref, s32[18,1,1]{2,1,0:T(1,128)S(4)} %get-tuple-element.41.ready_ref, bf16[18,18,128,128]{3,2,1,0:T(8,128)(2,1)S(1)} %get-tuple-element.42.compliance_ref, ...), custom_call_target="tpu_custom_call" | custom-call | flops 21233664 | bytes 21233664 | tf_op jit(solution)/shard_map/pallas_call | solution.py:402
  11.0 1.1 %collective-permute-start.2 = (f32[11,32,128]{2,1,0:T(8,128)S(1)}, f32[11,32,128]{2,1,0:T(8,128)S(1)}, u32[]{:S(2)}, u32[]{:S(2)}) collective-permute-start(f32[11,32,128]{2,1,0:T(8,128)S(1)} %shard_map.107.own_ref), channel_id=1, source_target_pairs={{0,1},{1,0},{2,4},{3,5},{4,2},{5,3},{6,8},{7,9},{8,6},{9,7},{10,12... | collective-permute-start | bytes 540680 | tf_op jit(solution)/shard_map/ppermute | solution.py:412
  12.1 1.7 %shard_map.105.own_ref = f32[10,32,128]{2,1,0:T(8,128)S(1)} custom-call(s32[18,1,18]{2,1,0:T(1,128)S(4)} %get-tuple-element.39.order_ref, s32[18,1,18]{2,1,0:T(1,128)S(4)} %get-tuple-element.40.sorted_ref, s32[18,1,1]{2,1,0:T(1,128)S(4)} %get-tuple-element.41.ready_ref, bf16[18,18,128,128]{3,2,1,0:T(8,128)(2,1)S(1)} %get-tuple-element.42.compliance_ref, ...), custom_call_target="tpu_custom_call" | custom-call | flops 21233664 | bytes 21233664 | tf_op jit(solution)/shard_map/pallas_call | solution.py:402
  13.8 0.7 %collective-permute-start.1 = (f32[10,32,128]{2,1,0:T(8,128)S(1)}, f32[10,32,128]{2,1,0:T(8,128)S(1)}, u32[]{:S(2)}, u32[]{:S(2)}) collective-permute-start(f32[10,32,128]{2,1,0:T(8,128)S(1)} %shard_map.105.own_ref), channel_id=1, source_target_pairs={{0,2},{2,0},{4,6},{6,4},{8,10},{10,8},{12,14},{14,12},{16,18},{18,... | collective-permute-start | bytes 491528 | tf_op jit(solution)/shard_map/ppermute | solution.py:412
  14.5 1.0 %collective-permute-done.1.mate_ref = f32[10,32,128]{2,1,0:T(8,128)S(1)} collective-permute-done((f32[10,32,128]{2,1,0:T(8,128)S(1)}, f32[10,32,128]{2,1,0:T(8,128)S(1)}, u32[]{:S(2)}, u32[]{:S(2)}) %collective-permute-start.1) | collective-permute-done | bytes 163872 | tf_op jit(solution)/shard_map/ppermute | solution.py:412
  15.8 1.1 %collective-permute-start.3 = (bf16[9,32,128]{2,1,0:T(8,128)(2,1)S(1)}, bf16[9,32,128]{2,1,0:T(8,128)(2,1)S(1)}, u32[]{:S(2)}, u32[]{:S(2)}) collective-permute-start(bf16[9,32,128]{2,1,0:T(8,128)(2,1)S(1)} %get-tuple-element.48.own0_ref), channel_id=1, source_target_pairs={{0,1},{1,0},{2,3},{3,2},{4,5},{5,4},{6,7},{7,6},{8,9},{9,8},{10,11... | collective-permute-start | bytes 221192 | tf_op jit(solution)/shard_map/ppermute | solution.py:393
  16.9 0.3 shard_map.108
  17.2 1.1 %collective-permute-start.4 = (bf16[9,32,128]{2,1,0:T(8,128)(2,1)S(1)}, bf16[9,32,128]{2,1,0:T(8,128)(2,1)S(1)}, u32[]{:S(2)}, u32[]{:S(2)}) collective-permute-start(bf16[9,32,128]{2,1,0:T(8,128)(2,1)S(1)} %get-tuple-element.49.own1_ref), channel_id=1, source_target_pairs={{0,1},{1,0},{2,3},{3,2},{4,5},{5,4},{6,7},{7,6},{8,9},{9,8},{10,11... | collective-permute-start | bytes 221192 | tf_op jit(solution)/shard_map/ppermute | solution.py:393
  18.3 0.7 %shard_map.109.early_ref.refs_1_ = f32[9,32,128]{2,1,0:T(8,128)S(1)} custom-call(s32[18,1,18]{2,1,0:T(1,128)S(4)} %get-tuple-element.39.order_ref, s32[18,1,18]{2,1,0:T(1,128)S(4)} %get-tuple-element.40.sorted_ref, s32[18,1,1]{2,1,0:T(1,128)S(4)} %get-tuple-element.41.ready_ref, bf16[18,18,128,128]{3,2,1,0:T(8,128)(2,1)S(1)} %get-tuple-element.42.compliance_ref, ...), custom_call_target="tpu_custom_call" | custom-call | flops 10616832 | bytes 10616832 | tf_op jit(solution)/shard_map/pallas_call | solution.py:396
  18.9 2.0 %collective-permute-done.3.other0_ref.refs_0_ = bf16[9,32,128]{2,1,0:T(8,128)(2,1)S(1)} collective-permute-done((bf16[9,32,128]{2,1,0:T(8,128)(2,1)S(1)}, bf16[9,32,128]{2,1,0:T(8,128)(2,1)S(1)}, u32[]{:S(2)}, u32[]{:S(2)}) %collective-permute-start.3) | collective-permute-done | bytes 73760 | tf_op jit(solution)/shard_map/ppermute | solution.py:393
  20.9 1.0 %shard_map.112.early_ref = f32[9,32,128]{2,1,0:T(8,128)S(1)} custom-call(s32[18,1,18]{2,1,0:T(1,128)S(4)} %get-tuple-element.39.order_ref, s32[18,1,18]{2,1,0:T(1,128)S(4)} %get-tuple-element.40.sorted_ref, s32[18,1,1]{2,1,0:T(1,128)S(4)} %get-tuple-element.41.ready_ref, bf16[18,18,128,128]{3,2,1,0:T(8,128)(2,1)S(1)} %get-tuple-element.42.compliance_ref, ...), custom_call_target="tpu_custom_call" | custom-call | flops 10616832 | bytes 10616832 | tf_op jit(solution)/shard_map/pallas_call | solution.py:396
  22.0 1.2 %shard_map.113 = (f32[9,32,128]{2,1,0:T(8,128)S(1)}, s16[11,32,128]{2,1,0:T(8,128)(2,1)S(1)}) custom-call(s32[18,1,18]{2,1,0:T(1,128)S(4)} %get-tuple-element.39.order_ref, s32[18,1,18]{2,1,0:T(1,128)S(4)} %get-tuple-element.40.sorted_ref, s32[18,1,1]{2,1,0:T(1,128)S(4)} %get-tuple-element.41.ready_ref, ...), custom_call_target="tpu_custom_call" | custom-call | flops 21233664 | bytes 21233664 | tf_op jit(solution)/shard_map/pallas_call | solution.py:407
  23.2 0.8 %collective-permute-start.6 = (s16[11,32,128]{2,1,0:T(8,128)(2,1)S(1)}, s16[11,32,128]{2,1,0:T(8,128)(2,1)S(1)}, u32[]{:S(2)}, u32[]{:S(2)}) collective-permute-start(s16[11,32,128]{2,1,0:T(8,128)(2,1)S(1)} %get-tuple-element.58), channel_id=1, source_target_pairs={{0,1},{1,0},{2,4},{3,5},{4,2},{5,3},{6,8},{7,9},{8,6},{9,7},{10,12... | collective-permute-start | bytes 270344 | tf_op jit(solution)/shard_map/ppermute | solution.py:412
  24.1 1.4 %shard_map.110 = (f32[9,32,128]{2,1,0:T(8,128)S(1)}, s16[10,32,128]{2,1,0:T(8,128)(2,1)S(1)}) custom-call(s32[18,1,18]{2,1,0:T(1,128)S(4)} %get-tuple-element.39.order_ref, s32[18,1,18]{2,1,0:T(1,128)S(4)} %get-tuple-element.40.sorted_ref, s32[18,1,1]{2,1,0:T(1,128)S(4)} %get-tuple-element.41.ready_ref, ...), custom_call_target="tpu_custom_call" | custom-call | flops 21233664 | bytes 21233664 | tf_op jit(solution)/shard_map/pallas_call | solution.py:407
  25.4 1.3 %collective-permute-start.5 = (s16[10,32,128]{2,1,0:T(8,128)(2,1)S(1)}, s16[10,32,128]{2,1,0:T(8,128)(2,1)S(1)}, u32[]{:S(2)}, u32[]{:S(2)}) collective-permute-start(s16[10,32,128]{2,1,0:T(8,128)(2,1)S(1)} %get-tuple-element.52), channel_id=1, source_target_pairs={{0,2},{2,0},{4,6},{6,4},{8,10},{10,8},{12,14},{14,12},{16,18},{18,... | collective-permute-start | bytes 245768 | tf_op jit(solution)/shard_map/ppermute | solution.py:412
  26.7 0.9 %collective-permute-done.5.refs_3_ = s16[10,32,128]{2,1,0:T(8,128)(2,1)S(1)} collective-permute-done((s16[10,32,128]{2,1,0:T(8,128)(2,1)S(1)}, s16[10,32,128]{2,1,0:T(8,128)(2,1)S(1)}, u32[]{:S(2)}, u32[]{:S(2)}) %collective-permute-start.5) | collective-permute-done | bytes 81952 | tf_op jit(solution)/shard_map/ppermute | solution.py:412
  27.9 1.1 %collective-permute-start.7 = (bf16[9,32,128]{2,1,0:T(8,128)(2,1)S(1)}, bf16[9,32,128]{2,1,0:T(8,128)(2,1)S(1)}, u32[]{:S(2)}, u32[]{:S(2)}) collective-permute-start(bf16[9,32,128]{2,1,0:T(8,128)(2,1)S(1)} %get-tuple-element.55.own0_ref), channel_id=1, source_target_pairs={{0,1},{1,0},{2,3},{3,2},{4,5},{5,4},{6,7},{7,6},{8,9},{9,8},{10,11... | collective-permute-start | bytes 221192 | tf_op jit(solution)/shard_map/ppermute | solution.py:393
  29.3 1.1 %collective-permute-start.8 = (bf16[9,32,128]{2,1,0:T(8,128)(2,1)S(1)}, bf16[9,32,128]{2,1,0:T(8,128)(2,1)S(1)}, u32[]{:S(2)}, u32[]{:S(2)}) collective-permute-start(bf16[9,32,128]{2,1,0:T(8,128)(2,1)S(1)} %get-tuple-element.61.own1_ref), channel_id=1, source_target_pairs={{0,1},{1,0},{2,3},{3,2},{4,5},{5,4},{6,7},{7,6},{8,9},{9,8},{10,11... | collective-permute-start | bytes 221192 | tf_op jit(solution)/shard_map/ppermute | solution.py:393
  30.3 0.7 %shard_map.115.refs_1_.early_ref = f32[9,32,128]{2,1,0:T(8,128)S(1)} custom-call(s32[18,1,18]{2,1,0:T(1,128)S(4)} %get-tuple-element.39.order_ref, s32[18,1,18]{2,1,0:T(1,128)S(4)} %get-tuple-element.40.sorted_ref, s32[18,1,1]{2,1,0:T(1,128)S(4)} %get-tuple-element.41.ready_ref, bf16[18,18,128,128]{3,2,1,0:T(8,128)(2,1)S(1)} %get-tuple-element.42.compliance_ref, ...), custom_call_target="tpu_custom_call" | custom-call | flops 10616832 | bytes 10616832 | tf_op jit(solution)/shard_map/pallas_call | solution.py:396
  31.0 2.0 %collective-permute-done.7.refs_0_.other0_ref = bf16[9,32,128]{2,1,0:T(8,128)(2,1)S(1)} collective-permute-done((bf16[9,32,128]{2,1,0:T(8,128)(2,1)S(1)}, bf16[9,32,128]{2,1,0:T(8,128)(2,1)S(1)}, u32[]{:S(2)}, u32[]{:S(2)}) %collective-permute-start.7) | collective-permute-done | bytes 73760 | tf_op jit(solution)/shard_map/ppermute | solution.py:393
  33.0 1.0 %shard_map.116.early_ref = f32[9,32,128]{2,1,0:T(8,128)S(1)} custom-call(s32[18,1,18]{2,1,0:T(1,128)S(4)} %get-tuple-element.39.order_ref, s32[18,1,18]{2,1,0:T(1,128)S(4)} %get-tuple-element.40.sorted_ref, s32[18,1,1]{2,1,0:T(1,128)S(4)} %get-tuple-element.41.ready_ref, bf16[18,18,128,128]{3,2,1,0:T(8,128)(2,1)S(1)} %get-tuple-element.42.compliance_ref, ...), custom_call_target="tpu_custom_call" | custom-call | flops 10616832 | bytes 10616832 | tf_op jit(solution)/shard_map/pallas_call | solution.py:396
  34.1 1.2 %shard_map.117 = (f32[9,32,128]{2,1,0:T(8,128)S(1)}, s16[11,32,128]{2,1,0:T(8,128)(2,1)S(1)}) custom-call(s32[18,1,18]{2,1,0:T(1,128)S(4)} %get-tuple-element.39.order_ref, s32[18,1,18]{2,1,0:T(1,128)S(4)} %get-tuple-element.40.sorted_ref, s32[18,1,1]{2,1,0:T(1,128)S(4)} %get-tuple-element.41.ready_ref, ...), custom_call_target="tpu_custom_call" | custom-call | flops 21233664 | bytes 21233664 | tf_op jit(solution)/shard_map/pallas_call | solution.py:407
  35.3 0.8 %collective-permute-start.9 = (s16[11,32,128]{2,1,0:T(8,128)(2,1)S(1)}, s16[11,32,128]{2,1,0:T(8,128)(2,1)S(1)}, u32[]{:S(2)}, u32[]{:S(2)}) collective-permute-start(s16[11,32,128]{2,1,0:T(8,128)(2,1)S(1)} %get-tuple-element.64), channel_id=1, source_target_pairs={{0,1},{1,0},{2,4},{3,5},{4,2},{5,3},{6,8},{7,9},{8,6},{9,7},{10,12... | collective-permute-start | bytes 270344 | tf_op jit(solution)/shard_map/ppermute | solution.py:412
  36.2 1.4 %shard_map.118 = (f32[9,32,128]{2,1,0:T(8,128)S(1)}, s16[10,32,128]{2,1,0:T(8,128)(2,1)S(1)}) custom-call(s32[18,1,18]{2,1,0:T(1,128)S(4)} %get-tuple-element.39.order_ref, s32[18,1,18]{2,1,0:T(1,128)S(4)} %get-tuple-element.40.sorted_ref, s32[18,1,1]{2,1,0:T(1,128)S(4)} %get-tuple-element.41.ready_ref, ...), custom_call_target="tpu_custom_call" | custom-call | flops 21233664 | bytes 21233664 | tf_op jit(solution)/shard_map/pallas_call | solution.py:407
  37.5 0.4 %collective-permute-start.10 = (s16[10,32,128]{2,1,0:T(8,128)(2,1)S(1)}, s16[10,32,128]{2,1,0:T(8,128)(2,1)S(1)}, u32[]{:S(2)}, u32[]{:S(2)}) collective-permute-start(s16[10,32,128]{2,1,0:T(8,128)(2,1)S(1)} %get-tuple-element.67), channel_id=1, source_target_pairs={{0,2},{2,0},{4,6},{6,4},{8,10},{10,8},{12,14},{14,12},{16,18},{18,... | collective-permute-start | bytes 245768 | tf_op jit(solution)/shard_map/ppermute | solution.py:412
  37.9 0.9 %collective-permute-done.10.refs_3_ = s16[10,32,128]{2,1,0:T(8,128)(2,1)S(1)} collective-permute-done((s16[10,32,128]{2,1,0:T(8,128)(2,1)S(1)}, s16[10,32,128]{2,1,0:T(8,128)(2,1)S(1)}, u32[]{:S(2)}, u32[]{:S(2)}) %collective-permute-start.10) | collective-permute-done | bytes 81952 | tf_op jit(solution)/shard_map/ppermute | solution.py:412
  38.9 0.3 shard_map.119
  39.1 0.8 %collective-permute-done.9.refs_3_ = s16[11,32,128]{2,1,0:T(8,128)(2,1)S(1)} collective-permute-done((s16[11,32,128]{2,1,0:T(8,128)(2,1)S(1)}, s16[11,32,128]{2,1,0:T(8,128)(2,1)S(1)}, u32[]{:S(2)}, u32[]{:S(2)}) %collective-permute-start.9) | collective-permute-done | bytes 90144 | tf_op jit(solution)/shard_map/ppermute | solution.py:412
  39.9 1.0 %shard_map.120 = (bf16[32,2304]{1,0:T(8,128)(2,1)}, bf16[32,2304]{1,0:T(8,128)(2,1)}) custom-call(s32[1,18]{1,0:T(1,128)S(4)} %get-tuple-element.37.partner_ref.refs_0_, s32[1,2304]{1,0:T(1,128)S(1)} %get-tuple-element.38.turn_ref.refs_1_, f32[9,32,128]{2,1,0:T(8,128)S(1)} %get-tuple-element.63.refs_2_, ...), custom_call_target="tpu_custom_call" | custom-call | tf_op jit(solution)/shard_map/pallas_call | solution.py:429
  (8 shorter events, 0.9 us)
Async XLA Ops:
  1.7 7.6 %collective-permute-start = (bf16[32,2304]{1,0:T(8,128)(2,1)S(1)}, bf16[32,2304]{1,0:T(8,128)(2,1)S(1)}, u32[]{:S(2)}, u32[]{:S(2)}) collective-permute-start(bf16[32,2304]{1,0:T(8,128)(2,1)S(1)} %add_convert_fusion.own_ref), channel_id=1, source_target_pairs={{0,1},{1,0},{2,3},{3,2},{4,5},{5,4},{6,7},{7,6},{8,9},{9,8},{10,11... | collective-permute-start | bytes 442376 | tf_op jit(solution)/shard_map/ppermute | solution.py:372
  11.0 5.9 %collective-permute-start.2 = (f32[11,32,128]{2,1,0:T(8,128)S(1)}, f32[11,32,128]{2,1,0:T(8,128)S(1)}, u32[]{:S(2)}, u32[]{:S(2)}) collective-permute-start(f32[11,32,128]{2,1,0:T(8,128)S(1)} %shard_map.107.own_ref), channel_id=1, source_target_pairs={{0,1},{1,0},{2,4},{3,5},{4,2},{5,3},{6,8},{7,9},{8,6},{9,7},{10,12... | collective-permute-start | bytes 540680 | tf_op jit(solution)/shard_map/ppermute | solution.py:412
  13.8 1.7 %collective-permute-start.1 = (f32[10,32,128]{2,1,0:T(8,128)S(1)}, f32[10,32,128]{2,1,0:T(8,128)S(1)}, u32[]{:S(2)}, u32[]{:S(2)}) collective-permute-start(f32[10,32,128]{2,1,0:T(8,128)S(1)} %shard_map.105.own_ref), channel_id=1, source_target_pairs={{0,2},{2,0},{4,6},{6,4},{8,10},{10,8},{12,14},{14,12},{16,18},{18,... | collective-permute-start | bytes 491528 | tf_op jit(solution)/shard_map/ppermute | solution.py:412
  15.8 5.1 %collective-permute-start.3 = (bf16[9,32,128]{2,1,0:T(8,128)(2,1)S(1)}, bf16[9,32,128]{2,1,0:T(8,128)(2,1)S(1)}, u32[]{:S(2)}, u32[]{:S(2)}) collective-permute-start(bf16[9,32,128]{2,1,0:T(8,128)(2,1)S(1)} %get-tuple-element.48.own0_ref), channel_id=1, source_target_pairs={{0,1},{1,0},{2,3},{3,2},{4,5},{5,4},{6,7},{7,6},{8,9},{9,8},{10,11... | collective-permute-start | bytes 221192 | tf_op jit(solution)/shard_map/ppermute | solution.py:393
  17.2 4.8 %collective-permute-start.4 = (bf16[9,32,128]{2,1,0:T(8,128)(2,1)S(1)}, bf16[9,32,128]{2,1,0:T(8,128)(2,1)S(1)}, u32[]{:S(2)}, u32[]{:S(2)}) collective-permute-start(bf16[9,32,128]{2,1,0:T(8,128)(2,1)S(1)} %get-tuple-element.49.own1_ref), channel_id=1, source_target_pairs={{0,1},{1,0},{2,3},{3,2},{4,5},{5,4},{6,7},{7,6},{8,9},{9,8},{10,11... | collective-permute-start | bytes 221192 | tf_op jit(solution)/shard_map/ppermute | solution.py:393
  23.2 5.8 %collective-permute-start.6 = (s16[11,32,128]{2,1,0:T(8,128)(2,1)S(1)}, s16[11,32,128]{2,1,0:T(8,128)(2,1)S(1)}, u32[]{:S(2)}, u32[]{:S(2)}) collective-permute-start(s16[11,32,128]{2,1,0:T(8,128)(2,1)S(1)} %get-tuple-element.58), channel_id=1, source_target_pairs={{0,1},{1,0},{2,4},{3,5},{4,2},{5,3},{6,8},{7,9},{8,6},{9,7},{10,12... | collective-permute-start | bytes 270344 | tf_op jit(solution)/shard_map/ppermute | solution.py:412
  25.4 2.2 %collective-permute-start.5 = (s16[10,32,128]{2,1,0:T(8,128)(2,1)S(1)}, s16[10,32,128]{2,1,0:T(8,128)(2,1)S(1)}, u32[]{:S(2)}, u32[]{:S(2)}) collective-permute-start(s16[10,32,128]{2,1,0:T(8,128)(2,1)S(1)} %get-tuple-element.52), channel_id=1, source_target_pairs={{0,2},{2,0},{4,6},{6,4},{8,10},{10,8},{12,14},{14,12},{16,18},{18,... | collective-permute-start | bytes 245768 | tf_op jit(solution)/shard_map/ppermute | solution.py:412
  27.9 5.1 %collective-permute-start.7 = (bf16[9,32,128]{2,1,0:T(8,128)(2,1)S(1)}, bf16[9,32,128]{2,1,0:T(8,128)(2,1)S(1)}, u32[]{:S(2)}, u32[]{:S(2)}) collective-permute-start(bf16[9,32,128]{2,1,0:T(8,128)(2,1)S(1)} %get-tuple-element.55.own0_ref), channel_id=1, source_target_pairs={{0,1},{1,0},{2,3},{3,2},{4,5},{5,4},{6,7},{7,6},{8,9},{9,8},{10,11... | collective-permute-start | bytes 221192 | tf_op jit(solution)/shard_map/ppermute | solution.py:393
  29.3 4.8 %collective-permute-start.8 = (bf16[9,32,128]{2,1,0:T(8,128)(2,1)S(1)}, bf16[9,32,128]{2,1,0:T(8,128)(2,1)S(1)}, u32[]{:S(2)}, u32[]{:S(2)}) collective-permute-start(bf16[9,32,128]{2,1,0:T(8,128)(2,1)S(1)} %get-tuple-element.61.own1_ref), channel_id=1, source_target_pairs={{0,1},{1,0},{2,3},{3,2},{4,5},{5,4},{6,7},{7,6},{8,9},{9,8},{10,11... | collective-permute-start | bytes 221192 | tf_op jit(solution)/shard_map/ppermute | solution.py:393
  35.3 4.6 %collective-permute-start.9 = (s16[11,32,128]{2,1,0:T(8,128)(2,1)S(1)}, s16[11,32,128]{2,1,0:T(8,128)(2,1)S(1)}, u32[]{:S(2)}, u32[]{:S(2)}) collective-permute-start(s16[11,32,128]{2,1,0:T(8,128)(2,1)S(1)} %get-tuple-element.64), channel_id=1, source_target_pairs={{0,1},{1,0},{2,4},{3,5},{4,2},{5,3},{6,8},{7,9},{8,6},{9,7},{10,12... | collective-permute-start | bytes 270344 | tf_op jit(solution)/shard_map/ppermute | solution.py:412
  37.5 1.3 %collective-permute-start.10 = (s16[10,32,128]{2,1,0:T(8,128)(2,1)S(1)}, s16[10,32,128]{2,1,0:T(8,128)(2,1)S(1)}, u32[]{:S(2)}, u32[]{:S(2)}) collective-permute-start(s16[10,32,128]{2,1,0:T(8,128)(2,1)S(1)} %get-tuple-element.67), channel_id=1, source_target_pairs={{0,2},{2,0},{4,6},{6,4},{8,10},{10,8},{12,14},{14,12},{16,18},{18,... | collective-permute-start | bytes 245768 | tf_op jit(solution)/shard_map/ppermute | solution.py:412

commit v5 on v4

--- a/solution.py
+++ b/solution.py
@@ -10,7 +10,7 @@
 ITERS = 3
 SUBLANES = 8
 LEAST = 2.0**-100
-EARLY = (6, 10)
+EARLY = (0, 6, 10)
 VMEM_BYTES = 24 * 2**20
 
 ONSET_JUMP = 0.15
@@ -31,47 +31,48 @@
     return pl.ds(pl.multiple_of(face * extent, extent), extent)
 
 
-def sort_blocks(columns_ref, order_ref, sorted_ref, ready_ref):
+def sort_blocks(columns_ref, order_ref, sorted_ref, own_ref, ready_ref):
     faces, _, stored = columns_ref.shape
     group = faces // 2
-    near, far, mine = position(group)
+    near, _, mine = position(group)
     columns = jnp.concatenate([columns_ref[face] for face in range(faces)], axis=0).astype(jnp.float32)
-    row = lax.broadcasted_iota(jnp.int32, columns.shape, 0)
     lane = lax.broadcasted_iota(jnp.int32, columns.shape, 1).astype(jnp.float32)
     own = (mine * faces).astype(jnp.float32)
     partner = ((1 - mine) * faces + near).astype(jnp.float32)
-    width = jnp.where((row >= far) & (row < far + group), group, 0).astype(jnp.float32)
     front = jnp.zeros_like(columns)
+    middle = front + jnp.sum(jnp.where((columns >= own) & (columns < own + faces), 1.0, 0.0), axis=1, keepdims=True)
     back = front + (stored - 1.0)
     order, placed = front, front
     for j in range(stored):
         column = jnp.broadcast_to(columns[:, j : j + 1], columns.shape)
-        early = ((column >= own) & (column < own + faces)) | ((column >= partner) & (column < partner + width))
-        there = lane == jnp.where(early, front, back)
+        owned = (column >= own) & (column < own + faces)
+        soon = (column >= partner) & (column < partner + group)
+        there = lane == jnp.where(owned, front, jnp.where(soon, middle, back))
         order = jnp.where(there, float(j), order)
         placed = jnp.where(there, column, placed)
-        front = front + jnp.where(early, 1.0, 0.0)
-        back = back - jnp.where(early, 0.0, 1.0)
-    for ref, values in ((order_ref, order), (sorted_ref, placed), (ready_ref, front[:, :1])):
+        front = front + jnp.where(owned, 1.0, 0.0)
+        middle = middle + jnp.where(soon, 1.0, 0.0)
+        back = back - jnp.where(owned | soon, 0.0, 1.0)
+    for ref, values in ((order_ref, order), (sorted_ref, placed), (own_ref, front[:, :1]), (ready_ref, middle[:, :1])):
         for face in range(faces):
             ref[face] = values[face : face + 1].astype(jnp.int32)
 
 
 def fetch(blocks_hbm, load_hbm, motion_hbm, stress_hbm, stiff_hbm, record_hbm, turn_hbm, columns_hbm, partner_hbm,
           blocks_ref, load_ref, motion_ref, stress_ref, stiff_ref, record_ref, turn_ref, partner_ref,
-          order_ref, sorted_ref, ready_ref, columns_ref, order_vmem, sorted_vmem, ready_vmem, sems):
+          order_ref, sorted_ref, own_ref, ready_ref, columns_ref, order_vmem, sorted_vmem, own_vmem, ready_vmem, sems):
     pairs = [
         (columns_hbm, columns_ref), (load_hbm, load_ref), (motion_hbm, motion_ref), (stress_hbm, stress_ref),
         (stiff_hbm, stiff_ref), (record_hbm, record_ref), (turn_hbm, turn_ref), (partner_hbm, partner_ref),
     ]
     pairs += [(blocks_hbm.at[face], blocks_ref.at[face]) for face in range(blocks_hbm.shape[0])]
-    pairs += [(order_vmem, order_ref), (sorted_vmem, sorted_ref), (ready_vmem, ready_ref)]
+    pairs += [(order_vmem, order_ref), (sorted_vmem, sorted_ref), (own_vmem, own_ref), (ready_vmem, ready_ref)]
     copies = [pltpu.make_async_copy(source, target, sems.at[n]) for n, (source, target) in enumerate(pairs)]
-    for copy in copies[:-3]:
+    for copy in copies[:-4]:
         copy.start()
     copies[0].wait()
-    sort_blocks(columns_ref, order_vmem, sorted_vmem, ready_vmem)
-    for copy in copies[-3:]:
+    sort_blocks(columns_ref, order_vmem, sorted_vmem, own_vmem, ready_vmem)
+    for copy in copies[-4:]:
         copy.start()
     for copy in copies[1:]:
         copy.wait()
@@ -101,57 +102,66 @@
         finish(group - 1, sum(block_products([whole[:cut], whole[cut:]])))
 
 
-def early_products(side, order_ref, sorted_ref, ready_ref, compliance_ref, own0_ref, own1_ref, *refs):
+def early_products(stage, order_ref, sorted_ref, count_ref, compliance_ref, own0_ref, own1_ref, *refs):
     out_ref, half_ref = refs[-2:]
-    group = out_ref.shape[0]
     faces = compliance_ref.shape[0]
+    group = faces // 2
     *starts, mine = position(group)
     none = half_ref.shape[0] - 1
     half_ref[none] = jnp.zeros_like(half_ref[none])
     for start, ref in zip(starts, (own0_ref, own1_ref)):
         half_ref[pl.ds(mine * faces + start, group)] = ref[...]
-    for ref in refs[:side]:
-        half_ref[pl.ds((1 - mine) * faces + starts[0], group)] = ref[...]
+    if stage:
+        half_ref[pl.ds((1 - mine) * faces + starts[0], group)] = refs[0][...]
 
     def entries(face):
-        ready = ready_ref[face, 0, 0]
+        count = count_ref[face, 0, 0]
         return [
-            (half_ref[jnp.where(slot < ready, sorted_ref[face, 0, slot], none)], compliance_ref[face, order_ref[face, 0, slot]])
-            for slot in range(EARLY[side])
+            (half_ref[jnp.where(slot < count, sorted_ref[face, 0, slot], none)], compliance_ref[face, order_ref[face, 0, slot]])
+            for slot in range(EARLY[stage], EARLY[stage + 1])
         ]
 
-    def finish(index, product):
-        out_ref[index] = product
-
-    group_products(starts[side], group, entries, finish)
-
-
-def late_products(first, done, order_ref, sorted_ref, ready_ref, compliance_ref, half_ref, finish, out_ref):
+    for side in range(2):
+        def finish(index, product):
+            place = side * group + index
+            out_ref[place] = refs[1][place] + product if stage else product
+
+        group_products(starts[side], group, entries, finish)
+
+
+def late_products(first, done, order_ref, sorted_ref, compliance_ref, half_ref, finish):
     group, stored = compliance_ref.shape[0] // 2, compliance_ref.shape[1]
 
-    def entry(face, slot):
-        return half_ref[sorted_ref[face, 0, slot]], compliance_ref[face, order_ref[face, 0, slot]]
-
-    group_products(first, group, lambda face: [entry(face, slot) for slot in range(done, stored)], finish)
-
-    if not done:
-        return
+    def entries(face):
+        return [
+            (half_ref[sorted_ref[face, 0, slot]], compliance_ref[face, order_ref[face, 0, slot]]) for slot in range(done, stored)
+        ]
+
+    group_products(first, group, entries, finish)
+
+
+def missed_products(first, order_ref, sorted_ref, own_ref, ready_ref, compliance_ref, half_ref, out_ref):
+    group = out_ref.shape[0]
 
     def missed(slot, index):
-        out_ref[index] -= 2.0 * block_products([[entry(first + index, slot)]])[0]
+        face = first + index
+        entry = (half_ref[sorted_ref[face, 0, slot]], compliance_ref[face, order_ref[face, 0, slot]])
+        out_ref[index] -= 2.0 * block_products([[entry]])[0]
         return index
 
-    least = ready_ref[first, 0, 0]
-    for index in range(1, group):
-        least = jnp.minimum(least, ready_ref[first + index, 0, 0])
-
-    @pl.when(least < done)
+    spare = jnp.int32(0)
+    for index in range(group):
+        spare = jnp.minimum(spare, own_ref[first + index, 0, 0] - EARLY[1])
+        spare = jnp.minimum(spare, ready_ref[first + index, 0, 0] - EARLY[2])
+
+    @pl.when(spare < 0)
     def _():
         for index in range(group):
-            lax.fori_loop(ready_ref[first + index, 0, 0], done, missed, index)
-
-
-def first_section(side, order_ref, sorted_ref, ready_ref, compliance_ref, own_ref, other_ref, motion_ref, stress_ref,
+            lax.fori_loop(own_ref[first + index, 0, 0], EARLY[1], missed, index)
+            lax.fori_loop(jnp.maximum(ready_ref[first + index, 0, 0], EARLY[1]), EARLY[2], missed, index)
+
+
+def first_section(side, order_ref, sorted_ref, compliance_ref, own_ref, other_ref, motion_ref, stress_ref,
                   load_ref, stiff_ref, record_ref, out_ref, half_ref):
     faces, _, extent, _ = compliance_ref.shape
     group = faces // 2
@@ -171,10 +181,10 @@
 
     for plane in range(group, out_ref.shape[0]):
         out_ref[plane] = jnp.zeros_like(out_ref[plane])
-    late_products(first, 0, order_ref, sorted_ref, ready_ref, compliance_ref, half_ref, finish, out_ref)
-
-
-def linear_section(side, order_ref, sorted_ref, ready_ref, compliance_ref, own0_ref, own1_ref, other0_ref, other1_ref,
+    late_products(first, 0, order_ref, sorted_ref, compliance_ref, half_ref, finish)
+
+
+def linear_section(side, order_ref, sorted_ref, count_ref, ready_ref, compliance_ref, own0_ref, own1_ref, other0_ref, other1_ref,
                    robin_ref, load_ref, early_ref, out_ref, sent_ref, half_ref):
     group, _, extent = own0_ref.shape
     faces = compliance_ref.shape[0]
@@ -185,10 +195,11 @@
             half_ref[pl.ds(run * faces + start, group)] = ref[...]
 
     def finish(index, product):
-        response = early_ref[index] + product + load_ref[:, lanes_of(first + index, extent)].astype(jnp.float32)
+        response = early_ref[side * group + index] + product + load_ref[:, lanes_of(first + index, extent)].astype(jnp.float32)
         out_ref[index] = robin_ref[index] - 2.0 * response
 
-    late_products(first, EARLY[side], order_ref, sorted_ref, ready_ref, compliance_ref, half_ref, finish, out_ref)
+    late_products(first, EARLY[2], order_ref, sorted_ref, compliance_ref, half_ref, finish)
+    missed_products(first, order_ref, sorted_ref, count_ref, ready_ref, compliance_ref, half_ref, out_ref)
     encode(out_ref, sent_ref)
 
 
@@ -370,20 +381,20 @@
     in_hbm = functools.partial(pltpu.with_memory_space_constraint, memory_space=pltpu.HBM)
     own = (start_traction[0].astype(jnp.float32) + starting_motion[0].astype(jnp.float32)).astype(jnp.bfloat16)
     other = lax.ppermute(own, "row", swap)
-    in_smem = [pltpu.SMEM((faces, 1, width), jnp.int32) for width in (stored, stored, 1)]
-    in_vmem = [pltpu.VMEM((faces, 1, width), jnp.int32) for width in (stored, stored, stored, 1)]
+    in_smem = [pltpu.SMEM((faces, 1, width), jnp.int32) for width in (stored, stored, 1, 1)]
+    in_vmem = [pltpu.VMEM((faces, 1, width), jnp.int32) for width in (stored, stored, stored, 1, 1)]
     blocks, load, motion, stress, stiff, record, turn, *tables = call(
         fetch, [HBM] * 9,
         (pltpu.VMEM((faces, stored, extent, extent), jnp.bfloat16), bf16(*flat), bf16(*flat), bf16(*flat),
          f32(1, faces * extent), f32(1, faces * extent), s32(1, faces * extent), pltpu.SMEM((1, faces), jnp.int32), *in_smem),
-        in_vmem + [pltpu.SemaphoreType.DMA((11 + faces,))],
-        block_bytes, (VMEM,) * 7 + (SMEM,) * 4,
+        in_vmem + [pltpu.SemaphoreType.DMA((12 + faces,))],
+        block_bytes, (VMEM,) * 7 + (SMEM,) * 5,
     )(
         in_hbm(compliance[0]), in_hbm(load_response[0]), in_hbm(starting_motion[0]), in_hbm(start_traction[0]),
         in_hbm(stiffness), in_hbm(history), in_hbm(orientation.reshape(1, -1)),
         in_hbm(jnp.transpose(block_columns, (1, 0, 2))), in_hbm(face_partner),
     )
-    partner, order, columns, ready = (pltpu.with_memory_space_constraint(value, pltpu.SMEM) for value in tables)
+    partner, order, columns, owned, ready = (pltpu.with_memory_space_constraint(value, pltpu.SMEM) for value in tables)
 
     robin, half = [None, None], [None, None]
     stiffs, records = [stiff, stiff], [record, record]
@@ -391,24 +402,26 @@
         begin, last = iteration == 0, iteration == ITERS - 1
         if not begin:
             other = [lax.ppermute(half[side], "row", swap) for side in range(2)]
-        ascent, mates, early = [None, None], [None, None], []
-        for side in range(0 if begin else 2):
-            early.append(call(
-                functools.partial(early_products, side), [SMEM] * 3 + [VMEM] * (3 + side) + [ANY] * side, f32(*part),
+        ascent, mates = [None, None], [None, None]
+        early = ()
+        for stage in range(0 if begin else 2):
+            late = (other[0], early) if stage else ()
+            early = call(
+                functools.partial(early_products, stage), [SMEM] * 3 + [VMEM] * (3 + len(late)), f32(faces, times, extent),
                 [pltpu.VMEM((rows * faces + 1, times, extent), jnp.bfloat16)], block_bytes,
-            )(order, columns, ready, blocks, *half, *other[:side], *early))
+            )(order, columns, (owned, ready)[stage], blocks, *half, *late)
         for side, (axes, pairs) in enumerate((("sub", near_pairs), (("sub", "row"), far_pairs))):
             if begin:
                 ascent[side] = sent = call(
-                    functools.partial(first_section, side), [SMEM] * 3 + [VMEM] * 8,
+                    functools.partial(first_section, side), [SMEM] * 2 + [VMEM] * 8,
                     f32(group + 1 + side, times, extent), [halves], 2 * block_bytes,
-                )(order, columns, ready, blocks, own, other, motion, stress, load, stiff, record)
+                )(order, columns, blocks, own, other, motion, stress, load, stiff, record)
             else:
                 ascent[side], sent = call(
-                    functools.partial(linear_section, side), [SMEM] * 3 + [VMEM] * 8,
+                    functools.partial(linear_section, side), [SMEM] * 4 + [VMEM] * 8,
                     (f32(*part), jax.ShapeDtypeStruct((group + 1 + side, times, extent), jnp.int16)),
                     [halves], 2 * block_bytes,
-                )(order, columns, ready, blocks, *half, *other, robin[side], load, early[side])
+                )(order, columns, owned, ready, blocks, *half, *other, robin[side], load, early)
             mates[side] = lax.ppermute(sent, axes, pairs)
         outs = ()
         for side in range(2):

time: 41 us -> 40.6 us (level)
  Pallas kernels: 18.8 us -> 18.2 us
  starting transfers between devices: 12.5 us -> 13 us
  waiting for transfers between devices: 7.84 us -> 7.34 us
    pallas_call x10, Pallas kernels: 12 us -> 11.3 us  [the longest x4 3.95 us: shards(): call(functools.partial(early_products, stage), [SMEM] * 3 + [VMEM] * (3 +...]
    ppermute x4, waiting for transfers between devices: 4.16 us -> 3.53 us  [shards(): other = [lax.ppermute(half[side], 'row', swap) for side in range(2)]]
    ppermute x6, starting transfers between devices: 5.14 us -> 5.62 us  [shards(): mates[side] = lax.ppermute(sent, axes, pairs)]
  transfers between devices with their start and end apart: 11 -> 11, of which waited for: 8 -> 8; matrix products, arithmetic and copies ran while one was open for 0% -> 0% of each run, Pallas kernels for 33% -> 34%
where the time goes in v5:
time: 40.6 us; the launch traced here: 40.2 us
  Pallas kernels  18.2 us (45%)
  starting transfers between devices  13 us (32%)
  waiting for transfers between devices  7.34 us (18%)
  other arithmetic  1.02 us (3%)
  between operations  0.77 us (2%)
    ppermute x6, starting transfers between devices, shards(): mates[side] = lax.ppermute(sent, axes, pairs)  5.62 us
    pallas_call x1, Pallas kernels, shards(): call(fetch, [HBM] * 9, (pltpu.VMEM((faces, stored, extent, extent), jnp.b...  4.58 us
    ppermute x4, starting transfers between devices, shards(): other = [lax.ppermute(half[side], 'row', swap) for side in range(2)]  4.33 us
    pallas_call x4, Pallas kernels, shards(): call(functools.partial(early_products, stage), [SMEM] * 3 + [VMEM] * (3 +...  3.95 us
    pallas_call x4, Pallas kernels, shards(): call(functools.partial(linear_section, side), [SMEM] * 4 + [VMEM] * 8, (f...  3.9 us
    ppermute x6, waiting for transfers between devices, shards(): mates[side] = lax.ppermute(sent, axes, pairs)  3.81 us
    ppermute x4, waiting for transfers between devices, shards(): other = [lax.ppermute(half[side], 'row', swap) for side in range(2)]  3.53 us
    pallas_call x2, Pallas kernels, shards(): call(functools.partial(first_section, side), [SMEM] * 2 + [VMEM] * 8, f32...  3.51 us
  transfers between devices with their start and end apart: 11, of which 8 were waited for; matrix products, arithmetic and copies ran while one was open for 0% of the time, Pallas kernels for 34%

profile of v5, /device:TPU:0, one launch (start us, length us, event | category | flops | bytes accessed | tf_op | source)
XLA Modules:
  0.0 40.2 jit_solution(4322736222973591449)
XLA Ops:
  0.6 1.0 %add_convert_fusion.own_ref = bf16[32,2304]{1,0:T(8,128)(2,1)S(1)} fusion(bf16[1,32,2304]{2,1,0:T(8,128)(2,1)} %param.13, bf16[1,32,2304]{2,1,0:T(8,128)(2,1)} %param.12), kind=kLoop, calls=%fused_computation | loop fusion | flops 294912 | bytes 442368 | tf_op jit(solution)/shard_map/convert_element_type | solution.py:382
  1.7 3.0 %collective-permute-start = (bf16[32,2304]{1,0:T(8,128)(2,1)S(1)}, bf16[32,2304]{1,0:T(8,128)(2,1)S(1)}, u32[]{:S(2)}, u32[]{:S(2)}) collective-permute-start(bf16[32,2304]{1,0:T(8,128)(2,1)S(1)} %add_convert_fusion.own_ref), channel_id=1, source_target_pairs={{0,1},{1,0},{2,3},{3,2},{4,5},{5,4},{6,7},{7,6},{8,9},{9,8},{10,11... | collective-permute-start | bytes 442376 | tf_op jit(solution)/shard_map/ppermute | solution.py:383
  4.7 4.6 %shard_map.104 = (bf16[18,18,128,128]{3,2,1,0:T(8,128)(2,1)S(1)}, bf16[32,2304]{1,0:T(8,128)(2,1)S(1)}, bf16[32,2304]{1,0:T(8,128)(2,1)S(1)}, bf16[32,2304]{1,0:...) custom-call(bf16[18,18,128,128]{3,2,1,0:T(8,128)(2,1)} %bitcast.10, ...), custom_call_target="tpu_custom_call" | custom-call | flops 10616832 | bytes 10616832 | tf_op jit(solution)/shard_map/pallas_call | solution.py:386
  9.3 1.8 %shard_map.107.own_ref = f32[11,32,128]{2,1,0:T(8,128)S(1)} custom-call(s32[18,1,18]{2,1,0:T(1,128)S(4)} %get-tuple-element.40.order_ref, s32[18,1,18]{2,1,0:T(1,128)S(4)} %get-tuple-element.41.sorted_ref, bf16[18,18,128,128]{3,2,1,0:T(8,128)(2,1)S(1)} %get-tuple-element.44.compliance_ref, bf16[32,2304]{1,0:T(8,128)(2,1)S(1)} %add_convert_fusion.own_ref, ...), custom_call_target="tpu_custom_call" | custom-call | flops 21233664 | bytes 21233664 | tf_op jit(solution)/shard_map/pallas_call | solution.py:415
  11.0 1.0 %collective-permute-start.2 = (f32[11,32,128]{2,1,0:T(8,128)S(1)}, f32[11,32,128]{2,1,0:T(8,128)S(1)}, u32[]{:S(2)}, u32[]{:S(2)}) collective-permute-start(f32[11,32,128]{2,1,0:T(8,128)S(1)} %shard_map.107.own_ref), channel_id=1, source_target_pairs={{0,1},{1,0},{2,4},{3,5},{4,2},{5,3},{6,8},{7,9},{8,6},{9,7},{10,12... | collective-permute-start | bytes 540680 | tf_op jit(solution)/shard_map/ppermute | solution.py:425
  12.1 1.7 %shard_map.105.own_ref = f32[10,32,128]{2,1,0:T(8,128)S(1)} custom-call(s32[18,1,18]{2,1,0:T(1,128)S(4)} %get-tuple-element.40.order_ref, s32[18,1,18]{2,1,0:T(1,128)S(4)} %get-tuple-element.41.sorted_ref, bf16[18,18,128,128]{3,2,1,0:T(8,128)(2,1)S(1)} %get-tuple-element.44.compliance_ref, bf16[32,2304]{1,0:T(8,128)(2,1)S(1)} %add_convert_fusion.own_ref, ...), custom_call_target="tpu_custom_call" | custom-call | flops 21233664 | bytes 21233664 | tf_op jit(solution)/shard_map/pallas_call | solution.py:415
  13.8 0.7 %collective-permute-start.1 = (f32[10,32,128]{2,1,0:T(8,128)S(1)}, f32[10,32,128]{2,1,0:T(8,128)S(1)}, u32[]{:S(2)}, u32[]{:S(2)}) collective-permute-start(f32[10,32,128]{2,1,0:T(8,128)S(1)} %shard_map.105.own_ref), channel_id=1, source_target_pairs={{0,2},{2,0},{4,6},{6,4},{8,10},{10,8},{12,14},{14,12},{16,18},{18,... | collective-permute-start | bytes 491528 | tf_op jit(solution)/shard_map/ppermute | solution.py:425
  14.6 1.0 %collective-permute-done.1.mate_ref = f32[10,32,128]{2,1,0:T(8,128)S(1)} collective-permute-done((f32[10,32,128]{2,1,0:T(8,128)S(1)}, f32[10,32,128]{2,1,0:T(8,128)S(1)}, u32[]{:S(2)}, u32[]{:S(2)}) %collective-permute-start.1) | collective-permute-done | bytes 163872 | tf_op jit(solution)/shard_map/ppermute | solution.py:425
  15.8 1.1 %collective-permute-start.3 = (bf16[9,32,128]{2,1,0:T(8,128)(2,1)S(1)}, bf16[9,32,128]{2,1,0:T(8,128)(2,1)S(1)}, u32[]{:S(2)}, u32[]{:S(2)}) collective-permute-start(bf16[9,32,128]{2,1,0:T(8,128)(2,1)S(1)} %get-tuple-element.50.own0_ref), channel_id=1, source_target_pairs={{0,1},{1,0},{2,3},{3,2},{4,5},{5,4},{6,7},{7,6},{8,9},{9,8},{10,11... | collective-permute-start | bytes 221192 | tf_op jit(solution)/shard_map/ppermute | solution.py:404
  16.9 0.3 shard_map.108
  17.2 1.1 %collective-permute-start.4 = (bf16[9,32,128]{2,1,0:T(8,128)(2,1)S(1)}, bf16[9,32,128]{2,1,0:T(8,128)(2,1)S(1)}, u32[]{:S(2)}, u32[]{:S(2)}) collective-permute-start(bf16[9,32,128]{2,1,0:T(8,128)(2,1)S(1)} %get-tuple-element.51.own1_ref), channel_id=1, source_target_pairs={{0,1},{1,0},{2,3},{3,2},{4,5},{5,4},{6,7},{7,6},{8,9},{9,8},{10,11... | collective-permute-start | bytes 221192 | tf_op jit(solution)/shard_map/ppermute | solution.py:404
  18.3 1.1 %shard_map.109.refs_1_ = f32[18,32,128]{2,1,0:T(8,128)S(1)} custom-call(s32[18,1,18]{2,1,0:T(1,128)S(4)} %get-tuple-element.40.order_ref, s32[18,1,18]{2,1,0:T(1,128)S(4)} %get-tuple-element.41.sorted_ref, s32[18,1,1]{2,1,0:T(1,128)S(4)} %get-tuple-element.42.count_ref, bf16[18,18,128,128]{3,2,1,0:T(8,128)(2,1)S(1)} %get-tuple-element.44.compliance_ref, ...), custom_call_target="tpu_custom_call" | custom-call | flops 10616832 | bytes 10616832 | tf_op jit(solution)/shard_map/pallas_call | solution.py:409
  19.4 1.5 %collective-permute-done.3.refs_0_.other0_ref = bf16[9,32,128]{2,1,0:T(8,128)(2,1)S(1)} collective-permute-done((bf16[9,32,128]{2,1,0:T(8,128)(2,1)S(1)}, bf16[9,32,128]{2,1,0:T(8,128)(2,1)S(1)}, u32[]{:S(2)}, u32[]{:S(2)}) %collective-permute-start.3) | collective-permute-done | bytes 73760 | tf_op jit(solution)/shard_map/ppermute | solution.py:404
  20.9 0.8 %shard_map.110.early_ref = f32[18,32,128]{2,1,0:T(8,128)S(1)} custom-call(s32[18,1,18]{2,1,0:T(1,128)S(4)} %get-tuple-element.40.order_ref, s32[18,1,18]{2,1,0:T(1,128)S(4)} %get-tuple-element.41.sorted_ref, s32[18,1,1]{2,1,0:T(1,128)S(4)} %get-tuple-element.43.count_ref.ready_ref, bf16[18,18,128,128]{3,2,1,0:T(8,128)(2,1)S(1)} %get-tuple-element.44.compliance_ref, ...), custom_call_target="tpu_custom_call" | custom-call | flops 10616832 | bytes 10616832 | tf_op jit(solution)/shard_map/pallas_call | solution.py:409
  21.8 0.3 collective-permute-done.4.other1_ref
  22.0 1.0 %shard_map.113 = (f32[9,32,128]{2,1,0:T(8,128)S(1)}, s16[11,32,128]{2,1,0:T(8,128)(2,1)S(1)}) custom-call(s32[18,1,18]{2,1,0:T(1,128)S(4)} %get-tuple-element.40.order_ref, s32[18,1,18]{2,1,0:T(1,128)S(4)} %get-tuple-element.41.sorted_ref, s32[18,1,1]{2,1,0:T(1,128)S(4)} %get-tuple-element.42.count_ref, ...), custom_call_target="tpu_custom_call" | custom-call | flops 21233664 | bytes 21233664 | tf_op jit(solution)/shard_map/pallas_call | solution.py:420
  23.0 1.0 %collective-permute-start.6 = (s16[11,32,128]{2,1,0:T(8,128)(2,1)S(1)}, s16[11,32,128]{2,1,0:T(8,128)(2,1)S(1)}, u32[]{:S(2)}, u32[]{:S(2)}) collective-permute-start(s16[11,32,128]{2,1,0:T(8,128)(2,1)S(1)} %get-tuple-element.60), channel_id=1, source_target_pairs={{0,1},{1,0},{2,4},{3,5},{4,2},{5,3},{6,8},{7,9},{8,6},{9,7},{10,12... | collective-permute-start | bytes 270344 | tf_op jit(solution)/shard_map/ppermute | solution.py:425
  24.0 1.0 %shard_map.111 = (f32[9,32,128]{2,1,0:T(8,128)S(1)}, s16[10,32,128]{2,1,0:T(8,128)(2,1)S(1)}) custom-call(s32[18,1,18]{2,1,0:T(1,128)S(4)} %get-tuple-element.40.order_ref, s32[18,1,18]{2,1,0:T(1,128)S(4)} %get-tuple-element.41.sorted_ref, s32[18,1,1]{2,1,0:T(1,128)S(4)} %get-tuple-element.42.count_ref, ...), custom_call_target="tpu_custom_call" | custom-call | flops 21233664 | bytes 21233664 | tf_op jit(solution)/shard_map/pallas_call | solution.py:420
  25.0 1.3 %collective-permute-start.5 = (s16[10,32,128]{2,1,0:T(8,128)(2,1)S(1)}, s16[10,32,128]{2,1,0:T(8,128)(2,1)S(1)}, u32[]{:S(2)}, u32[]{:S(2)}) collective-permute-start(s16[10,32,128]{2,1,0:T(8,128)(2,1)S(1)} %get-tuple-element.54), channel_id=1, source_target_pairs={{0,2},{2,0},{4,6},{6,4},{8,10},{10,8},{12,14},{14,12},{16,18},{18,... | collective-permute-start | bytes 245768 | tf_op jit(solution)/shard_map/ppermute | solution.py:425
  26.4 0.9 %collective-permute-done.5.refs_3_ = s16[10,32,128]{2,1,0:T(8,128)(2,1)S(1)} collective-permute-done((s16[10,32,128]{2,1,0:T(8,128)(2,1)S(1)}, s16[10,32,128]{2,1,0:T(8,128)(2,1)S(1)}, u32[]{:S(2)}, u32[]{:S(2)}) %collective-permute-start.5) | collective-permute-done | bytes 81952 | tf_op jit(solution)/shard_map/ppermute | solution.py:425
  27.5 1.0 %collective-permute-start.7 = (bf16[9,32,128]{2,1,0:T(8,128)(2,1)S(1)}, bf16[9,32,128]{2,1,0:T(8,128)(2,1)S(1)}, u32[]{:S(2)}, u32[]{:S(2)}) collective-permute-start(bf16[9,32,128]{2,1,0:T(8,128)(2,1)S(1)} %get-tuple-element.57.own0_ref), channel_id=1, source_target_pairs={{0,1},{1,0},{2,3},{3,2},{4,5},{5,4},{6,7},{7,6},{8,9},{9,8},{10,11... | collective-permute-start | bytes 221192 | tf_op jit(solution)/shard_map/ppermute | solution.py:404
  28.9 1.1 %collective-permute-start.8 = (bf16[9,32,128]{2,1,0:T(8,128)(2,1)S(1)}, bf16[9,32,128]{2,1,0:T(8,128)(2,1)S(1)}, u32[]{:S(2)}, u32[]{:S(2)}) collective-permute-start(bf16[9,32,128]{2,1,0:T(8,128)(2,1)S(1)} %get-tuple-element.63.own1_ref), channel_id=1, source_target_pairs={{0,1},{1,0},{2,3},{3,2},{4,5},{5,4},{6,7},{7,6},{8,9},{9,8},{10,11... | collective-permute-start | bytes 221192 | tf_op jit(solution)/shard_map/ppermute | solution.py:404
  30.0 1.1 %shard_map.115.refs_1_ = f32[18,32,128]{2,1,0:T(8,128)S(1)} custom-call(s32[18,1,18]{2,1,0:T(1,128)S(4)} %get-tuple-element.40.order_ref, s32[18,1,18]{2,1,0:T(1,128)S(4)} %get-tuple-element.41.sorted_ref, s32[18,1,1]{2,1,0:T(1,128)S(4)} %get-tuple-element.42.count_ref, bf16[18,18,128,128]{3,2,1,0:T(8,128)(2,1)S(1)} %get-tuple-element.44.compliance_ref, ...), custom_call_target="tpu_custom_call" | custom-call | flops 10616832 | bytes 10616832 | tf_op jit(solution)/shard_map/pallas_call | solution.py:409
  31.1 1.6 %collective-permute-done.7.refs_0_.other0_ref = bf16[9,32,128]{2,1,0:T(8,128)(2,1)S(1)} collective-permute-done((bf16[9,32,128]{2,1,0:T(8,128)(2,1)S(1)}, bf16[9,32,128]{2,1,0:T(8,128)(2,1)S(1)}, u32[]{:S(2)}, u32[]{:S(2)}) %collective-permute-start.7) | collective-permute-done | bytes 73760 | tf_op jit(solution)/shard_map/ppermute | solution.py:404
  32.7 0.8 %shard_map.116.early_ref = f32[18,32,128]{2,1,0:T(8,128)S(1)} custom-call(s32[18,1,18]{2,1,0:T(1,128)S(4)} %get-tuple-element.40.order_ref, s32[18,1,18]{2,1,0:T(1,128)S(4)} %get-tuple-element.41.sorted_ref, s32[18,1,1]{2,1,0:T(1,128)S(4)} %get-tuple-element.43.count_ref.ready_ref, bf16[18,18,128,128]{3,2,1,0:T(8,128)(2,1)S(1)} %get-tuple-element.44.compliance_ref, ...), custom_call_target="tpu_custom_call" | custom-call | flops 10616832 | bytes 10616832 | tf_op jit(solution)/shard_map/pallas_call | solution.py:409
  33.7 1.0 %shard_map.117 = (f32[9,32,128]{2,1,0:T(8,128)S(1)}, s16[11,32,128]{2,1,0:T(8,128)(2,1)S(1)}) custom-call(s32[18,1,18]{2,1,0:T(1,128)S(4)} %get-tuple-element.40.order_ref, s32[18,1,18]{2,1,0:T(1,128)S(4)} %get-tuple-element.41.sorted_ref, s32[18,1,1]{2,1,0:T(1,128)S(4)} %get-tuple-element.42.count_ref, ...), custom_call_target="tpu_custom_call" | custom-call | flops 21233664 | bytes 21233664 | tf_op jit(solution)/shard_map/pallas_call | solution.py:420
  34.7 1.0 %collective-permute-start.9 = (s16[11,32,128]{2,1,0:T(8,128)(2,1)S(1)}, s16[11,32,128]{2,1,0:T(8,128)(2,1)S(1)}, u32[]{:S(2)}, u32[]{:S(2)}) collective-permute-start(s16[11,32,128]{2,1,0:T(8,128)(2,1)S(1)} %get-tuple-element.66), channel_id=1, source_target_pairs={{0,1},{1,0},{2,4},{3,5},{4,2},{5,3},{6,8},{7,9},{8,6},{9,7},{10,12... | collective-permute-start | bytes 270344 | tf_op jit(solution)/shard_map/ppermute | solution.py:425
  35.7 1.0 %shard_map.118 = (f32[9,32,128]{2,1,0:T(8,128)S(1)}, s16[10,32,128]{2,1,0:T(8,128)(2,1)S(1)}) custom-call(s32[18,1,18]{2,1,0:T(1,128)S(4)} %get-tuple-element.40.order_ref, s32[18,1,18]{2,1,0:T(1,128)S(4)} %get-tuple-element.41.sorted_ref, s32[18,1,1]{2,1,0:T(1,128)S(4)} %get-tuple-element.42.count_ref, ...), custom_call_target="tpu_custom_call" | custom-call | flops 21233664 | bytes 21233664 | tf_op jit(solution)/shard_map/pallas_call | solution.py:420
  36.7 0.4 %collective-permute-start.10 = (s16[10,32,128]{2,1,0:T(8,128)(2,1)S(1)}, s16[10,32,128]{2,1,0:T(8,128)(2,1)S(1)}, u32[]{:S(2)}, u32[]{:S(2)}) collective-permute-start(s16[10,32,128]{2,1,0:T(8,128)(2,1)S(1)} %get-tuple-element.69), channel_id=1, source_target_pairs={{0,2},{2,0},{4,6},{6,4},{8,10},{10,8},{12,14},{14,12},{16,18},{18,... | collective-permute-start | bytes 245768 | tf_op jit(solution)/shard_map/ppermute | solution.py:425
  37.2 0.9 %collective-permute-done.10.refs_3_ = s16[10,32,128]{2,1,0:T(8,128)(2,1)S(1)} collective-permute-done((s16[10,32,128]{2,1,0:T(8,128)(2,1)S(1)}, s16[10,32,128]{2,1,0:T(8,128)(2,1)S(1)}, u32[]{:S(2)}, u32[]{:S(2)}) %collective-permute-start.10) | collective-permute-done | bytes 81952 | tf_op jit(solution)/shard_map/ppermute | solution.py:425
  38.4 0.9 %collective-permute-done.9.refs_3_ = s16[11,32,128]{2,1,0:T(8,128)(2,1)S(1)} collective-permute-done((s16[11,32,128]{2,1,0:T(8,128)(2,1)S(1)}, s16[11,32,128]{2,1,0:T(8,128)(2,1)S(1)}, u32[]{:S(2)}, u32[]{:S(2)}) %collective-permute-start.9) | collective-permute-done | bytes 90144 | tf_op jit(solution)/shard_map/ppermute | solution.py:425
  39.3 1.0 %shard_map.120 = (bf16[32,2304]{1,0:T(8,128)(2,1)}, bf16[32,2304]{1,0:T(8,128)(2,1)}) custom-call(s32[1,18]{1,0:T(1,128)S(4)} %get-tuple-element.38.partner_ref.refs_0_, s32[1,2304]{1,0:T(1,128)S(1)} %get-tuple-element.39.turn_ref.refs_1_, f32[9,32,128]{2,1,0:T(8,128)S(1)} %get-tuple-element.65.refs_2_, ...), custom_call_target="tpu_custom_call" | custom-call | tf_op jit(solution)/shard_map/pallas_call | solution.py:442
  (8 shorter events, 1.2 us)
Async XLA Ops:
  1.7 7.6 %collective-permute-start = (bf16[32,2304]{1,0:T(8,128)(2,1)S(1)}, bf16[32,2304]{1,0:T(8,128)(2,1)S(1)}, u32[]{:S(2)}, u32[]{:S(2)}) collective-permute-start(bf16[32,2304]{1,0:T(8,128)(2,1)S(1)} %add_convert_fusion.own_ref), channel_id=1, source_target_pairs={{0,1},{1,0},{2,3},{3,2},{4,5},{5,4},{6,7},{7,6},{8,9},{9,8},{10,11... | collective-permute-start | bytes 442376 | tf_op jit(solution)/shard_map/ppermute | solution.py:383
  11.0 5.9 %collective-permute-start.2 = (f32[11,32,128]{2,1,0:T(8,128)S(1)}, f32[11,32,128]{2,1,0:T(8,128)S(1)}, u32[]{:S(2)}, u32[]{:S(2)}) collective-permute-start(f32[11,32,128]{2,1,0:T(8,128)S(1)} %shard_map.107.own_ref), channel_id=1, source_target_pairs={{0,1},{1,0},{2,4},{3,5},{4,2},{5,3},{6,8},{7,9},{8,6},{9,7},{10,12... | collective-permute-start | bytes 540680 | tf_op jit(solution)/shard_map/ppermute | solution.py:425
  13.8 1.7 %collective-permute-start.1 = (f32[10,32,128]{2,1,0:T(8,128)S(1)}, f32[10,32,128]{2,1,0:T(8,128)S(1)}, u32[]{:S(2)}, u32[]{:S(2)}) collective-permute-start(f32[10,32,128]{2,1,0:T(8,128)S(1)} %shard_map.105.own_ref), channel_id=1, source_target_pairs={{0,2},{2,0},{4,6},{6,4},{8,10},{10,8},{12,14},{14,12},{16,18},{18,... | collective-permute-start | bytes 491528 | tf_op jit(solution)/shard_map/ppermute | solution.py:425
  15.8 5.1 %collective-permute-start.3 = (bf16[9,32,128]{2,1,0:T(8,128)(2,1)S(1)}, bf16[9,32,128]{2,1,0:T(8,128)(2,1)S(1)}, u32[]{:S(2)}, u32[]{:S(2)}) collective-permute-start(bf16[9,32,128]{2,1,0:T(8,128)(2,1)S(1)} %get-tuple-element.50.own0_ref), channel_id=1, source_target_pairs={{0,1},{1,0},{2,3},{3,2},{4,5},{5,4},{6,7},{7,6},{8,9},{9,8},{10,11... | collective-permute-start | bytes 221192 | tf_op jit(solution)/shard_map/ppermute | solution.py:404
  17.2 4.9 %collective-permute-start.4 = (bf16[9,32,128]{2,1,0:T(8,128)(2,1)S(1)}, bf16[9,32,128]{2,1,0:T(8,128)(2,1)S(1)}, u32[]{:S(2)}, u32[]{:S(2)}) collective-permute-start(bf16[9,32,128]{2,1,0:T(8,128)(2,1)S(1)} %get-tuple-element.51.own1_ref), channel_id=1, source_target_pairs={{0,1},{1,0},{2,3},{3,2},{4,5},{5,4},{6,7},{7,6},{8,9},{9,8},{10,11... | collective-permute-start | bytes 221192 | tf_op jit(solution)/shard_map/ppermute | solution.py:404
  23.0 5.6 %collective-permute-start.6 = (s16[11,32,128]{2,1,0:T(8,128)(2,1)S(1)}, s16[11,32,128]{2,1,0:T(8,128)(2,1)S(1)}, u32[]{:S(2)}, u32[]{:S(2)}) collective-permute-start(s16[11,32,128]{2,1,0:T(8,128)(2,1)S(1)} %get-tuple-element.60), channel_id=1, source_target_pairs={{0,1},{1,0},{2,4},{3,5},{4,2},{5,3},{6,8},{7,9},{8,6},{9,7},{10,12... | collective-permute-start | bytes 270344 | tf_op jit(solution)/shard_map/ppermute | solution.py:425
  25.0 2.3 %collective-permute-start.5 = (s16[10,32,128]{2,1,0:T(8,128)(2,1)S(1)}, s16[10,32,128]{2,1,0:T(8,128)(2,1)S(1)}, u32[]{:S(2)}, u32[]{:S(2)}) collective-permute-start(s16[10,32,128]{2,1,0:T(8,128)(2,1)S(1)} %get-tuple-element.54), channel_id=1, source_target_pairs={{0,2},{2,0},{4,6},{6,4},{8,10},{10,8},{12,14},{14,12},{16,18},{18,... | collective-permute-start | bytes 245768 | tf_op jit(solution)/shard_map/ppermute | solution.py:425
  27.5 5.1 %collective-permute-start.7 = (bf16[9,32,128]{2,1,0:T(8,128)(2,1)S(1)}, bf16[9,32,128]{2,1,0:T(8,128)(2,1)S(1)}, u32[]{:S(2)}, u32[]{:S(2)}) collective-permute-start(bf16[9,32,128]{2,1,0:T(8,128)(2,1)S(1)} %get-tuple-element.57.own0_ref), channel_id=1, source_target_pairs={{0,1},{1,0},{2,3},{3,2},{4,5},{5,4},{6,7},{7,6},{8,9},{9,8},{10,11... | collective-permute-start | bytes 221192 | tf_op jit(solution)/shard_map/ppermute | solution.py:404
  28.9 4.9 %collective-permute-start.8 = (bf16[9,32,128]{2,1,0:T(8,128)(2,1)S(1)}, bf16[9,32,128]{2,1,0:T(8,128)(2,1)S(1)}, u32[]{:S(2)}, u32[]{:S(2)}) collective-permute-start(bf16[9,32,128]{2,1,0:T(8,128)(2,1)S(1)} %get-tuple-element.63.own1_ref), channel_id=1, source_target_pairs={{0,1},{1,0},{2,3},{3,2},{4,5},{5,4},{6,7},{7,6},{8,9},{9,8},{10,11... | collective-permute-start | bytes 221192 | tf_op jit(solution)/shard_map/ppermute | solution.py:404
  34.7 4.6 %collective-permute-start.9 = (s16[11,32,128]{2,1,0:T(8,128)(2,1)S(1)}, s16[11,32,128]{2,1,0:T(8,128)(2,1)S(1)}, u32[]{:S(2)}, u32[]{:S(2)}) collective-permute-start(s16[11,32,128]{2,1,0:T(8,128)(2,1)S(1)} %get-tuple-element.66), channel_id=1, source_target_pairs={{0,1},{1,0},{2,4},{3,5},{4,2},{5,3},{6,8},{7,9},{8,6},{9,7},{10,12... | collective-permute-start | bytes 270344 | tf_op jit(solution)/shard_map/ppermute | solution.py:425
  36.7 1.4 %collective-permute-start.10 = (s16[10,32,128]{2,1,0:T(8,128)(2,1)S(1)}, s16[10,32,128]{2,1,0:T(8,128)(2,1)S(1)}, u32[]{:S(2)}, u32[]{:S(2)}) collective-permute-start(s16[10,32,128]{2,1,0:T(8,128)(2,1)S(1)} %get-tuple-element.69), channel_id=1, source_target_pairs={{0,2},{2,0},{4,6},{6,4},{8,10},{10,8},{12,14},{14,12},{16,18},{18,... | collective-permute-start | bytes 245768 | tf_op jit(solution)/shard_map/ppermute | solution.py:425
